TPU v7x, 32 devices: a whole 2x2x4 slice. The times are simulated.
32 devices in a mesh: grid: 4 (over z), lev: 4 (over y, x), side: 2 (over core).
Axes of the slice: x: 2, y: 2, z: 4, core: 2. Of those that a mesh axis runs over, the one named last changes fastest.
Arguments:
- model_state: float32 [2, 8, 6, 32768], P('side', 'lev', None, 'grid'), may hold values from -6 to 6
- terrain_level: int32 [2, 8, 32768], P('side', None, 'grid'), may hold values from 0 to 7
- panel_owner: int32 [4096, 1], P('grid'), may hold values from 0 to 3, as said below
- panel_cell: int32 [4096], P('grid'), may hold values from 0 to 8191
- block_weight: float32 [256, 16, 128], P('grid'), may hold values from 0 to 0.015625
- block_owner: int32 [256, 1], P('grid'), may hold values from 0 to 3, as said below
- block_row: int32 [256], P('grid'), may hold values from 0 to 511
Outputs:
- new_state: float32 [2, 8, 6, 32768], P('side', 'lev', None, 'grid')
Inputs may be any that keep to these rules, and one draw needn't show every extreme that they name: `panel_owner`: the panel slots of nest tile t name only the global tiles (t - 1), (t + 1) and (t + 2), taken modulo 4; within the 1024 slots of one nest tile no global tile is named more than 512 times, and some global tile is named exactly that often. `block_owner`: the blocks of nest tile t name only the global tiles (t - 1), (t + 1) and (t + 2), taken modulo 4; within the 64 blocks of one nest tile no global tile is named more than 32 times, and some global tile is named exactly that often.
All inputs are finite; a program needn't handle non-finite values.
Results may differ from a plain program's by a relative error of at most 0.00005.
Values sent between devices are 32-bit elements; how exact they have to be, the bound alone decides.
No kernel may reach another device: no remote copies, remote signals or barrier semaphores. Data moves between devices by JAX's collectives and lax.ppermute only.
A program may use at most 192 MiB of HBM per device.

v0:
```python
import jax
import jax.numpy as jnp
from jax import lax
from jax.sharding import PartitionSpec as P


def from_behind(value, axis, steps):
    count = lax.axis_size(axis)
    pairs = [(source, (source + steps) % count) for source in range(count)]
    return lax.ppermute(value, axis, pairs)


def from_partner(block, axis, distance):
    count = lax.axis_size(axis)
    route = []
    for low in range(count):
        high = low | 1 << distance
        if high != low and high < count:
            route += [(low, high), (high, low)]
    return lax.ppermute(block, axis, route)


def bucket_slots(owners, targets, capacity):
    matches = (owners[:, None] == targets[None, :]).astype(jnp.int32)
    before = jnp.cumsum(matches, axis=0) - 1
    section = jnp.sum(matches * jnp.arange(3, dtype=jnp.int32)[None, :], axis=1)
    return section * capacity + jnp.sum(matches * before, axis=1)


def on_device(
    model_state, terrain_level, panel_owner, panel_cell, block_weight, block_owner, block_row
):
    groups = lax.axis_size("grid")
    steps_list = [-1, 1, groups // 2]
    flipped = [1, 0, 2]
    my_tile = lax.axis_index("grid")
    my_side = lax.axis_index("side")
    my_group = lax.axis_index("lev")
    fields = model_state[0]
    lev_dev, field_count, cell_dev = fields.shape
    level_map = terrain_level[0]
    panel_dev = panel_cell.shape[0]
    blocks_dev, block_coarse, block_fine = block_weight.shape
    block_cap = blocks_dev // 2
    slot_cap = block_cap * block_coarse
    partner_tiles = jnp.mod(my_tile + jnp.array(steps_list, jnp.int32), groups)
    panel_slots = bucket_slots(panel_owner[:, 0], partner_tiles, slot_cap)
    block_slots = bucket_slots(block_owner[:, 0], partner_tiles, block_cap)
    cell_request = (
        jnp.full((3 * slot_cap,), -1, jnp.int32)
        .at[panel_slots]
        .set(panel_cell)
        .reshape(3, slot_cap)
    )
    row_request = (
        jnp.full((3 * block_cap,), -1, jnp.int32)
        .at[block_slots]
        .set(block_row)
        .reshape(3, block_cap)
    )
    cell_parts = []
    row_parts = []
    for number, step in enumerate(steps_list):
        got_cells, got_rows = from_behind((cell_request[number], row_request[number]), "grid", step)
        cell_parts.append(got_cells)
        row_parts.append(got_rows)
    cells_wanted = jnp.concatenate(cell_parts)
    rows_coming = jnp.concatenate(row_parts)
    group_size = min(8, blocks_dev)
    group_count = blocks_dev // group_size
    same_block = (
        jnp.arange(group_size, dtype=jnp.int32)[:, None]
        == jnp.arange(group_size, dtype=jnp.int32)[None, :]
    )
    grouped_weight = block_weight.reshape(
        group_count, group_size, block_coarse, block_fine
    ).transpose(0, 2, 1, 3)
    expanded_weight = jnp.where(same_block[None, :, None, :, None], grouped_weight[:, None], 0.0)
    expanded_weight = expanded_weight.reshape(
        group_count, group_size * block_coarse, group_size * block_fine
    )
    full_placement = (
        block_slots[:, None] == jnp.arange(3 * block_cap, dtype=jnp.int32)[None, :]
    ).astype(jnp.int32)
    block_of_slot = jnp.sum(
        full_placement * jnp.arange(blocks_dev, dtype=jnp.int32)[:, None], axis=0
    )
    slot_filled = jnp.sum(full_placement, axis=0) > 0
    slot_source = (
        block_of_slot[:, None] * block_coarse + jnp.arange(block_coarse, dtype=jnp.int32)[None, :]
    ).reshape(-1)
    slot_live = jnp.broadcast_to(slot_filled[:, None], (3 * block_cap, block_coarse)).reshape(-1)
    target_levels = lax.dynamic_slice_in_dim(level_map, my_group * lev_dev, lev_dev, 0)
    piece = lax.all_gather(fields, "lev", axis=0, tiled=True)
    present = jnp.arange(piece.shape[0], dtype=jnp.int32)
    chosen = target_levels[:, None, None, :] == present[None, :, None, None]
    moved = jnp.sum(jnp.where(chosen, piece[None], 0.0), axis=1)
    depth = moved.shape[0]
    valid = cells_wanted >= 0
    panel_rows = jnp.take(moved, jnp.maximum(cells_wanted, 0), axis=2)
    panel_rows = jnp.where(valid[None, None, :], panel_rows, 0.0)
    pieces = moved.reshape(depth, field_count, group_count, group_size * block_fine)
    partial_sums = jnp.einsum(
        "kfgj,grj->kfgr", pieces, expanded_weight, precision=lax.Precision.HIGHEST
    )
    partial_sums = partial_sums.reshape(depth, field_count, blocks_dev * block_coarse)
    block_rows = jnp.take(partial_sums, slot_source, axis=2)
    block_rows = jnp.where(slot_live[None, None, :], block_rows, 0.0)
    outgoing = jnp.where(my_side == 0, panel_rows, block_rows)
    block_mass = jnp.sum(block_weight, axis=2).reshape(-1)
    mass_rows = jnp.where(slot_live, jnp.take(block_mass, slot_source), 0.0)
    mass_rows = jnp.where(my_side == 1, mass_rows.reshape(1, 1, 3 * slot_cap), 0.0)

    def pick_section(sections, number, panel_here):
        return jnp.where(panel_here, sections[:, :, flipped[number]], sections[:, :, number])

    def assemble(received, panel_here):
        parts = [
            jnp.where(panel_here, received[flipped[number]], received[number])
            for number in range(3)
        ]
        return jnp.concatenate(parts, axis=2)

    panel_here = my_side == 0
    value_sections = outgoing.reshape(outgoing.shape[0], field_count, 3, slot_cap)
    mass_sections = mass_rows.reshape(1, 1, 3, slot_cap)
    got_values = []
    got_masses = []
    for number, step in enumerate(steps_list):
        shifted_values, shifted_mass = from_behind(
            (
                pick_section(value_sections, number, panel_here),
                pick_section(mass_sections, number, panel_here),
            ),
            "grid",
            step,
        )
        got_values.append(shifted_values)
        got_masses.append(shifted_mass)
    crossed_values = assemble(got_values, panel_here)
    crossed_mass = assemble(got_masses, panel_here)
    arrived, arrived_mass = from_partner((crossed_values, crossed_mass), "side", 0)
    rim_values = jnp.take(arrived, panel_slots, axis=2)
    blended = 0.5 * (fields[:, :, :panel_dev] + rim_values)
    new_nested = jnp.concatenate([blended, fields[:, :, panel_dev:]], axis=2)
    landing = (
        rows_coming[:, None] * block_coarse + jnp.arange(block_coarse, dtype=jnp.int32)[None, :]
    )
    landing = jnp.where(rows_coming[:, None] >= 0, landing, cell_dev).reshape(-1)
    feedback = (
        jnp.zeros((lev_dev, field_count, cell_dev), jnp.float32)
        .at[:, :, landing]
        .add(arrived, mode="drop")
    )
    weight_sum = (
        jnp.zeros((cell_dev,), jnp.float32).at[landing].add(arrived_mass.reshape(-1), mode="drop")
    )
    new_coarse = (fields + feedback) / (1.0 + weight_sum)
    result = jnp.where(my_side == 0, new_coarse, new_nested)
    return result[None]


def solution(mesh):
    in_specs = (
        P("side", "lev", None, "grid"),
        P("side", None, "grid"),
        P("grid", None),
        P("grid"),
        P("grid", None, None),
        P("grid", None),
        P("grid"),
    )
    out_specs = P("side", "lev", None, "grid")
    return jax.shard_map(
        on_device, mesh=mesh, in_specs=in_specs, out_specs=out_specs, check_vma=False
    )
```

profile of v0, /device:TPU:0, one launch (start us, length us, event | category | flops | bytes accessed | tf_op | source)
XLA Modules:
  0.0 358.1 jit_solution(6575937821085165754)
XLA Ops:
  10.1 4.5 %scatter_custom_fusion.1 = s32[1536]{0:T(1024)S(1)} fusion(s32[1024]{0:T(1024)S(1)} %bitcast.96, s32[1024]{0:T(1024)} %param.11, s32[]{:T(128)} %constant.77.clone.1), kind=kCustom, calls=%fused_computation.71 | custom fusion | bytes 6656 | tf_op jit(solution)/shard_map/scatter | solution.py:52
  14.6 5.1 %collective-permute-start.3 = (s32[512]{0:T(512)S(1)}, s32[512]{0:T(512)S(1)}, u32[]{:S(2)}, u32[]{:S(2)}) collective-permute-start(s32[512]{0:T(512)S(1)} %get-tuple-element.25), channel_id=1, source_target_pairs={{0,24},{8,0},{16,8},{24,16},{1,25},{9,1},{17,9},{25,17},{2,26},{10... | collective-permute-start | bytes 6152 | tf_op jit(solution)/shard_map/ppermute | solution.py:10
  19.8 1.0 collective-permute-start.4
  23.4 2.8 collective-permute-start
  26.2 1.1 collective-permute-start.2
  27.4 2.1 copy.55
  30.5 9.3 %copy.54 = f32[1,2,6,8192]{2,1,3,0:T(2,128)} copy(f32[1,2,6,8192]{3,1,2,0:T(2,128)} %param.8) | data formatting | bytes 786432 | tf_op args[0]
  40.3 5.9 %gather_fusion.2 = f32[1536]{0:T(1024)S(1)} fusion(f32[1024]{0:T(1024)S(1)} %reshape.524, s32[2048]{0:T(1024)S(1)} %pad_clamp_fusion), kind=kCustom, calls=%fused_computation.2 | custom fusion | bytes 18432 | tf_op jit(solution)/shard_map/jit(_take)/gather | solution.py:111
  46.7 2.5 broadcast_in_dim.185
  49.1 4.9 %broadcast_in_dim.186 = f32[8,128,1024]{2,1,0:T(8,128)} reshape(f32[8,8,16,8,128]{4,3,2,1,0:T(8,128)} %broadcast_in_dim.185) | data formatting | bytes 8388608 | tf_op jit(solution)/shard_map/jit(_where)/broadcast_in_dim | solution.py:78
  54.2 6.6 %slice.95 = f32[2,6,7168]{1,0,2:T(2,128)} slice(f32[2,6,8192]{1,0,2:T(2,128)} %bitcast.77), slice={[0:2], [0:6], [1024:8192]} | slice | bytes 688128 | tf_op jit(solution)/shard_map/slice | solution.py:145
  60.9 2.3 collective-permute-start.10
  63.2 3.0 collective-permute-done.1
  66.5 0.9 collective-permute-start.11
  67.5 2.8 collective-permute-done.11
  70.3 2.3 copy.80
  72.6 0.9 select_reduce_fusion
  73.8 7.9 %copy.57 = f32[2,6,8192]{1,0,2:T(2,128)} copy(f32[2,6,8192]{2,1,0:T(8,128)S(1)} %select_reduce_fusion) | data formatting | bytes 786432 | tf_op jit(solution)/shard_map/reduce_sum | solution.py:97
  81.7 6.2 %fusion.6 = f32[2,6,8,128]{3,1,0,2:T(8,128)S(1)} fusion(f32[8,128,1024]{2,1,0:T(8,128)} %broadcast_in_dim.186, pred[128,1024]{1,0:T(8,128)(4,1)S(1)} %bitcast.85, f32[2,6,8,1024]{3,2,1,0:T(8,128)S(1)} %reshape.592), kind=kOutput, calls=%fused_computation.17 | convolution fusion | flops 152043520 | bytes 4767744 | tf_op jit(solution)/shard_map/kfgj,grj->kfgr/dot_general | solution.py:103
  88.5 5.1 %gather_fusion.1 = f32[1536,2,6]{2,1,0:T(2,128)S(1)} fusion(f32[2,6,1024]{1,0,2:T(2,128)S(1)} %bitcast.84, s32[2048]{0:T(1024)S(1)} %pad_clamp_fusion), kind=kCustom, calls=%fused_computation.1 | custom fusion | bytes 153600 | tf_op jit(solution)/shard_map/jit(_take)/gather | solution.py:107
  94.3 6.8 %gather_fusion = f32[1536,2,6]{2,1,0:T(2,128)S(1)} fusion(f32[2,6,8192]{1,0,2:T(2,128)} %copy.57, s32[2048]{0:T(1024)S(1)} %pad_clamp_fusion.1), kind=kCustom, calls=%fused_computation | custom fusion | bytes 153600 | tf_op jit(solution)/shard_map/jit(_take)/gather | solution.py:100
  101.9 1.5 collective-permute-start.6
  103.4 2.4 collective-permute-start.7
  105.9 1.2 collective-permute-start.8
  107.6 3.1 collective-permute-done.8
  110.9 10.7 %scatter_custom_fusion.3 = f32[8192]{0:T(1024)S(1)} fusion(s32[1536]{0:T(1024)S(1)} %fusion.18, f32[1536]{0:T(1024)S(1)} %reduce.5, f32[]{:T(128)} %constant.131.clone.1), kind=kCustom, calls=%fused_computation.52 | custom fusion | flops 1536 | bytes 32772 | tf_op jit(solution)/shard_map/scatter-add | solution.py:156
  122.5 2.1 copy.66
  124.6 8.9 %gather_fusion.3 = f32[1024,2,6]{2,1,0:T(2,128)} fusion(f32[2,6,1536]{1,0,2:T(2,128)} %copy.66, s32[1024]{0:T(1024)S(1)} %broadcast_clamp_fusion), kind=kCustom, calls=%fused_computation.3 | custom fusion | bytes 102400 | tf_op jit(solution)/shard_map/jit(_take)/gather | solution.py:143
  133.5 5.6 %fusion.9 = f32[2,6,1024]{1,0,2:T(2,128)S(1)} fusion(f32[2,6,8192]{1,0,2:T(2,128)} %bitcast.78, f32[1024,2,6]{2,1,0:T(2,128)} %gather_fusion.3, pred[1024]{0:T(1024)(128)(4,1)S(1)} %get-tuple-element.15), kind=kLoop, calls=%fused_computation.19 | loop fusion | flops 36864 | bytes 148480 | tf_op jit(solution)/shard_map/mul | solution.py:144
  139.1 145.4 %scatter_fusion = f32[2,6,8192]{1,0,2:T(2,128)} fusion(f32[2,6,8192]{1,0,2:T(2,128)} %bitcast.79, s32[1536]{0:T(1024)S(1)} %fusion.18, f32[1536,2,6]{2,1,0:T(2,128)S(1)} %copy.65), kind=kCustom, calls=%fused_computation.6 | custom fusion | flops 18432 | bytes 227328 | tf_op jit(solution)/shard_map/scatter-add | solution.py:153
  284.5 56.7 %fusion = f32[1,2,6,8192]{2,1,3,0:T(2,128)} fusion(f32[2,6,7168]{1,0,2:T(2,128)} %slice.95, f32[2,6,1024]{1,0,2:T(2,128)S(1)} %fusion.9, f32[2,6,8192]{1,0,2:T(2,128)} %scatter_fusion, pred[]{:T(512)S(6)} %eq.100, f32[8192]{0:T(1024)S(1)} %scatter_custom_fusion.3), kind=kLoop, calls=%fused_computation.9 | loop fusion | flops 294912 | bytes 1212417 | tf_op jit(solution)/shard_map/broadcast_in_dim | solution.py:160
  341.2 10.1 %copy.67 = f32[1,2,6,8192]{3,1,2,0:T(2,128)} copy(f32[1,2,6,8192]{2,1,3,0:T(2,128)} %fusion) | data formatting | bytes 786432 | tf_op jit(solution)/shard_map/broadcast_in_dim | solution.py:160
  (94 shorter events, 12.6 us)
Async XLA Ops:
  6.5 47.5 %copy-start = (s32[1,8,8192]{2,1,0:T(8,128)S(1)}, s32[1,8,8192]{2,1,0:T(8,128)}, u32[]{:S(2)}) copy-start(s32[1,8,8192]{2,1,0:T(8,128)} %param.9) | copy-start | bytes 786436
  6.5 63.8 %all-gather.3.cloned.1.call-start = ((), (), s32[]{:S(2)}) async-start(), calls=%async_computation | async-start | bytes 1966080 | tf_op jit(solution)/shard_map/all_gather | solution.py:94
  14.6 51.8 %collective-permute-start.3 = (s32[512]{0:T(512)S(1)}, s32[512]{0:T(512)S(1)}, u32[]{:S(2)}, u32[]{:S(2)}) collective-permute-start(s32[512]{0:T(512)S(1)} %get-tuple-element.25), channel_id=1, source_target_pairs={{0,24},{8,0},{16,8},{24,16},{1,25},{9,1},{17,9},{25,17},{2,26},{10... | collective-permute-start | bytes 6152 | tf_op jit(solution)/shard_map/ppermute | solution.py:10
  19.7 47.6 %collective-permute-start.5 = (s32[512]{0:T(512)S(1)}, s32[512]{0:T(512)S(1)}, u32[]{:S(2)}, u32[]{:S(2)}) collective-permute-start(s32[512]{0:T(512)S(1)} %get-tuple-element.26), channel_id=1, source_target_pairs={{0,16},{8,24},{16,0},{24,8},{1,17},{9,25},{17,1},{25,9},{2,18},{10... | collective-permute-start | bytes 6152 | tf_op jit(solution)/shard_map/ppermute | solution.py:10
  19.8 47.6 %collective-permute-start.4 = (s32[512]{0:T(512)S(1)}, s32[512]{0:T(512)S(1)}, u32[]{:S(2)}, u32[]{:S(2)}) collective-permute-start(s32[512]{0:T(512)S(1)} %get-tuple-element.27), channel_id=1, source_target_pairs={{0,8},{8,16},{16,24},{24,0},{1,9},{9,17},{17,25},{25,1},{2,10},{10... | collective-permute-start | bytes 6152 | tf_op jit(solution)/shard_map/ppermute | solution.py:10
  23.4 37.4 %collective-permute-start = (s32[32]{0:T(128)S(1)}, s32[32]{0:T(128)S(1)}, u32[]{:S(2)}, u32[]{:S(2)}) collective-permute-start(s32[32]{0:T(128)S(1)} %get-tuple-element.30), channel_id=1, source_target_pairs={{0,24},{8,0},{16,8},{24,16},{1,25},{9,1},{17,9},{25,17},{2,26},{10... | collective-permute-start | bytes 392 | tf_op jit(solution)/shard_map/ppermute | solution.py:10
  26.2 34.6 %collective-permute-start.2 = (s32[32]{0:T(128)S(1)}, s32[32]{0:T(128)S(1)}, u32[]{:S(2)}, u32[]{:S(2)}) collective-permute-start(s32[32]{0:T(128)S(1)} %get-tuple-element.31), channel_id=1, source_target_pairs={{0,16},{8,24},{16,0},{24,8},{1,17},{9,25},{17,1},{25,9},{2,18},{10... | collective-permute-start | bytes 392 | tf_op jit(solution)/shard_map/ppermute | solution.py:10
  30.5 9.4 %copy-start.1 = (f32[64,16,128]{2,1,0:T(8,128)S(1)}, f32[64,16,128]{2,1,0:T(8,128)}, u32[]{:S(2)}) copy-start(f32[64,16,128]{2,1,0:T(8,128)} %param.12) | copy-start | bytes 1572868
  60.8 5.3 %collective-permute-start.1 = (s32[32]{0:T(128)S(1)}, s32[32]{0:T(128)S(1)}, u32[]{:S(2)}, u32[]{:S(2)}) collective-permute-start(s32[32]{0:T(128)S(1)} %get-tuple-element.32), channel_id=1, source_target_pairs={{0,8},{8,16},{16,24},{24,0},{1,9},{9,17},{17,25},{25,1},{2,10},{10... | collective-permute-start | bytes 392 | tf_op jit(solution)/shard_map/ppermute | solution.py:10
  60.9 6.7 %collective-permute-start.10 = (f32[1,1,512]{2,1,0:T(1,128)S(1)}, f32[1,1,512]{2,1,0:T(1,128)S(1)}, u32[]{:S(2)}, u32[]{:S(2)}) collective-permute-start(f32[1,1,512]{2,1,0:T(1,128)S(1)} %get-tuple-element.22), channel_id=1, source_target_pairs={{0,8},{8,16},{16,24},{24,0},{1,9},{9,17},{17,25},{25,1},{2,10},{10... | collective-permute-start | bytes 6152 | tf_op jit(solution)/shard_map/ppermute | solution.py:10
  66.2 39.6 %collective-permute-start.12 = (f32[1,1,512]{2,1,0:T(1,128)S(1)}, f32[1,1,512]{2,1,0:T(1,128)S(1)}, u32[]{:S(2)}, u32[]{:S(2)}) collective-permute-start(f32[1,1,512]{2,1,0:T(1,128)S(1)} %get-tuple-element.23), channel_id=1, source_target_pairs={{0,16},{8,24},{16,0},{24,8},{1,17},{9,25},{17,1},{25,9},{2,18},{10... | collective-permute-start | bytes 6152 | tf_op jit(solution)/shard_map/ppermute | solution.py:10
  66.5 3.8 %collective-permute-start.11 = (f32[1,1,512]{2,1,0:T(1,128)S(1)}, f32[1,1,512]{2,1,0:T(1,128)S(1)}, u32[]{:S(2)}, u32[]{:S(2)}) collective-permute-start(f32[1,1,512]{2,1,0:T(1,128)S(1)} %get-tuple-element.24), channel_id=1, source_target_pairs={{0,24},{8,0},{16,8},{24,16},{1,25},{9,1},{17,9},{25,17},{2,26},{10... | collective-permute-start | bytes 6152 | tf_op jit(solution)/shard_map/ppermute | solution.py:10
  101.9 5.7 %collective-permute-start.6 = (f32[2,6,512]{2,0,1:T(2,128)S(1)}, f32[2,6,512]{2,0,1:T(2,128)S(1)}, u32[]{:S(2)}, u32[]{:S(2)}) collective-permute-start(f32[2,6,512]{2,0,1:T(2,128)S(1)} %get-tuple-element.17), channel_id=1, source_target_pairs={{0,8},{8,16},{16,24},{24,0},{1,9},{9,17},{17,25},{25,1},{2,10},{10... | collective-permute-start | bytes 73736 | tf_op jit(solution)/shard_map/ppermute | solution.py:10
  103.4 4.2 %collective-permute-start.7 = (f32[2,6,512]{2,0,1:T(2,128)S(1)}, f32[2,6,512]{2,0,1:T(2,128)S(1)}, u32[]{:S(2)}, u32[]{:S(2)}) collective-permute-start(f32[2,6,512]{2,0,1:T(2,128)S(1)} %get-tuple-element.19), channel_id=1, source_target_pairs={{0,24},{8,0},{16,8},{24,16},{1,25},{9,1},{17,9},{25,17},{2,26},{10... | collective-permute-start | bytes 73736 | tf_op jit(solution)/shard_map/ppermute | solution.py:10
  105.8 5.0 %collective-permute-start.13 = (f32[1,1,1536]{2,1,0:T(1,128)S(1)}, f32[1,1,1536]{2,1,0:T(1,128)S(1)}, u32[]{:S(2)}, u32[]{:S(2)}) collective-permute-start(f32[1,1,1536]{2,1,0:T(1,128)S(1)} %pad_maximum_fusion.1), channel_id=1, source_target_pairs={{0,1},{1,0},{2,3},{3,2},{4,5},{5,4},{6,7},{7,6},{8,9},{9,8},{10,11... | collective-permute-start | bytes 18440 | tf_op jit(solution)/shard_map/ppermute | solution.py:20
  105.9 4.8 %collective-permute-start.8 = (f32[2,6,512]{2,0,1:T(2,128)S(1)}, f32[2,6,512]{2,0,1:T(2,128)S(1)}, u32[]{:S(2)}, u32[]{:S(2)}) collective-permute-start(f32[2,6,512]{2,0,1:T(2,128)S(1)} %get-tuple-element.18), channel_id=1, source_target_pairs={{0,16},{8,24},{16,0},{24,8},{1,17},{9,25},{17,1},{25,9},{2,18},{10... | collective-permute-start | bytes 73736 | tf_op jit(solution)/shard_map/ppermute | solution.py:10
  110.7 10.9 %collective-permute-start.9 = (f32[2,6,1536]{2,0,1:T(2,128)S(1)}, f32[2,6,1536]{2,0,1:T(2,128)S(1)}, u32[]{:S(2)}, u32[]{:S(2)}) collective-permute-start(f32[2,6,1536]{2,0,1:T(2,128)S(1)} %pad_maximum_fusion), channel_id=1, source_target_pairs={{0,1},{1,0},{2,3},{3,2},{4,5},{5,4},{6,7},{7,6},{8,9},{9,8},{10,11... | collective-permute-start | bytes 221192 | tf_op jit(solution)/shard_map/ppermute | solution.py:20
Sparse Core Ops, SparseCore 0:
  29.7 30.4 all-gather.2
where the time goes:
time: 361 us; the launch traced here: 358 us
  other arithmetic  225 us (62%)
  local copies, waits for them, and re-layouts  84.8 us (23%)
  starting transfers between devices  18.5 us (5%)
  between operations  13.8 us (4%)
  waiting for transfers between devices  9.35 us (3%)
  matrix products  6.18 us (2%)
    scatter-add x1, other arithmetic, on_device(): feedback = jnp.zeros((lev_dev, field_count, cell_dev), jnp.float32).at[:,...  145 us
    broadcast_in_dim x1, other arithmetic, on_device(): return result[None]  56.7 us
    ppermute x12, starting transfers between devices, from_behind(): return lax.ppermute(value, axis, pairs)  18.4 us
    unnamed x7, local copies, waits for them, and re-layouts  11.5 us
    scatter-add x1, other arithmetic, on_device(): jnp.zeros((cell_dev,), jnp.float32).at[landing]  10.7 us
    broadcast_in_dim x1, local copies, waits for them, and re-layouts, on_device(): return result[None]  10.1 us
    ppermute x12, waiting for transfers between devices, from_behind(): return lax.ppermute(value, axis, pairs)  9.33 us
    gather x1, local copies, waits for them, and re-layouts, on_device(): rim_values = jnp.take(arrived, panel_slots, axis=2)  8.89 us
  transfers between devices with their start and end apart: 15, of which 4 were waited for; matrix products, arithmetic and copies ran while one was open for 22% of the time, Pallas kernels for 0%

commit v1 on v0

v1 whole, which is shorter than its diff:
```python
import functools

import jax
import jax.numpy as jnp
from jax import lax
from jax.experimental import pallas as pl
from jax.experimental.pallas import tpu as pltpu
from jax.sharding import PartitionSpec as P

LANES = 128
SUBLANES = 8
VALUE_BITS = 16
ID_BITS = 8
MESSAGE_ROWS = 8
FLIPPED = (1, 0, 2)
VMEM = pltpu.VMEM
SMEM = pltpu.SMEM


def grid_steps(groups):
    return (groups - 1, 1, groups // 2)


def iota(shape, dimension):
    return lax.broadcasted_iota(jnp.int32, shape, dimension)


def rank_of(hit):
    rows, lanes = hit.shape
    lane, row = iota(hit.shape, 1), iota(hit.shape, 0)
    ones = hit.astype(jnp.int32)
    running = ones
    step = 1
    while step < lanes:
        running = running + jnp.where(lane >= step, pltpu.roll(running, step, 1), 0)
        step *= 2
    total = jnp.broadcast_to(jnp.sum(ones, axis=1, keepdims=True), hit.shape)
    above = jnp.where(row >= 1, pltpu.roll(total, 1, 0), 0)
    step = 1
    while step < rows:
        above = above + jnp.where(row >= step, pltpu.roll(above, step, 0), 0)
        step *= 2
    return running - ones + above


def squeeze(hit, rank, value, value_bits):
    rows, lanes = hit.shape
    lane, row = iota(hit.shape, 1), iota(hit.shape, 0)
    held = jnp.where(hit, ((row * lanes + lane - rank) << value_bits) | value, -1)
    bit = 0
    while 1 << bit < rows * lanes:
        step = 1 << bit
        if step < lanes:
            turned = pltpu.roll(held, lanes - step, 1)
            coming = jnp.where(lane < lanes - step, turned, pltpu.roll(turned, rows - 1, 0))
        else:
            coming = pltpu.roll(held, rows - step // lanes, 0)
        comes = (coming >= 0) & ((coming >> (value_bits + bit)) & 1 == 1)
        stays = (held >= 0) & ((held >> (value_bits + bit)) & 1 == 0)
        held = jnp.where(comes, coming, jnp.where(stays, held, -1))
        bit += 1
    return jnp.where(held >= 0, held & ((1 << value_bits) - 1), -1)


def list_kernel(groups, panel_owner, panel_cell, block_owner, block_row, *refs):
    requests, own_ref, slot_ref, owner_pad, row_pad = refs[:3], refs[3], refs[4], refs[5], refs[6]
    tile = lax.axis_index("grid")
    blocks = block_owner.shape[1]
    owner_pad[...] = jnp.full(owner_pad.shape, -1, jnp.int32)
    row_pad[...] = jnp.zeros(row_pad.shape, jnp.int32)
    owner_pad[0:1, 0:blocks] = block_owner[...]
    row_pad[0:1, 0:blocks] = block_row[...]
    owners, cells = panel_owner[...], panel_cell[...]
    landing = owner_pad[...]
    lane = iota(landing.shape, 1)
    marked = row_pad[...] | (lane << VALUE_BITS)
    half = owners.shape[0] // 2
    slots = jnp.zeros_like(owners)
    own_ref[...] = jnp.full(own_ref.shape, -1, jnp.int32)
    for number, step in enumerate(grid_steps(groups)):
        partner = lax.rem(tile + step, groups)
        hit = owners == partner
        rank = rank_of(hit)
        slots = jnp.where(hit, number * half * LANES + rank, slots)
        wanted = squeeze(hit, rank, cells, VALUE_BITS)
        lands = landing == partner
        block = squeeze(lands, rank_of(lands), marked, VALUE_BITS + ID_BITS)
        requests[number][...] = jnp.full(requests[number].shape, -1, jnp.int32)
        requests[number][0:half, :] = jnp.maximum(wanted[0:half], 0)
        requests[number][half : half + 1, :] = jnp.where(
            block >= 0, block & ((1 << VALUE_BITS) - 1), -1
        )[0:1]
        own_ref[number : number + 1, :] = jnp.where(block >= 0, block >> VALUE_BITS, -1)[0:1]
    slot_ref[...] = slots


def gather_lanes(values, index):
    return jnp.take_along_axis(values, index, axis=1)


def fold(values, least):
    step = values.shape[0] // 2
    while step >= least:
        values = values + pltpu.roll(values, step, 0)
        step //= 2
    return values


def panel_rows(lev_dev, fields, tiles, lists, group, state, terrain, packed, scratch):
    levels = SUBLANES
    bits = (levels - 1).bit_length()
    total = jnp.zeros((tiles, LANES), jnp.int32)
    for level in range(levels):
        total = total | (terrain[pl.ds(level, tiles, stride=levels), :] << (bits * level))
    packed[...] = total
    shape = (SUBLANES, LANES)
    sub = iota(shape, 0)
    per = SUBLANES // lev_dev
    quarters = lists[0].shape[0] // 2
    for number in range(3):
        for quarter in range(quarters):
            cells = jnp.broadcast_to(lists[number][quarter : quarter + 1, :], shape)
            high, low = cells // LANES, cells % LANES
            sums = [jnp.zeros(shape, jnp.float32) for _ in range(fields)]
            for chunk in range(tiles // per):
                here = high == chunk * per + sub // lev_dev
                for field in range(fields):
                    start = field * tiles * lev_dev + chunk * SUBLANES
                    got = gather_lanes(state[start : start + SUBLANES, :], low)
                    sums[field] = jnp.where(here, got, sums[field])
            code = jnp.zeros(shape, jnp.int32)
            for chunk in range(tiles // SUBLANES):
                got = gather_lanes(packed[chunk * SUBLANES : (chunk + 1) * SUBLANES, :], low)
                code = jnp.where(high == chunk * SUBLANES + sub, got, code)
            code = fold(code, 1)
            source = (code >> (bits * sub)) & (levels - 1)
            section = FLIPPED[number]
            for field in range(fields):
                both = fold(sums[field], lev_dev)
                placed = jnp.zeros(shape, jnp.float32)
                for level in range(lev_dev):
                    one = both
                    for turn in range(1, lev_dev):
                        one = jnp.where((sub - level) % lev_dev == turn, pltpu.roll(both, turn, 0), one)
                    placed = jnp.where(source == group * lev_dev + level, one, placed)
                row = ((section * fields + field) * quarters + quarter) * levels
                scratch[row : row + levels, :] = placed


def block_rows(lev_dev, fields, tiles, own, group, state, terrain, weight, scratch, mass):
    levels = SUBLANES
    coarse = weight.shape[1]
    per = LANES // coarse
    quarters = tiles // 2 // per

    def one_tile(index, carry):
        number, quarter = index // quarters, index % quarters
        lefts, rights = [], []
        for place in range(per):
            name = own[number, quarter * per + place]
            block = jnp.maximum(name, 0)
            source = terrain[pl.ds(pl.multiple_of(block * levels, levels), levels), :]
            parts = []
            for field in range(fields):
                placed = jnp.zeros((levels, LANES), jnp.float32)
                for level in range(lev_dev):
                    line = state[pl.ds((field * tiles + block) * lev_dev + level, 1), :]
                    placed = jnp.where(source == group * lev_dev + level, line, placed)
                parts.append(placed)
            moved = jnp.concatenate(parts, axis=0)
            moved_high = moved.astype(jnp.bfloat16)
            moved_low = (moved - moved_high.astype(jnp.float32)).astype(jnp.bfloat16)
            lefts.append(
                jnp.concatenate(
                    [moved_high, moved_low, jnp.ones((2 * SUBLANES, LANES), jnp.bfloat16)], axis=0
                )
            )
            dense = jnp.where(name >= 0, weight[block], 0.0)
            dense_high = dense.astype(jnp.bfloat16)
            dense_low = (dense - dense_high.astype(jnp.float32)).astype(jnp.bfloat16)
            blank = jnp.zeros((coarse, LANES), jnp.bfloat16)
            rights.append(
                jnp.concatenate(
                    [dense_high if other == place else blank for other in range(per)]
                    + [dense_low if other == place else blank for other in range(per)],
                    axis=0,
                )
            )
        product = lax.dot_general(
            jnp.concatenate(lefts, axis=1),
            jnp.concatenate(rights, axis=1),
            (((1,), (1,)), ((), ())),
            preferred_element_type=jnp.float32,
        )
        product = product[:, :LANES] + product[:, LANES:]
        rows = fields * levels
        result = product[:rows] + product[rows : 2 * rows]
        for field in range(fields):
            row = ((number * fields + field) * quarters + quarter) * levels
            scratch[pl.ds(pl.multiple_of(row, levels), levels), :] = result[
                field * levels : (field + 1) * levels
            ]
        mass[pl.ds(index, 1), :] = product[2 * rows : 2 * rows + 1]
        return carry

    lax.fori_loop(0, 3 * quarters, one_tile, 0)


def produce_kernel(lev_dev, fields, partners, own, *refs):
    lists, state, terrain, weight = refs[:3], refs[3], refs[4], refs[5]
    parts = refs[6 : 6 + partners]
    mass, scratch, packed = refs[6 + partners :]
    tiles = terrain.shape[0] // SUBLANES
    side, group = lax.axis_index("side"), lax.axis_index("lev")

    @pl.when(side == 0)
    def _():
        mass[...] = jnp.zeros_like(mass)
        panel_rows(lev_dev, fields, tiles, lists, group, state, terrain, packed, scratch)

    @pl.when(side == 1)
    def _():
        block_rows(lev_dev, fields, tiles, own, group, state, terrain, weight, scratch, mass)

    rows = scratch.shape[0] // SUBLANES
    for distance in range(partners):
        target = group ^ distance
        for level in range(lev_dev):
            parts[distance][level * rows : (level + 1) * rows, :] = scratch[
                pl.ds(target * lev_dev + level, rows, stride=SUBLANES), :
            ]


def sum_kernel(lev_dev, fields, partners, *refs):
    parts, mass, sections = refs[:partners], refs[partners], refs[partners + 1 :]
    total = parts[0][...]
    for part in parts[1:]:
        total = total + part[...]
    rows = total.shape[0] // lev_dev
    span = rows // 3
    quarters = span // fields
    for number, section in enumerate(sections):
        for level in range(lev_dev):
            start = level * rows + number * span
            section[level * span : (level + 1) * span, :] = total[start : start + span]
        section[lev_dev * span : lev_dev * span + quarters, :] = mass[
            number * quarters : (number + 1) * quarters, :
        ]
        tail = lev_dev * span + quarters
        section[tail:, :] = jnp.zeros((section.shape[0] - tail, LANES), jnp.float32)


def finish_panel(lev_dev, fields, tiles, sections, slots, state, out):
    shape = (SUBLANES, LANES)
    sub = iota(shape, 0)
    out[...] = state[...]
    panel_tiles = slots.shape[0]
    quarters = panel_tiles // 2
    span = fields * quarters
    share = SUBLANES // quarters
    for tile in range(panel_tiles):
        place = jnp.broadcast_to(slots[tile : tile + 1, :], shape)
        high, low = place // LANES, place % LANES
        here = [high == number * quarters + sub % quarters for number in range(3)]
        for level in range(lev_dev):
            for chunk in range(span // SUBLANES):
                start = level * span + chunk * SUBLANES
                found = jnp.zeros(shape, jnp.float32)
                for number in range(3):
                    values = sections[FLIPPED[number]][start : start + SUBLANES, :]
                    found = jnp.where(here[number], gather_lanes(values, low), found)
                for part in range(share):
                    field = chunk * share + part
                    rim = jnp.sum(
                        jnp.where(sub // quarters == part, found, 0.0), axis=0, keepdims=True
                    )
                    row = (field * tiles + tile) * lev_dev + level
                    out[row : row + 1, :] = 0.5 * (state[row : row + 1, :] + rim)


def finish_coarse(lev_dev, fields, tiles, coarse, sections, lists, state, out, landed):
    per = LANES // coarse
    kinds = lev_dev * fields + 1
    stride = landed.shape[0] // (tiles + 1)
    landed[...] = jnp.zeros_like(landed)
    quarters = lists[0].shape[0] // 2
    rows = sections[0].shape[0] // quarters
    lane = iota((rows, LANES), 1)
    for number in range(3):
        for quarter in range(quarters):
            chunk = sections[number][pl.ds(quarter, rows, stride=quarters), :]
            for place in range(per):
                run = lists[number][quarters, quarter * per + place]
                run = jnp.where(run < 0, tiles * per, run)
                tile, offset = run // per, run % per
                piece = jnp.where(lane // coarse == place, chunk, 0.0)
                turn = lax.rem(offset + per - place, per) * coarse
                start = pl.multiple_of(tile * stride, SUBLANES)
                landed[pl.ds(start, rows), :] = landed[pl.ds(start, rows), :] + pltpu.roll(
                    piece, turn, 1
                )
    weight_sum = landed[pl.ds(kinds - 1, tiles, stride=stride), :]
    scale = 1.0 / (1.0 + weight_sum)
    for field in range(fields):
        for level in range(lev_dev):
            here = pl.ds(field * tiles * lev_dev + level, tiles, stride=lev_dev)
            feedback = landed[pl.ds(level * fields + field, tiles, stride=stride), :]
            out[here, :] = (state[here, :] + feedback) * scale


def finish_kernel(lev_dev, fields, coarse, *refs):
    sections, lists, slots, state, out, landed = refs[:3], refs[3:6], *refs[6:]
    tiles = state.shape[0] // (fields * lev_dev)
    side = lax.axis_index("side")

    @pl.when(side == 0)
    def _():
        finish_coarse(lev_dev, fields, tiles, coarse, sections, lists, state, out, landed)

    @pl.when(side == 1)
    def _():
        finish_panel(lev_dev, fields, tiles, sections, slots, state, out)


def specs(*spaces):
    return [pl.BlockSpec(memory_space=space) for space in spaces]


def params():
    return pltpu.CompilerParams(vmem_limit_bytes=16 * 1024 * 1024)


def struct(shape, dtype=jnp.float32):
    return jax.ShapeDtypeStruct(shape, dtype)


def on_device(
    model_state, terrain_level, panel_owner, panel_cell, block_weight, block_owner, block_row
):
    groups, partners = lax.axis_size("grid"), lax.axis_size("lev")
    sides = lax.axis_size("side")
    steps = grid_steps(groups)
    _, lev_dev, fields, cell_dev = model_state.shape
    levels = terrain_level.shape[1]
    tiles = cell_dev // LANES
    blocks, coarse, _ = block_weight.shape
    panel_tiles = panel_cell.shape[0] // LANES
    quarters = panel_tiles // 2
    state = (
        model_state.reshape(lev_dev, fields, tiles, LANES)
        .transpose(1, 2, 0, 3)
        .reshape(fields * tiles * lev_dev, LANES)
    )
    terrain = (
        terrain_level.reshape(levels, tiles, LANES).transpose(1, 0, 2).reshape(tiles * levels, LANES)
    )
    message = struct((MESSAGE_ROWS, LANES), jnp.int32)
    *requests, own, slots = pl.pallas_call(
        functools.partial(list_kernel, groups),
        out_shape=[message] * 4 + [struct((panel_tiles, LANES), jnp.int32)],
        in_specs=specs(*[VMEM] * 4),
        out_specs=specs(*[VMEM] * 5),
        scratch_shapes=[VMEM((SUBLANES, LANES), jnp.int32)] * 2,
        compiler_params=params(),
        name="lists",
    )(
        panel_owner.reshape(panel_tiles, LANES),
        panel_cell.reshape(panel_tiles, LANES),
        block_owner.reshape(1, blocks),
        block_row.reshape(1, blocks),
    )
    lists = [
        lax.ppermute(
            request,
            ("grid", "side"),
            [(tile * sides, (tile + step) % groups * sides) for tile in range(groups)],
        )
        for request, step in zip(requests, steps)
    ]
    scratch_rows = 3 * fields * quarters
    part = struct((lev_dev * scratch_rows, LANES))
    *parts, mass = pl.pallas_call(
        functools.partial(produce_kernel, lev_dev, fields, partners),
        out_shape=[part] * partners + [struct((2 * SUBLANES, LANES))],
        in_specs=specs(SMEM, *[VMEM] * 6),
        out_specs=specs(*[VMEM] * (partners + 1)),
        scratch_shapes=[
            VMEM((scratch_rows * SUBLANES, LANES), jnp.float32),
            VMEM((tiles, LANES), jnp.int32),
        ],
        compiler_params=params(),
        name="produce",
    )(own, *lists, state, terrain, block_weight)
    arrived = [parts[0]] + [
        lax.ppermute(parts[distance], "lev", [(rank, rank ^ distance) for rank in range(partners)])
        for distance in range(1, partners)
    ]
    section_rows = lev_dev * fields * quarters + quarters
    section_rows += -section_rows % SUBLANES
    sections = pl.pallas_call(
        functools.partial(sum_kernel, lev_dev, fields, partners),
        out_shape=[struct((section_rows, LANES))] * 3,
        in_specs=specs(*[VMEM] * (partners + 1)),
        out_specs=specs(*[VMEM] * 3),
        compiler_params=params(),
        name="sections",
    )(*arrived, mass)
    sections = [
        lax.ppermute(
            section,
            ("grid", "side"),
            [
                (tile * sides + side, (tile + step) % groups * sides + (1 - side))
                for tile in range(groups)
                for side in range(sides)
            ],
        )
        for section, step in zip(sections, steps)
    ]
    stride = lev_dev * fields + 1
    stride += -stride % SUBLANES
    result = pl.pallas_call(
        functools.partial(finish_kernel, lev_dev, fields, coarse),
        out_shape=struct(state.shape),
        in_specs=specs(*[VMEM] * 3, *[SMEM] * 3, VMEM, VMEM),
        out_specs=pl.BlockSpec(memory_space=VMEM),
        scratch_shapes=[VMEM(((tiles + 1) * stride, LANES), jnp.float32)],
        compiler_params=params(),
        name="finish",
    )(*sections, *lists, slots, state)
    return (
        result.reshape(fields, tiles, lev_dev, LANES)
        .transpose(2, 0, 1, 3)
        .reshape(1, lev_dev, fields, cell_dev)
    )


def solution(mesh):
    in_specs = (
        P("side", "lev", None, "grid"),
        P("side", None, "grid"),
        P("grid", None),
        P("grid"),
        P("grid", None, None),
        P("grid", None),
        P("grid"),
    )
    out_specs = P("side", "lev", None, "grid")
    return jax.shard_map(
        on_device, mesh=mesh, in_specs=in_specs, out_specs=out_specs, check_vma=False
    )
```

time: 361 us -> 42 us (0.12)
  the two profiles are of different devices: /device:TPU:0 before, /device:TPU:1 now
where the time goes in v1:
time: 42 us; the launch traced here: 41.6 us
  starting transfers between devices  21 us (50%)
  waiting for transfers between devices  9.18 us (22%)
  Pallas kernels  6.96 us (17%)
  local copies, waits for them, and re-layouts  4.36 us (10%)
    ppermute x3, starting transfers between devices, on_device(): lax.ppermute(section, ('grid', 'side'), [(tile * sides + side, (tile + st...  15.6 us
    ppermute x3, waiting for transfers between devices, on_device(): lax.ppermute(section, ('grid', 'side'), [(tile * sides + side, (tile + st...  5.09 us
    unnamed x16, local copies, waits for them, and re-layouts  4.36 us
    pallas_call x1, Pallas kernels, on_device(): pl.pallas_call(functools.partial(produce_kernel, lev_dev, fields, partner...  4.13 us
    ppermute x3, waiting for transfers between devices, on_device(): lax.ppermute(parts[distance], 'lev', [(rank, rank ^ distance) for rank in...  4.08 us
    ppermute x3, starting transfers between devices, on_device(): lax.ppermute(parts[distance], 'lev', [(rank, rank ^ distance) for rank in...  3.37 us
    ppermute x3, starting transfers between devices, on_device(): lax.ppermute(request, ('grid', 'side'), [(tile * sides, (tile + step) % g...  1.98 us
    pallas_call x1, Pallas kernels, on_device(): pl.pallas_call(functools.partial(finish_kernel, lev_dev, fields, coarse),...  1.76 us
  transfers between devices with their start and end apart: 9, of which 5 were waited for; matrix products, arithmetic and copies ran while one was open for 0% of the time, Pallas kernels for 0%

profile of v1, /device:TPU:1, one launch (start us, length us, event | category | flops | bytes accessed | tf_op | source)
XLA Modules:
  0.0 41.6 jit_solution(10823841248470970644)
XLA Ops:
  0.0 0.0 copy-start.6
  0.0 0.0 copy-start.7
  0.0 0.7 %copy-done.4 = s32[1024,1]{0,1:T(1,128)S(1)} copy-done((s32[1024,1]{0,1:T(1,128)S(1)}, s32[1024,1]{0,1:T(1,128)}, u32[]{:S(2)}) %copy-start.4) | copy-done | bytes 4120
  0.7 0.0 copy-done.6
  0.7 0.0 copy-done.7
  0.7 0.7 %copy-done.5 = s32[1024]{0:T(1024)S(1)} copy-done((s32[1024]{0:T(1024)S(1)}, s32[1024]{0:T(1024)}, u32[]{:S(2)}) %copy-start.5) | copy-done | bytes 4120
  1.4 1.1 %lists.1 = (s32[8,128]{1,0:T(8,128)S(1)}, s32[8,128]{1,0:T(8,128)S(1)}, s32[8,128]{1,0:T(8,128)S(1)}, s32[8,128]{1,0:T(8,128)S(1)}, s32[8,128]{1,0:T(8,128)S(1)}) custom-call(s32[8,128]{1,0:T(8,128)S(1)} %bitcast.22, s32[8,128]{1,0:T(8,128)S(1)} %bitcast.23, s32[1,64]{1,0:T(1,128)S(1)} %bitcast.24, s32[1,64]{1,0:T(1,128)S(1)} %bitcast.25), custom_call_target="tpu_custom_call" | custom-call | tf_op jit(solution)/shard_map/lists/pallas_call | solution.py:358
  2.4 0.7 %collective-permute-start = (s32[8,128]{1,0:T(8,128)S(1)}, s32[8,128]{1,0:T(8,128)S(1)}, u32[]{:S(2)}, u32[]{:S(2)}) collective-permute-start(s32[8,128]{1,0:T(8,128)S(1)} %get-tuple-element.19), channel_id=1, source_target_pairs={{0,24},{8,0},{16,8},{24,16},{2,26},{10,2},{18,10},{26,18},{4,28},{... | collective-permute-start | bytes 12296 | tf_op jit(solution)/shard_map/ppermute | solution.py:373
  3.1 0.7 %collective-permute-start.1 = (s32[8,128]{1,0:T(8,128)S(1)}, s32[8,128]{1,0:T(8,128)S(1)}, u32[]{:S(2)}, u32[]{:S(2)}) collective-permute-start(s32[8,128]{1,0:T(8,128)S(1)} %get-tuple-element.20), channel_id=1, source_target_pairs={{0,8},{8,16},{16,24},{24,0},{2,10},{10,18},{18,26},{26,2},{4,12},{... | collective-permute-start | bytes 12296 | tf_op jit(solution)/shard_map/ppermute | solution.py:373
  3.8 0.7 %collective-permute-start.2 = (s32[8,128]{1,0:T(8,128)S(1)}, s32[8,128]{1,0:T(8,128)S(1)}, u32[]{:S(2)}, u32[]{:S(2)}) collective-permute-start(s32[8,128]{1,0:T(8,128)S(1)} %get-tuple-element.21), channel_id=1, source_target_pairs={{0,16},{8,24},{16,0},{24,8},{2,18},{10,26},{18,2},{26,10},{4,20},{... | collective-permute-start | bytes 12296 | tf_op jit(solution)/shard_map/ppermute | solution.py:373
  4.4 0.0 collective-permute-done.refs_0_.refs_3_
  4.5 0.0 collective-permute-done.1.refs_1_.refs_4_
  4.5 0.0 collective-permute-done.2.refs_2_.refs_5_
  4.5 0.0 copy-start
  4.5 1.0 %copy-done = f32[1,2,6,8192]{3,1,2,0:T(2,128)S(1)} copy-done((f32[1,2,6,8192]{3,1,2,0:T(2,128)S(1)}, f32[1,2,6,8192]{3,1,2,0:T(2,128)}, u32[]{:S(2)}) %copy-start) | copy-done | bytes 393240
  5.5 1.0 %copy-done.2 = f32[64,16,128]{2,1,0:T(8,128)S(1)} copy-done((f32[64,16,128]{2,1,0:T(8,128)S(1)}, f32[64,16,128]{2,1,0:T(8,128)}, u32[]{:S(2)}) %copy-start.2) | copy-done | bytes 524312
  6.5 0.9 %copy-done.3 = s32[1,8,8192]{2,1,0:T(8,128)S(1)} copy-done((s32[1,8,8192]{2,1,0:T(8,128)S(1)}, s32[1,8,8192]{2,1,0:T(8,128)}, u32[]{:S(2)}) %copy-start.3) | copy-done | bytes 262168
  7.5 4.1 %produce.1 = (f32[144,128]{1,0:T(8,128)S(1)}, f32[144,128]{1,0:T(8,128)S(1)}, f32[144,128]{1,0:T(8,128)S(1)}, f32[144,128]{1,0:T(8,128)S(1)}, f32[16,128]{1,0:T(8,128)S(1)}) custom-call(s32[8,128]{1,0:T(8,128)S(1)} %get-tuple-element.18.own, s32[8,128]{1,0:T(8,128)S(1)} %collective-permute-done.refs_0_.refs_3_, ...), custom_call_target="tpu_custom_call" | custom-call | tf_op jit(solution)/shard_map/produce/pallas_call | solution.py:382
  11.6 2.1 %collective-permute-start.3 = (f32[144,128]{1,0:T(8,128)S(1)}, f32[144,128]{1,0:T(8,128)S(1)}, u32[]{:S(2)}, u32[]{:S(2)}) collective-permute-start(f32[144,128]{1,0:T(8,128)S(1)} %get-tuple-element.23), channel_id=1, source_target_pairs={{0,2},{2,0},{4,6},{6,4},{1,3},{3,1},{5,7},{7,5},{8,10},{10,8},{12,... | collective-permute-start | bytes 221192 | tf_op jit(solution)/shard_map/ppermute | solution.py:395
  13.7 1.2 %collective-permute-start.4 = (f32[144,128]{1,0:T(8,128)S(1)}, f32[144,128]{1,0:T(8,128)S(1)}, u32[]{:S(2)}, u32[]{:S(2)}) collective-permute-start(f32[144,128]{1,0:T(8,128)S(1)} %get-tuple-element.24), channel_id=1, source_target_pairs={{0,4},{2,6},{4,0},{6,2},{1,5},{3,7},{5,1},{7,3},{8,12},{10,14},{12... | collective-permute-start | bytes 221192 | tf_op jit(solution)/shard_map/ppermute | solution.py:395
  15.0 0.0 collective-permute-start.5
  15.0 0.8 %collective-permute-done.3.refs_1_ = f32[144,128]{1,0:T(8,128)S(1)} collective-permute-done((f32[144,128]{1,0:T(8,128)S(1)}, f32[144,128]{1,0:T(8,128)S(1)}, u32[]{:S(2)}, u32[]{:S(2)}) %collective-permute-start.3) | collective-permute-done | bytes 73760 | tf_op jit(solution)/shard_map/ppermute | solution.py:395
  15.8 1.5 %collective-permute-done.4.refs_2_ = f32[144,128]{1,0:T(8,128)S(1)} collective-permute-done((f32[144,128]{1,0:T(8,128)S(1)}, f32[144,128]{1,0:T(8,128)S(1)}, u32[]{:S(2)}, u32[]{:S(2)}) %collective-permute-start.4) | collective-permute-done | bytes 73760 | tf_op jit(solution)/shard_map/ppermute | solution.py:395
  17.2 1.8 %collective-permute-done.5.refs_3_ = f32[144,128]{1,0:T(8,128)S(1)} collective-permute-done((f32[144,128]{1,0:T(8,128)S(1)}, f32[144,128]{1,0:T(8,128)S(1)}, u32[]{:S(2)}, u32[]{:S(2)}) %collective-permute-start.5) | collective-permute-done | bytes 73760 | tf_op jit(solution)/shard_map/ppermute | solution.py:395
  19.1 15.6 %collective-permute-start.6 = (f32[56,128]{1,0:T(8,128)S(1)}, f32[56,128]{1,0:T(8,128)S(1)}, u32[]{:S(2)}, u32[]{:S(2)}) collective-permute-start(f32[56,128]{1,0:T(8,128)S(1)} %get-tuple-element.27), channel_id=1, source_target_pairs={{0,25},{1,24},{8,1},{9,0},{16,9},{17,8},{24,17},{25,16},{2,27},{3,... | collective-permute-start | bytes 86024 | tf_op jit(solution)/shard_map/ppermute | solution.py:409
  34.7 0.0 collective-permute-start.7
  34.7 0.0 collective-permute-start.8
  34.7 1.0 %collective-permute-done.6.refs_0_ = f32[56,128]{1,0:T(8,128)S(1)} collective-permute-done((f32[56,128]{1,0:T(8,128)S(1)}, f32[56,128]{1,0:T(8,128)S(1)}, u32[]{:S(2)}, u32[]{:S(2)}) %collective-permute-start.6) | collective-permute-done | bytes 28704 | tf_op jit(solution)/shard_map/ppermute | solution.py:409
  35.7 4.1 %collective-permute-done.7.refs_1_ = f32[56,128]{1,0:T(8,128)S(1)} collective-permute-done((f32[56,128]{1,0:T(8,128)S(1)}, f32[56,128]{1,0:T(8,128)S(1)}, u32[]{:S(2)}, u32[]{:S(2)}) %collective-permute-start.7) | collective-permute-done | bytes 28704 | tf_op jit(solution)/shard_map/ppermute | solution.py:409
  39.8 0.0 collective-permute-done.8.refs_2_
  39.8 0.0 copy-done.1
  39.8 1.8 %finish.1 = f32[768,128]{1,0:T(8,128)} custom-call(f32[56,128]{1,0:T(8,128)S(1)} %collective-permute-done.6.refs_0_, f32[56,128]{1,0:T(8,128)S(1)} %collective-permute-done.7.refs_1_, f32[56,128]{1,0:T(8,128)S(1)} %collective-permute-done.8.refs_2_, s32[8,128]{1,0:T(8,128)S(1)} %collective-permute-done.refs_0_.refs_3_, ...), custom_call_target="tpu_custom_call" | custom-call | tf_op jit(solution)/shard_map/finish/pallas_call | solution.py:422
  (6 shorter events, 0.0 us)
Async XLA Ops:
  0.0 0.7 %copy-start.4 = (s32[1024,1]{0,1:T(1,128)S(1)}, s32[1024,1]{0,1:T(1,128)}, u32[]{:S(2)}) copy-start(s32[1024,1]{0,1:T(1,128)} %param.9) | copy-start | bytes 12292
  0.0 0.7 %copy-start.6 = (s32[64,1]{0,1:T(1,128)S(1)}, s32[64,1]{0,1:T(1,128)}, u32[]{:S(2)}) copy-start(s32[64,1]{0,1:T(1,128)} %param.12) | copy-start | bytes 772
  0.0 0.7 %copy-start.7 = (s32[64]{0:T(128)S(1)}, s32[64]{0:T(128)}, u32[]{:S(2)}) copy-start(s32[64]{0:T(128)} %param.13) | copy-start | bytes 772
  0.7 0.7 %copy-start.5 = (s32[1024]{0:T(1024)S(1)}, s32[1024]{0:T(1024)}, u32[]{:S(2)}) copy-start(s32[1024]{0:T(1024)} %param.10) | copy-start | bytes 12292
  2.4 2.0 %collective-permute-start = (s32[8,128]{1,0:T(8,128)S(1)}, s32[8,128]{1,0:T(8,128)S(1)}, u32[]{:S(2)}, u32[]{:S(2)}) collective-permute-start(s32[8,128]{1,0:T(8,128)S(1)} %get-tuple-element.19), channel_id=1, source_target_pairs={{0,24},{8,0},{16,8},{24,16},{2,26},{10,2},{18,10},{26,18},{4,28},{... | collective-permute-start | bytes 12296 | tf_op jit(solution)/shard_map/ppermute | solution.py:373
  3.1 1.4 %collective-permute-start.1 = (s32[8,128]{1,0:T(8,128)S(1)}, s32[8,128]{1,0:T(8,128)S(1)}, u32[]{:S(2)}, u32[]{:S(2)}) collective-permute-start(s32[8,128]{1,0:T(8,128)S(1)} %get-tuple-element.20), channel_id=1, source_target_pairs={{0,8},{8,16},{16,24},{24,0},{2,10},{10,18},{18,26},{26,2},{4,12},{... | collective-permute-start | bytes 12296 | tf_op jit(solution)/shard_map/ppermute | solution.py:373
  3.8 0.7 %collective-permute-start.2 = (s32[8,128]{1,0:T(8,128)S(1)}, s32[8,128]{1,0:T(8,128)S(1)}, u32[]{:S(2)}, u32[]{:S(2)}) collective-permute-start(s32[8,128]{1,0:T(8,128)S(1)} %get-tuple-element.21), channel_id=1, source_target_pairs={{0,16},{8,24},{16,0},{24,8},{2,18},{10,26},{18,2},{26,10},{4,20},{... | collective-permute-start | bytes 12296 | tf_op jit(solution)/shard_map/ppermute | solution.py:373
  4.5 1.0 %copy-start = (f32[1,2,6,8192]{3,1,2,0:T(2,128)S(1)}, f32[1,2,6,8192]{3,1,2,0:T(2,128)}, u32[]{:S(2)}) copy-start(f32[1,2,6,8192]{3,1,2,0:T(2,128)} %param.7) | copy-start | bytes 1179652
  5.5 1.0 %copy-start.2 = (f32[64,16,128]{2,1,0:T(8,128)S(1)}, f32[64,16,128]{2,1,0:T(8,128)}, u32[]{:S(2)}) copy-start(f32[64,16,128]{2,1,0:T(8,128)} %refs_5_.1) | copy-start | bytes 1572868
  6.5 0.9 %copy-start.3 = (s32[1,8,8192]{2,1,0:T(8,128)S(1)}, s32[1,8,8192]{2,1,0:T(8,128)}, u32[]{:S(2)}) copy-start(s32[1,8,8192]{2,1,0:T(8,128)} %param.8) | copy-start | bytes 786436
  7.5 32.4 %copy-start.1 = (f32[1,2,6,8192]{3,1,2,0:T(2,128)S(1)}, f32[1,2,6,8192]{3,1,2,0:T(2,128)}, u32[]{:S(2)}) copy-start(f32[1,2,6,8192]{3,1,2,0:T(2,128)} %param.7) | copy-start | bytes 1179652
  11.6 4.1 %collective-permute-start.3 = (f32[144,128]{1,0:T(8,128)S(1)}, f32[144,128]{1,0:T(8,128)S(1)}, u32[]{:S(2)}, u32[]{:S(2)}) collective-permute-start(f32[144,128]{1,0:T(8,128)S(1)} %get-tuple-element.23), channel_id=1, source_target_pairs={{0,2},{2,0},{4,6},{6,4},{1,3},{3,1},{5,7},{7,5},{8,10},{10,8},{12,... | collective-permute-start | bytes 221192 | tf_op jit(solution)/shard_map/ppermute | solution.py:395
  13.7 3.5 %collective-permute-start.4 = (f32[144,128]{1,0:T(8,128)S(1)}, f32[144,128]{1,0:T(8,128)S(1)}, u32[]{:S(2)}, u32[]{:S(2)}) collective-permute-start(f32[144,128]{1,0:T(8,128)S(1)} %get-tuple-element.24), channel_id=1, source_target_pairs={{0,4},{2,6},{4,0},{6,2},{1,5},{3,7},{5,1},{7,3},{8,12},{10,14},{12... | collective-permute-start | bytes 221192 | tf_op jit(solution)/shard_map/ppermute | solution.py:395
  15.0 4.1 %collective-permute-start.5 = (f32[144,128]{1,0:T(8,128)S(1)}, f32[144,128]{1,0:T(8,128)S(1)}, u32[]{:S(2)}, u32[]{:S(2)}) collective-permute-start(f32[144,128]{1,0:T(8,128)S(1)} %get-tuple-element.25), channel_id=1, source_target_pairs={{0,6},{2,4},{4,2},{6,0},{1,7},{3,5},{5,3},{7,1},{8,14},{10,12},{12... | collective-permute-start | bytes 221192 | tf_op jit(solution)/shard_map/ppermute | solution.py:395
  19.1 16.6 %collective-permute-start.6 = (f32[56,128]{1,0:T(8,128)S(1)}, f32[56,128]{1,0:T(8,128)S(1)}, u32[]{:S(2)}, u32[]{:S(2)}) collective-permute-start(f32[56,128]{1,0:T(8,128)S(1)} %get-tuple-element.27), channel_id=1, source_target_pairs={{0,25},{1,24},{8,1},{9,0},{16,9},{17,8},{24,17},{25,16},{2,27},{3,... | collective-permute-start | bytes 86024 | tf_op jit(solution)/shard_map/ppermute | solution.py:409
  34.7 5.1 %collective-permute-start.7 = (f32[56,128]{1,0:T(8,128)S(1)}, f32[56,128]{1,0:T(8,128)S(1)}, u32[]{:S(2)}, u32[]{:S(2)}) collective-permute-start(f32[56,128]{1,0:T(8,128)S(1)} %get-tuple-element.28), channel_id=1, source_target_pairs={{0,9},{1,8},{8,17},{9,16},{16,25},{17,24},{24,1},{25,0},{2,11},{3,... | collective-permute-start | bytes 86024 | tf_op jit(solution)/shard_map/ppermute | solution.py:409
  34.7 5.1 %collective-permute-start.8 = (f32[56,128]{1,0:T(8,128)S(1)}, f32[56,128]{1,0:T(8,128)S(1)}, u32[]{:S(2)}, u32[]{:S(2)}) collective-permute-start(f32[56,128]{1,0:T(8,128)S(1)} %get-tuple-element.29), channel_id=1, source_target_pairs={{0,17},{1,16},{8,25},{9,24},{16,1},{17,0},{24,9},{25,8},{2,19},{3,... | collective-permute-start | bytes 86024 | tf_op jit(solution)/shard_map/ppermute | solution.py:409

commit v2 on v1

--- a/solution.py
+++ b/solution.py
@@ -8,17 +8,24 @@
 from jax.sharding import PartitionSpec as P
 
 LANES = 128
+LANE_BITS = 7
 SUBLANES = 8
 VALUE_BITS = 16
 ID_BITS = 8
 MESSAGE_ROWS = 8
-FLIPPED = (1, 0, 2)
+ROUNDS = 3
 VMEM = pltpu.VMEM
 SMEM = pltpu.SMEM
 
 
-def grid_steps(groups):
-    return (groups - 1, 1, groups // 2)
+def partner_of(tile, number, groups):
+    if groups == ROUNDS + 1:
+        return tile ^ (number + 1)
+    return (tile + (groups - 1, 1, groups // 2)[number]) % groups
+
+
+def answer_round(number, groups):
+    return number if groups == ROUNDS + 1 else (1, 0, 2)[number]
 
 
 def iota(shape, dimension):
@@ -62,36 +69,39 @@
     return jnp.where(held >= 0, held & ((1 << value_bits) - 1), -1)
 
 
-def list_kernel(groups, panel_owner, panel_cell, block_owner, block_row, *refs):
-    requests, own_ref, slot_ref, owner_pad, row_pad = refs[:3], refs[3], refs[4], refs[5], refs[6]
-    tile = lax.axis_index("grid")
-    blocks = block_owner.shape[1]
-    owner_pad[...] = jnp.full(owner_pad.shape, -1, jnp.int32)
+def list_kernel(groups, owner_ref, block_ref, row_ref, cell_ref, *refs):
+    first, second, own_ref, slot_ref, block_pad, row_pad = refs
+    blocks = block_ref.shape[1]
+    block_pad[...] = jnp.full(block_pad.shape, -1, jnp.int32)
     row_pad[...] = jnp.zeros(row_pad.shape, jnp.int32)
-    owner_pad[0:1, 0:blocks] = block_owner[...]
-    row_pad[0:1, 0:blocks] = block_row[...]
-    owners, cells = panel_owner[...], panel_cell[...]
-    landing = owner_pad[...]
-    lane = iota(landing.shape, 1)
-    marked = row_pad[...] | (lane << VALUE_BITS)
+    block_pad[0:1, 0:blocks] = block_ref[...]
+    row_pad[0:1, 0:blocks] = row_ref[...]
+    tile, side = lax.axis_index("grid"), lax.axis_index("side")
+    owners = owner_ref[...]
+    landing = block_pad[...]
+    marked = row_pad[...] | (iota(landing.shape, 1) << VALUE_BITS)
     half = owners.shape[0] // 2
+    hits = [owners == partner_of(tile, number, groups) for number in range(ROUNDS)]
+    ranks = [rank_of(hit) for hit in hits]
+    cells = cell_ref[...]
     slots = jnp.zeros_like(owners)
     own_ref[...] = jnp.full(own_ref.shape, -1, jnp.int32)
-    for number, step in enumerate(grid_steps(groups)):
-        partner = lax.rem(tile + step, groups)
-        hit = owners == partner
-        rank = rank_of(hit)
+    pages = []
+    for number in range(ROUNDS):
+        partner = partner_of(tile, number, groups)
+        hit, rank = hits[number], ranks[number]
         slots = jnp.where(hit, number * half * LANES + rank, slots)
         wanted = squeeze(hit, rank, cells, VALUE_BITS)
         lands = landing == partner
         block = squeeze(lands, rank_of(lands), marked, VALUE_BITS + ID_BITS)
-        requests[number][...] = jnp.full(requests[number].shape, -1, jnp.int32)
-        requests[number][0:half, :] = jnp.maximum(wanted[0:half], 0)
-        requests[number][half : half + 1, :] = jnp.where(
-            block >= 0, block & ((1 << VALUE_BITS) - 1), -1
-        )[0:1]
+        rows = jnp.where(block >= 0, block & ((1 << VALUE_BITS) - 1), -1)
+        pages.append((jnp.maximum(wanted[0:half], 0), rows[0:1]))
         own_ref[number : number + 1, :] = jnp.where(block >= 0, block >> VALUE_BITS, -1)[0:1]
     slot_ref[...] = slots
+    for target, (here, there) in ((first, (pages[0], pages[2])), (second, (pages[1], pages[1]))):
+        target[...] = jnp.full(target.shape, -1, jnp.int32)
+        target[0:half, :] = jnp.where(side == 0, here[0], there[0])
+        target[half : half + 1, :] = jnp.where(side == 0, here[1], there[1])
 
 
 def gather_lanes(values, index):
@@ -106,7 +116,7 @@
     return values
 
 
-def panel_rows(lev_dev, fields, tiles, lists, group, state, terrain, packed, scratch):
+def panel_rows(lev_dev, fields, tiles, groups, lists, group, state, terrain, packed, scratch):
     levels = SUBLANES
     bits = (levels - 1).bit_length()
     total = jnp.zeros((tiles, LANES), jnp.int32)
@@ -117,10 +127,10 @@
     sub = iota(shape, 0)
     per = SUBLANES // lev_dev
     quarters = lists[0].shape[0] // 2
-    for number in range(3):
+    for number in range(ROUNDS):
         for quarter in range(quarters):
             cells = jnp.broadcast_to(lists[number][quarter : quarter + 1, :], shape)
-            high, low = cells // LANES, cells % LANES
+            high, low = cells >> LANE_BITS, cells & (LANES - 1)
             sums = [jnp.zeros(shape, jnp.float32) for _ in range(fields)]
             for chunk in range(tiles // per):
                 here = high == chunk * per + sub // lev_dev
@@ -134,7 +144,7 @@
                 code = jnp.where(high == chunk * SUBLANES + sub, got, code)
             code = fold(code, 1)
             source = (code >> (bits * sub)) & (levels - 1)
-            section = FLIPPED[number]
+            section = answer_round(number, groups)
             for field in range(fields):
                 both = fold(sums[field], lev_dev)
                 placed = jnp.zeros(shape, jnp.float32)
@@ -155,6 +165,10 @@
 
     def one_tile(index, carry):
         number, quarter = index // quarters, index % quarters
+        pl.when(own[number, quarter * per] >= 0)(lambda: fill_tile(index, number, quarter))
+        return carry
+
+    def fill_tile(index, number, quarter):
         lefts, rights = [], []
         for place in range(per):
             name = own[number, quarter * per + place]
@@ -201,12 +215,11 @@
                 field * levels : (field + 1) * levels
             ]
         mass[pl.ds(index, 1), :] = product[2 * rows : 2 * rows + 1]
-        return carry
-
-    lax.fori_loop(0, 3 * quarters, one_tile, 0)
-
-
-def produce_kernel(lev_dev, fields, partners, own, *refs):
+
+    lax.fori_loop(0, ROUNDS * quarters, one_tile, 0)
+
+
+def produce_kernel(lev_dev, fields, partners, groups, own, *refs):
     lists, state, terrain, weight = refs[:3], refs[3], refs[4], refs[5]
     parts = refs[6 : 6 + partners]
     mass, scratch, packed = refs[6 + partners :]
@@ -216,7 +229,7 @@
     @pl.when(side == 0)
     def _():
         mass[...] = jnp.zeros_like(mass)
-        panel_rows(lev_dev, fields, tiles, lists, group, state, terrain, packed, scratch)
+        panel_rows(lev_dev, fields, tiles, groups, lists, group, state, terrain, packed, scratch)
 
     @pl.when(side == 1)
     def _():
@@ -250,7 +263,7 @@
         section[tail:, :] = jnp.zeros((section.shape[0] - tail, LANES), jnp.float32)
 
 
-def finish_panel(lev_dev, fields, tiles, sections, slots, state, out):
+def finish_panel(lev_dev, fields, tiles, groups, sections, slots, state, out):
     shape = (SUBLANES, LANES)
     sub = iota(shape, 0)
     out[...] = state[...]
@@ -260,14 +273,14 @@
     share = SUBLANES // quarters
     for tile in range(panel_tiles):
         place = jnp.broadcast_to(slots[tile : tile + 1, :], shape)
-        high, low = place // LANES, place % LANES
-        here = [high == number * quarters + sub % quarters for number in range(3)]
+        high, low = place >> LANE_BITS, place & (LANES - 1)
+        here = [high == number * quarters + sub % quarters for number in range(ROUNDS)]
         for level in range(lev_dev):
             for chunk in range(span // SUBLANES):
                 start = level * span + chunk * SUBLANES
                 found = jnp.zeros(shape, jnp.float32)
-                for number in range(3):
-                    values = sections[FLIPPED[number]][start : start + SUBLANES, :]
+                for number in range(ROUNDS):
+                    values = sections[answer_round(number, groups)][start : start + SUBLANES, :]
                     found = jnp.where(here[number], gather_lanes(values, low), found)
                 for part in range(share):
                     field = chunk * share + part
@@ -286,7 +299,7 @@
     quarters = lists[0].shape[0] // 2
     rows = sections[0].shape[0] // quarters
     lane = iota((rows, LANES), 1)
-    for number in range(3):
+    for number in range(ROUNDS):
         for quarter in range(quarters):
             chunk = sections[number][pl.ds(quarter, rows, stride=quarters), :]
             for place in range(per):
@@ -308,7 +321,7 @@
             out[here, :] = (state[here, :] + feedback) * scale
 
 
-def finish_kernel(lev_dev, fields, coarse, *refs):
+def finish_kernel(lev_dev, fields, coarse, groups, *refs):
     sections, lists, slots, state, out, landed = refs[:3], refs[3:6], *refs[6:]
     tiles = state.shape[0] // (fields * lev_dev)
     side = lax.axis_index("side")
@@ -319,7 +332,7 @@
 
     @pl.when(side == 1)
     def _():
-        finish_panel(lev_dev, fields, tiles, sections, slots, state, out)
+        finish_panel(lev_dev, fields, tiles, groups, sections, slots, state, out)
 
 
 def specs(*spaces):
@@ -339,7 +352,6 @@
 ):
     groups, partners = lax.axis_size("grid"), lax.axis_size("lev")
     sides = lax.axis_size("side")
-    steps = grid_steps(groups)
     _, lev_dev, fields, cell_dev = model_state.shape
     levels = terrain_level.shape[1]
     tiles = cell_dev // LANES
@@ -355,32 +367,38 @@
         terrain_level.reshape(levels, tiles, LANES).transpose(1, 0, 2).reshape(tiles * levels, LANES)
     )
     message = struct((MESSAGE_ROWS, LANES), jnp.int32)
-    *requests, own, slots = pl.pallas_call(
+    page = struct((panel_tiles, LANES), jnp.int32)
+    first, second, own, slots = pl.pallas_call(
         functools.partial(list_kernel, groups),
-        out_shape=[message] * 4 + [struct((panel_tiles, LANES), jnp.int32)],
+        out_shape=[message] * 3 + [page],
         in_specs=specs(*[VMEM] * 4),
-        out_specs=specs(*[VMEM] * 5),
+        out_specs=specs(*[VMEM] * 4),
         scratch_shapes=[VMEM((SUBLANES, LANES), jnp.int32)] * 2,
+        cost_estimate=pl.CostEstimate(flops=0, bytes_accessed=40_000_000, transcendentals=0),
         compiler_params=params(),
         name="lists",
     )(
-        panel_owner.reshape(panel_tiles, LANES),
-        panel_cell.reshape(panel_tiles, LANES),
+        panel_owner.reshape(page.shape),
         block_owner.reshape(1, blocks),
         block_row.reshape(1, blocks),
-    )
-    lists = [
-        lax.ppermute(
-            request,
-            ("grid", "side"),
-            [(tile * sides, (tile + step) % groups * sides) for tile in range(groups)],
-        )
-        for request, step in zip(requests, steps)
-    ]
-    scratch_rows = 3 * fields * quarters
+        panel_cell.reshape(page.shape),
+    )
+
+    def towards(number_of, cross):
+        return [
+            (tile * sides + side, partner_of(tile, number_of(side), groups) * sides + (side ^ cross))
+            for tile in range(groups)
+            for side in range(sides)
+        ]
+
+    first = lax.ppermute(first, ("grid", "side"), towards(lambda side: 2 * side, 0))
+    second = lax.ppermute(second, ("grid", "side"), towards(lambda side: 1, 0))
+    third = lax.ppermute(first, "side", [(0, 1), (1, 0)])
+    lists = [first, second, third]
+    scratch_rows = ROUNDS * fields * quarters
     part = struct((lev_dev * scratch_rows, LANES))
     *parts, mass = pl.pallas_call(
-        functools.partial(produce_kernel, lev_dev, fields, partners),
+        functools.partial(produce_kernel, lev_dev, fields, partners, groups),
         out_shape=[part] * partners + [struct((2 * SUBLANES, LANES))],
         in_specs=specs(SMEM, *[VMEM] * 6),
         out_specs=specs(*[VMEM] * (partners + 1)),
@@ -393,7 +411,7 @@
     )(own, *lists, state, terrain, block_weight)
     arrived = [parts[0]] + [
         lax.ppermute(parts[distance], "lev", [(rank, rank ^ distance) for rank in range(partners)])
-        for distance in range(1, partners)
+        for distance in range(partners - 1, 0, -1)
     ]
     section_rows = lev_dev * fields * quarters + quarters
     section_rows += -section_rows % SUBLANES
@@ -406,21 +424,13 @@
         name="sections",
     )(*arrived, mass)
     sections = [
-        lax.ppermute(
-            section,
-            ("grid", "side"),
-            [
-                (tile * sides + side, (tile + step) % groups * sides + (1 - side))
-                for tile in range(groups)
-                for side in range(sides)
-            ],
-        )
-        for section, step in zip(sections, steps)
-    ]
+        lax.ppermute(sections[number], ("grid", "side"), towards(lambda side: number, 1))
+        for number in range(ROUNDS - 1, -1, -1)
+    ][::-1]
     stride = lev_dev * fields + 1
     stride += -stride % SUBLANES
     result = pl.pallas_call(
-        functools.partial(finish_kernel, lev_dev, fields, coarse),
+        functools.partial(finish_kernel, lev_dev, fields, coarse, groups),
         out_shape=struct(state.shape),
         in_specs=specs(*[VMEM] * 3, *[SMEM] * 3, VMEM, VMEM),
         out_specs=pl.BlockSpec(memory_space=VMEM),

time: 42 us -> 34.1 us (0.81)
  the two profiles are of different devices: /device:TPU:1 before, /device:TPU:0 now
where the time goes in v2:
time: 34.1 us; the launch traced here: 33.8 us
  starting transfers between devices  13.1 us (38%)
  waiting for transfers between devices  10.5 us (31%)
  Pallas kernels  5.79 us (17%)
  local copies, waits for them, and re-layouts  4.37 us (13%)
    ppermute x3, waiting for transfers between devices, on_device(): lax.ppermute(parts[distance], 'lev', [(rank, rank ^ distance) for rank in...  4.37 us
    unnamed x16, local copies, waits for them, and re-layouts  4.37 us
    ppermute x3, waiting for transfers between devices, on_device(): lax.ppermute(sections[number], ('grid', 'side'), towards(lambda side: num...  4.23 us
    ppermute x3, starting transfers between devices, on_device(): lax.ppermute(sections[number], ('grid', 'side'), towards(lambda side: num...  3.88 us
    ppermute x3, starting transfers between devices, on_device(): lax.ppermute(parts[distance], 'lev', [(rank, rank ^ distance) for rank in...  3.55 us
    ppermute x1, starting transfers between devices, on_device(): lax.ppermute(first, ('grid', 'side'), towards(lambda side: 2 * side, 0))  3.09 us
    pallas_call x1, Pallas kernels, on_device(): pl.pallas_call(functools.partial(finish_kernel, lev_dev, fields, coarse,...  2.61 us
    ppermute x1, starting transfers between devices, on_device(): second = lax.ppermute(second, ('grid', 'side'), towards(lambda side: 1, 0))  2.59 us
  transfers between devices with their start and end apart: 9, of which 6 were waited for; matrix products, arithmetic and copies ran while one was open for 0% of the time, Pallas kernels for 0%

profile of v2, /device:TPU:0, one launch (start us, length us, event | category | flops | bytes accessed | tf_op | source)
XLA Modules:
  0.0 33.8 jit_solution(12217426129598453718)
XLA Ops:
  0.0 0.0 copy-start.4
  0.0 0.0 copy-start.6
  0.0 0.0 copy-start.7
  0.0 0.7 %copy-done.4 = s32[1024,1]{0,1:T(1,128)S(1)} copy-done((s32[1024,1]{0,1:T(1,128)S(1)}, s32[1024,1]{0,1:T(1,128)}, u32[]{:S(2)}) %copy-start.4) | copy-done | bytes 4120
  0.7 0.0 copy-done.6
  0.7 0.0 copy-done.7
  0.7 0.7 %copy-done.5 = s32[1024]{0:T(1024)S(1)} copy-done((s32[1024]{0:T(1024)S(1)}, s32[1024]{0:T(1024)}, u32[]{:S(2)}) %copy-start.5) | copy-done | bytes 4120
  1.4 1.1 %lists.1 = (s32[8,128]{1,0:T(8,128)S(1)}, s32[8,128]{1,0:T(8,128)S(1)}, s32[8,128]{1,0:T(8,128)S(1)}, s32[8,128]{1,0:T(8,128)S(1)}) custom-call(s32[8,128]{1,0:T(8,128)S(1)} %bitcast.22, s32[1,64]{1,0:T(1,128)S(1)} %bitcast.24, s32[1,64]{1,0:T(1,128)S(1)} %bitcast.25, s32[8,128]{1,0:T(8,128)S(1)} %bitcast.23), custom_call_target="tpu_custom_call" | custom-call | bytes 40000000 | tf_op jit(solution)/shard_map/lists/pallas_call | solution.py:371
  2.4 3.1 %collective-permute-start = (s32[8,128]{1,0:T(8,128)S(1)}, s32[8,128]{1,0:T(8,128)S(1)}, u32[]{:S(2)}, u32[]{:S(2)}) collective-permute-start(s32[8,128]{1,0:T(8,128)S(1)} %get-tuple-element.18), channel_id=1, source_target_pairs={{0,8},{1,25},{8,0},{9,17},{16,24},{17,9},{24,16},{25,1},{2,10},{3,... | collective-permute-start | bytes 12296 | tf_op jit(solution)/shard_map/ppermute | solution.py:394
  5.5 2.6 %collective-permute-start.1 = (s32[8,128]{1,0:T(8,128)S(1)}, s32[8,128]{1,0:T(8,128)S(1)}, u32[]{:S(2)}, u32[]{:S(2)}) collective-permute-start(s32[8,128]{1,0:T(8,128)S(1)} %get-tuple-element.19), channel_id=1, source_target_pairs={{0,16},{1,17},{8,24},{9,25},{16,0},{17,1},{24,8},{25,9},{2,18},{3,... | collective-permute-start | bytes 12296 | tf_op jit(solution)/shard_map/ppermute | solution.py:395
  8.1 0.0 collective-permute-done.refs_0_.refs_3_
  8.1 0.0 collective-permute-start.2
  8.1 1.9 %collective-permute-done.1.refs_1_.refs_4_ = s32[8,128]{1,0:T(8,128)S(1)} collective-permute-done((s32[8,128]{1,0:T(8,128)S(1)}, s32[8,128]{1,0:T(8,128)S(1)}, u32[]{:S(2)}, u32[]{:S(2)}) %collective-permute-start.1) | collective-permute-done | bytes 4128 | tf_op jit(solution)/shard_map/ppermute | solution.py:395
  10.0 0.0 collective-permute-done.2.refs_2_.refs_5_
  10.0 1.0 %copy-done = f32[1,2,6,8192]{3,1,2,0:T(2,128)S(1)} copy-done((f32[1,2,6,8192]{3,1,2,0:T(2,128)S(1)}, f32[1,2,6,8192]{3,1,2,0:T(2,128)}, u32[]{:S(2)}) %copy-start) | copy-done | bytes 393240
  11.0 1.0 %copy-done.2 = f32[64,16,128]{2,1,0:T(8,128)S(1)} copy-done((f32[64,16,128]{2,1,0:T(8,128)S(1)}, f32[64,16,128]{2,1,0:T(8,128)}, u32[]{:S(2)}) %copy-start.2) | copy-done | bytes 524312
  12.1 0.9 %copy-done.3 = s32[1,8,8192]{2,1,0:T(8,128)S(1)} copy-done((s32[1,8,8192]{2,1,0:T(8,128)S(1)}, s32[1,8,8192]{2,1,0:T(8,128)}, u32[]{:S(2)}) %copy-start.3) | copy-done | bytes 262168
  13.0 2.1 %produce.1 = (f32[144,128]{1,0:T(8,128)S(1)}, f32[144,128]{1,0:T(8,128)S(1)}, f32[144,128]{1,0:T(8,128)S(1)}, f32[144,128]{1,0:T(8,128)S(1)}, f32[16,128]{1,0:T(8,128)S(1)}) custom-call(s32[8,128]{1,0:T(8,128)S(1)} %get-tuple-element.17.own, s32[8,128]{1,0:T(8,128)S(1)} %collective-permute-done.refs_0_.refs_3_, ...), custom_call_target="tpu_custom_call" | custom-call | tf_op jit(solution)/shard_map/produce/pallas_call | solution.py:400
  15.1 2.5 %collective-permute-start.3 = (f32[144,128]{1,0:T(8,128)S(1)}, f32[144,128]{1,0:T(8,128)S(1)}, u32[]{:S(2)}, u32[]{:S(2)}) collective-permute-start(f32[144,128]{1,0:T(8,128)S(1)} %get-tuple-element.21), channel_id=1, source_target_pairs={{0,6},{2,4},{4,2},{6,0},{1,7},{3,5},{5,3},{7,1},{8,14},{10,12},{12... | collective-permute-start | bytes 221192 | tf_op jit(solution)/shard_map/ppermute | solution.py:413
  17.7 0.5 %collective-permute-start.4 = (f32[144,128]{1,0:T(8,128)S(1)}, f32[144,128]{1,0:T(8,128)S(1)}, u32[]{:S(2)}, u32[]{:S(2)}) collective-permute-start(f32[144,128]{1,0:T(8,128)S(1)} %get-tuple-element.22), channel_id=1, source_target_pairs={{0,4},{2,6},{4,0},{6,2},{1,5},{3,7},{5,1},{7,3},{8,12},{10,14},{12... | collective-permute-start | bytes 221192 | tf_op jit(solution)/shard_map/ppermute | solution.py:413
  18.2 0.5 %collective-permute-start.5 = (f32[144,128]{1,0:T(8,128)S(1)}, f32[144,128]{1,0:T(8,128)S(1)}, u32[]{:S(2)}, u32[]{:S(2)}) collective-permute-start(f32[144,128]{1,0:T(8,128)S(1)} %get-tuple-element.23), channel_id=1, source_target_pairs={{0,2},{2,0},{4,6},{6,4},{1,3},{3,1},{5,7},{7,5},{8,10},{10,8},{12,... | collective-permute-start | bytes 221192 | tf_op jit(solution)/shard_map/ppermute | solution.py:413
  18.7 1.8 %collective-permute-done.3.refs_1_ = f32[144,128]{1,0:T(8,128)S(1)} collective-permute-done((f32[144,128]{1,0:T(8,128)S(1)}, f32[144,128]{1,0:T(8,128)S(1)}, u32[]{:S(2)}, u32[]{:S(2)}) %collective-permute-start.3) | collective-permute-done | bytes 73760 | tf_op jit(solution)/shard_map/ppermute | solution.py:413
  20.5 2.0 %collective-permute-done.4.refs_2_ = f32[144,128]{1,0:T(8,128)S(1)} collective-permute-done((f32[144,128]{1,0:T(8,128)S(1)}, f32[144,128]{1,0:T(8,128)S(1)}, u32[]{:S(2)}, u32[]{:S(2)}) %collective-permute-start.4) | collective-permute-done | bytes 73760 | tf_op jit(solution)/shard_map/ppermute | solution.py:413
  22.4 0.6 %collective-permute-done.5.refs_3_ = f32[144,128]{1,0:T(8,128)S(1)} collective-permute-done((f32[144,128]{1,0:T(8,128)S(1)}, f32[144,128]{1,0:T(8,128)S(1)}, u32[]{:S(2)}, u32[]{:S(2)}) %collective-permute-start.5) | collective-permute-done | bytes 73760 | tf_op jit(solution)/shard_map/ppermute | solution.py:413
  23.1 0.1 collective-permute-start.6
  23.2 2.9 %collective-permute-start.7 = (f32[56,128]{1,0:T(8,128)S(1)}, f32[56,128]{1,0:T(8,128)S(1)}, u32[]{:S(2)}, u32[]{:S(2)}) collective-permute-start(f32[56,128]{1,0:T(8,128)S(1)} %get-tuple-element.26), channel_id=1, source_target_pairs={{0,17},{1,16},{8,25},{9,24},{16,1},{17,0},{24,9},{25,8},{2,19},{3,... | collective-permute-start | bytes 86024 | tf_op jit(solution)/shard_map/ppermute | solution.py:427
  26.1 0.9 %collective-permute-start.8 = (f32[56,128]{1,0:T(8,128)S(1)}, f32[56,128]{1,0:T(8,128)S(1)}, u32[]{:S(2)}, u32[]{:S(2)}) collective-permute-start(f32[56,128]{1,0:T(8,128)S(1)} %get-tuple-element.27), channel_id=1, source_target_pairs={{0,25},{1,24},{8,17},{9,16},{16,9},{17,8},{24,1},{25,0},{2,27},{3,... | collective-permute-start | bytes 86024 | tf_op jit(solution)/shard_map/ppermute | solution.py:427
  27.0 0.0 collective-permute-done.6.refs_0_
  27.0 0.7 %collective-permute-done.7.refs_1_ = f32[56,128]{1,0:T(8,128)S(1)} collective-permute-done((f32[56,128]{1,0:T(8,128)S(1)}, f32[56,128]{1,0:T(8,128)S(1)}, u32[]{:S(2)}, u32[]{:S(2)}) %collective-permute-start.7) | collective-permute-done | bytes 28704 | tf_op jit(solution)/shard_map/ppermute | solution.py:427
  27.6 3.6 %collective-permute-done.8.refs_2_ = f32[56,128]{1,0:T(8,128)S(1)} collective-permute-done((f32[56,128]{1,0:T(8,128)S(1)}, f32[56,128]{1,0:T(8,128)S(1)}, u32[]{:S(2)}, u32[]{:S(2)}) %collective-permute-start.8) | collective-permute-done | bytes 28704 | tf_op jit(solution)/shard_map/ppermute | solution.py:427
  31.2 0.0 copy-done.1
  31.2 2.6 %finish.1 = f32[768,128]{1,0:T(8,128)} custom-call(f32[56,128]{1,0:T(8,128)S(1)} %collective-permute-done.6.refs_0_, f32[56,128]{1,0:T(8,128)S(1)} %collective-permute-done.7.refs_1_, f32[56,128]{1,0:T(8,128)S(1)} %collective-permute-done.8.refs_2_, s32[8,128]{1,0:T(8,128)S(1)} %collective-permute-done.refs_0_.refs_3_, ...), custom_call_target="tpu_custom_call" | custom-call | tf_op jit(solution)/shard_map/finish/pallas_call | solution.py:432
  (6 shorter events, 0.0 us)
Async XLA Ops:
  0.0 0.7 %copy-start.4 = (s32[1024,1]{0,1:T(1,128)S(1)}, s32[1024,1]{0,1:T(1,128)}, u32[]{:S(2)}) copy-start(s32[1024,1]{0,1:T(1,128)} %param.9) | copy-start | bytes 12292
  0.0 0.7 %copy-start.6 = (s32[64,1]{0,1:T(1,128)S(1)}, s32[64,1]{0,1:T(1,128)}, u32[]{:S(2)}) copy-start(s32[64,1]{0,1:T(1,128)} %param.12) | copy-start | bytes 772
  0.0 0.7 %copy-start.7 = (s32[64]{0:T(128)S(1)}, s32[64]{0:T(128)}, u32[]{:S(2)}) copy-start(s32[64]{0:T(128)} %param.13) | copy-start | bytes 772
  0.7 0.7 %copy-start.5 = (s32[1024]{0:T(1024)S(1)}, s32[1024]{0:T(1024)}, u32[]{:S(2)}) copy-start(s32[1024]{0:T(1024)} %param.10) | copy-start | bytes 12292
  2.4 5.7 %collective-permute-start = (s32[8,128]{1,0:T(8,128)S(1)}, s32[8,128]{1,0:T(8,128)S(1)}, u32[]{:S(2)}, u32[]{:S(2)}) collective-permute-start(s32[8,128]{1,0:T(8,128)S(1)} %get-tuple-element.18), channel_id=1, source_target_pairs={{0,8},{1,25},{8,0},{9,17},{16,24},{17,9},{24,16},{25,1},{2,10},{3,... | collective-permute-start | bytes 12296 | tf_op jit(solution)/shard_map/ppermute | solution.py:394
  5.5 4.5 %collective-permute-start.1 = (s32[8,128]{1,0:T(8,128)S(1)}, s32[8,128]{1,0:T(8,128)S(1)}, u32[]{:S(2)}, u32[]{:S(2)}) collective-permute-start(s32[8,128]{1,0:T(8,128)S(1)} %get-tuple-element.19), channel_id=1, source_target_pairs={{0,16},{1,17},{8,24},{9,25},{16,0},{17,1},{24,8},{25,9},{2,18},{3,... | collective-permute-start | bytes 12296 | tf_op jit(solution)/shard_map/ppermute | solution.py:395
  8.1 1.9 %collective-permute-start.2 = (s32[8,128]{1,0:T(8,128)S(1)}, s32[8,128]{1,0:T(8,128)S(1)}, u32[]{:S(2)}, u32[]{:S(2)}) collective-permute-start(s32[8,128]{1,0:T(8,128)S(1)} %collective-permute-done.refs_0_.refs_3_), channel_id=1, source_target_pairs={{0,1},{1,0},{2,3},{3,2},{4,5},{5,4},{6,7},{7,6},{8,9},{9,8},{10,11... | collective-permute-start | bytes 12296 | tf_op jit(solution)/shard_map/ppermute | solution.py:396
  10.0 1.0 %copy-start = (f32[1,2,6,8192]{3,1,2,0:T(2,128)S(1)}, f32[1,2,6,8192]{3,1,2,0:T(2,128)}, u32[]{:S(2)}) copy-start(f32[1,2,6,8192]{3,1,2,0:T(2,128)} %param.7) | copy-start | bytes 1179652
  11.0 1.0 %copy-start.2 = (f32[64,16,128]{2,1,0:T(8,128)S(1)}, f32[64,16,128]{2,1,0:T(8,128)}, u32[]{:S(2)}) copy-start(f32[64,16,128]{2,1,0:T(8,128)} %refs_5_.1) | copy-start | bytes 1572868
  12.1 0.9 %copy-start.3 = (s32[1,8,8192]{2,1,0:T(8,128)S(1)}, s32[1,8,8192]{2,1,0:T(8,128)}, u32[]{:S(2)}) copy-start(s32[1,8,8192]{2,1,0:T(8,128)} %param.8) | copy-start | bytes 786436
  13.0 18.2 %copy-start.1 = (f32[1,2,6,8192]{3,1,2,0:T(2,128)S(1)}, f32[1,2,6,8192]{3,1,2,0:T(2,128)}, u32[]{:S(2)}) copy-start(f32[1,2,6,8192]{3,1,2,0:T(2,128)} %param.7) | copy-start | bytes 1179652
  15.1 5.3 %collective-permute-start.3 = (f32[144,128]{1,0:T(8,128)S(1)}, f32[144,128]{1,0:T(8,128)S(1)}, u32[]{:S(2)}, u32[]{:S(2)}) collective-permute-start(f32[144,128]{1,0:T(8,128)S(1)} %get-tuple-element.21), channel_id=1, source_target_pairs={{0,6},{2,4},{4,2},{6,0},{1,7},{3,5},{5,3},{7,1},{8,14},{10,12},{12... | collective-permute-start | bytes 221192 | tf_op jit(solution)/shard_map/ppermute | solution.py:413
  17.7 4.8 %collective-permute-start.4 = (f32[144,128]{1,0:T(8,128)S(1)}, f32[144,128]{1,0:T(8,128)S(1)}, u32[]{:S(2)}, u32[]{:S(2)}) collective-permute-start(f32[144,128]{1,0:T(8,128)S(1)} %get-tuple-element.22), channel_id=1, source_target_pairs={{0,4},{2,6},{4,0},{6,2},{1,5},{3,7},{5,1},{7,3},{8,12},{10,14},{12... | collective-permute-start | bytes 221192 | tf_op jit(solution)/shard_map/ppermute | solution.py:413
  18.2 4.9 %collective-permute-start.5 = (f32[144,128]{1,0:T(8,128)S(1)}, f32[144,128]{1,0:T(8,128)S(1)}, u32[]{:S(2)}, u32[]{:S(2)}) collective-permute-start(f32[144,128]{1,0:T(8,128)S(1)} %get-tuple-element.23), channel_id=1, source_target_pairs={{0,2},{2,0},{4,6},{6,4},{1,3},{3,1},{5,7},{7,5},{8,10},{10,8},{12,... | collective-permute-start | bytes 221192 | tf_op jit(solution)/shard_map/ppermute | solution.py:413
  23.1 3.9 %collective-permute-start.6 = (f32[56,128]{1,0:T(8,128)S(1)}, f32[56,128]{1,0:T(8,128)S(1)}, u32[]{:S(2)}, u32[]{:S(2)}) collective-permute-start(f32[56,128]{1,0:T(8,128)S(1)} %get-tuple-element.25), channel_id=1, source_target_pairs={{0,9},{1,8},{8,1},{9,0},{16,25},{17,24},{24,17},{25,16},{2,11},{3,... | collective-permute-start | bytes 86024 | tf_op jit(solution)/shard_map/ppermute | solution.py:427
  23.2 4.5 %collective-permute-start.7 = (f32[56,128]{1,0:T(8,128)S(1)}, f32[56,128]{1,0:T(8,128)S(1)}, u32[]{:S(2)}, u32[]{:S(2)}) collective-permute-start(f32[56,128]{1,0:T(8,128)S(1)} %get-tuple-element.26), channel_id=1, source_target_pairs={{0,17},{1,16},{8,25},{9,24},{16,1},{17,0},{24,9},{25,8},{2,19},{3,... | collective-permute-start | bytes 86024 | tf_op jit(solution)/shard_map/ppermute | solution.py:427
  26.1 5.1 %collective-permute-start.8 = (f32[56,128]{1,0:T(8,128)S(1)}, f32[56,128]{1,0:T(8,128)S(1)}, u32[]{:S(2)}, u32[]{:S(2)}) collective-permute-start(f32[56,128]{1,0:T(8,128)S(1)} %get-tuple-element.27), channel_id=1, source_target_pairs={{0,25},{1,24},{8,17},{9,16},{16,9},{17,8},{24,1},{25,0},{2,27},{3,... | collective-permute-start | bytes 86024 | tf_op jit(solution)/shard_map/ppermute | solution.py:427

commit v3 on v2

--- a/solution.py
+++ b/solution.py
@@ -13,7 +13,9 @@
 VALUE_BITS = 16
 ID_BITS = 8
 MESSAGE_ROWS = 8
+HELD_ROWS = 16
 ROUNDS = 3
+TOGETHER = 2
 VMEM = pltpu.VMEM
 SMEM = pltpu.SMEM
 
@@ -69,8 +71,15 @@
     return jnp.where(held >= 0, held & ((1 << value_bits) - 1), -1)
 
 
-def list_kernel(groups, owner_ref, block_ref, row_ref, cell_ref, *refs):
-    first, second, own_ref, slot_ref, block_pad, row_pad = refs
+def list_kernel(groups, owner_ref, block_ref, row_ref, *refs):
+    sources, (first, second, own_ref, slot_ref, *kept) = refs[:4], refs[4:11]
+    cell_ref, block_pad, row_pad, sems = refs[11:]
+    copies = [
+        pltpu.make_async_copy(source, target, sems.at[index])
+        for index, (source, target) in enumerate(zip(sources, (cell_ref, *kept)))
+    ]
+    for copy in copies:
+        copy.start()
     blocks = block_ref.shape[1]
     block_pad[...] = jnp.full(block_pad.shape, -1, jnp.int32)
     row_pad[...] = jnp.zeros(row_pad.shape, jnp.int32)
@@ -83,6 +92,7 @@
     half = owners.shape[0] // 2
     hits = [owners == partner_of(tile, number, groups) for number in range(ROUNDS)]
     ranks = [rank_of(hit) for hit in hits]
+    copies[0].wait()
     cells = cell_ref[...]
     slots = jnp.zeros_like(owners)
     own_ref[...] = jnp.full(own_ref.shape, -1, jnp.int32)
@@ -102,10 +112,12 @@
         target[...] = jnp.full(target.shape, -1, jnp.int32)
         target[0:half, :] = jnp.where(side == 0, here[0], there[0])
         target[half : half + 1, :] = jnp.where(side == 0, here[1], there[1])
+    for copy in copies[1:]:
+        copy.wait()
 
 
 def gather_lanes(values, index):
-    return jnp.take_along_axis(values, index, axis=1)
+    return jnp.take_along_axis(values, index, axis=1, mode="promise_in_bounds")
 
 
 def fold(values, least):
@@ -132,18 +144,17 @@
             cells = jnp.broadcast_to(lists[number][quarter : quarter + 1, :], shape)
             high, low = cells >> LANE_BITS, cells & (LANES - 1)
             sums = [jnp.zeros(shape, jnp.float32) for _ in range(fields)]
+            code = jnp.zeros(shape, jnp.int32)
             for chunk in range(tiles // per):
                 here = high == chunk * per + sub // lev_dev
                 for field in range(fields):
                     start = field * tiles * lev_dev + chunk * SUBLANES
                     got = gather_lanes(state[start : start + SUBLANES, :], low)
                     sums[field] = jnp.where(here, got, sums[field])
-            code = jnp.zeros(shape, jnp.int32)
             for chunk in range(tiles // SUBLANES):
                 got = gather_lanes(packed[chunk * SUBLANES : (chunk + 1) * SUBLANES, :], low)
                 code = jnp.where(high == chunk * SUBLANES + sub, got, code)
-            code = fold(code, 1)
-            source = (code >> (bits * sub)) & (levels - 1)
+            source = (fold(code, 1) >> (bits * sub)) & (levels - 1)
             section = answer_round(number, groups)
             for field in range(fields):
                 both = fold(sums[field], lev_dev)
@@ -163,9 +174,14 @@
     per = LANES // coarse
     quarters = tiles // 2 // per
 
-    def one_tile(index, carry):
-        number, quarter = index // quarters, index % quarters
-        pl.when(own[number, quarter * per] >= 0)(lambda: fill_tile(index, number, quarter))
+    def some_tiles(index, carry):
+        number, quarter = index // (quarters // TOGETHER), index % (quarters // TOGETHER) * TOGETHER
+
+        @pl.when(own[number, quarter * per] >= 0)
+        def _():
+            for more in range(TOGETHER):
+                fill_tile(number * quarters + quarter + more, number, quarter + more)
+
         return carry
 
     def fill_tile(index, number, quarter):
@@ -216,7 +232,7 @@
             ]
         mass[pl.ds(index, 1), :] = product[2 * rows : 2 * rows + 1]
 
-    lax.fori_loop(0, ROUNDS * quarters, one_tile, 0)
+    lax.fori_loop(0, ROUNDS * quarters // TOGETHER, some_tiles, 0)
 
 
 def produce_kernel(lev_dev, fields, partners, groups, own, *refs):
@@ -263,76 +279,125 @@
         section[tail:, :] = jnp.zeros((section.shape[0] - tail, LANES), jnp.float32)
 
 
-def finish_panel(lev_dev, fields, tiles, groups, sections, slots, state, out):
+def place_panel(lev_dev, fields, number, section, slots, held):
     shape = (SUBLANES, LANES)
     sub = iota(shape, 0)
-    out[...] = state[...]
     panel_tiles = slots.shape[0]
     quarters = panel_tiles // 2
-    span = fields * quarters
-    share = SUBLANES // quarters
+    chunks = lev_dev * fields * quarters // SUBLANES
     for tile in range(panel_tiles):
         place = jnp.broadcast_to(slots[tile : tile + 1, :], shape)
-        high, low = place >> LANE_BITS, place & (LANES - 1)
-        here = [high == number * quarters + sub % quarters for number in range(ROUNDS)]
-        for level in range(lev_dev):
-            for chunk in range(span // SUBLANES):
-                start = level * span + chunk * SUBLANES
-                found = jnp.zeros(shape, jnp.float32)
-                for number in range(ROUNDS):
-                    values = sections[answer_round(number, groups)][start : start + SUBLANES, :]
-                    found = jnp.where(here[number], gather_lanes(values, low), found)
-                for part in range(share):
-                    field = chunk * share + part
-                    rim = jnp.sum(
-                        jnp.where(sub // quarters == part, found, 0.0), axis=0, keepdims=True
-                    )
-                    row = (field * tiles + tile) * lev_dev + level
-                    out[row : row + 1, :] = 0.5 * (state[row : row + 1, :] + rim)
-
-
-def finish_coarse(lev_dev, fields, tiles, coarse, sections, lists, state, out, landed):
+        here = place >> LANE_BITS == number * quarters + sub % quarters
+        for chunk in range(chunks):
+            got = gather_lanes(
+                section[chunk * SUBLANES : (chunk + 1) * SUBLANES, :], place & (LANES - 1)
+            )
+            row = (tile * chunks + chunk) * SUBLANES
+            held[row : row + SUBLANES, :] = jnp.where(here, got, held[row : row + SUBLANES, :])
+
+
+def place_blocks(coarse, spare, section, runs, held):
     per = LANES // coarse
-    kinds = lev_dev * fields + 1
-    stride = landed.shape[0] // (tiles + 1)
-    landed[...] = jnp.zeros_like(landed)
-    quarters = lists[0].shape[0] // 2
-    rows = sections[0].shape[0] // quarters
-    lane = iota((rows, LANES), 1)
-    for number in range(ROUNDS):
-        for quarter in range(quarters):
-            chunk = sections[number][pl.ds(quarter, rows, stride=quarters), :]
-            for place in range(per):
-                run = lists[number][quarters, quarter * per + place]
-                run = jnp.where(run < 0, tiles * per, run)
-                tile, offset = run // per, run % per
-                piece = jnp.where(lane // coarse == place, chunk, 0.0)
-                turn = lax.rem(offset + per - place, per) * coarse
-                start = pl.multiple_of(tile * stride, SUBLANES)
-                landed[pl.ds(start, rows), :] = landed[pl.ds(start, rows), :] + pltpu.roll(
-                    piece, turn, 1
+    quarters = section.shape[0] // HELD_ROWS
+    lane = iota((HELD_ROWS, LANES), 1)
+    for quarter in range(quarters):
+        chunk = section[pl.ds(quarter, HELD_ROWS, stride=quarters), :]
+        for place in range(per):
+            run = runs[quarters, quarter * per + place]
+            run = jnp.where(run < 0, spare * per, run)
+            turn = (run + (per - place)) % per * coarse
+            start = pl.multiple_of(run // per * HELD_ROWS, SUBLANES)
+            piece = pltpu.roll(jnp.where(lane // coarse == place, chunk, 0.0), turn, 1)
+            held[pl.ds(start, HELD_ROWS), :] = held[pl.ds(start, HELD_ROWS), :] + piece
+
+
+def place_kernel(lev_dev, fields, coarse, groups, spare, numbers, *refs):
+    count = len(numbers)
+    sections, runs = refs[:count], refs[count : 2 * count]
+    slots, held_in, held = refs[2 * count], refs[2 * count + 1], refs[-1]
+    del held_in
+    side = lax.axis_index("side")
+
+    @pl.when(side == 0)
+    def _():
+        for section, run in zip(sections, runs):
+            place_blocks(coarse, spare, section, run, held)
+
+    @pl.when(side == 1)
+    def _():
+        for section, number in zip(sections, numbers):
+            place_panel(lev_dev, fields, answer_round(number, groups), section, slots, held)
+
+
+def finish_panel(lev_dev, fields, tiles, panel_tiles, held, state, staged, send):
+    shape = (SUBLANES, LANES)
+    sub = iota(shape, 0)
+    quarters = panel_tiles // 2
+    chunks = lev_dev * fields * quarters // SUBLANES
+    share = SUBLANES // quarters
+    rows = tiles * lev_dev
+    for field in range(fields):
+        start = field * rows
+        part = field % share
+        for tile in range(panel_tiles):
+            for level in range(lev_dev):
+                chunk = (level * fields + field) // share
+                row = (tile * chunks + chunk) * SUBLANES
+                rim = jnp.sum(
+                    jnp.where(sub // quarters == part, held[row : row + SUBLANES, :], 0.0),
+                    axis=0,
+                    keepdims=True,
                 )
-    weight_sum = landed[pl.ds(kinds - 1, tiles, stride=stride), :]
+                row = start + tile * lev_dev + level
+                staged[row : row + 1, :] = 0.5 * (state[row : row + 1, :] + rim)
+        rest = start + panel_tiles * lev_dev
+        staged[rest : start + rows, :] = state[rest : start + rows, :]
+        send(field)
+
+
+def finish_coarse(lev_dev, fields, tiles, held, state, staged, send):
+    weight_sum = held[pl.ds(lev_dev * fields, tiles, stride=HELD_ROWS), :]
     scale = 1.0 / (1.0 + weight_sum)
     for field in range(fields):
         for level in range(lev_dev):
             here = pl.ds(field * tiles * lev_dev + level, tiles, stride=lev_dev)
-            feedback = landed[pl.ds(level * fields + field, tiles, stride=stride), :]
-            out[here, :] = (state[here, :] + feedback) * scale
-
-
-def finish_kernel(lev_dev, fields, coarse, groups, *refs):
-    sections, lists, slots, state, out, landed = refs[:3], refs[3:6], *refs[6:]
-    tiles = state.shape[0] // (fields * lev_dev)
+            feedback = held[pl.ds(level * fields + field, tiles, stride=HELD_ROWS), :]
+            staged[here, :] = (state[here, :] + feedback) * scale
+        send(field)
+
+
+def finish_kernel(lev_dev, fields, coarse, groups, spare, numbers, *refs):
+    count = len(numbers)
+    slots, state = refs[2 * count], refs[2 * count + 2]
+    out, held, staged, sems = refs[2 * count + 3 :]
+    held[...] = refs[2 * count + 1][...]
+    place_kernel(lev_dev, fields, coarse, groups, spare, numbers, *refs[: 2 * count + 2], held)
+    tiles = spare
+    rows = tiles * lev_dev
+    copies = [
+        pltpu.make_async_copy(
+            staged.at[field * rows : (field + 1) * rows],
+            out.at[field * rows : (field + 1) * rows],
+            sems.at[field],
+        )
+        for field in range(fields)
+    ]
     side = lax.axis_index("side")
 
     @pl.when(side == 0)
     def _():
-        finish_coarse(lev_dev, fields, tiles, coarse, sections, lists, state, out, landed)
+        finish_coarse(
+            lev_dev, fields, tiles, held, state, staged, lambda field: copies[field].start()
+        )
 
     @pl.when(side == 1)
     def _():
-        finish_panel(lev_dev, fields, tiles, groups, sections, slots, state, out)
+        finish_panel(
+            lev_dev, fields, tiles, slots.shape[0], held, state, staged, lambda field: copies[field].start()
+        )
+
+    for copy in copies:
+        copy.wait()
 
 
 def specs(*spaces):
@@ -341,6 +406,10 @@
 
 def params():
     return pltpu.CompilerParams(vmem_limit_bytes=16 * 1024 * 1024)
+
+
+def in_hbm(value):
+    return pltpu.with_memory_space_constraint(value, pltpu.HBM)
 
 
 def struct(shape, dtype=jnp.float32):
@@ -368,13 +437,19 @@
     )
     message = struct((MESSAGE_ROWS, LANES), jnp.int32)
     page = struct((panel_tiles, LANES), jnp.int32)
-    first, second, own, slots = pl.pallas_call(
+    first, second, own, slots, state, terrain, weight = pl.pallas_call(
         functools.partial(list_kernel, groups),
-        out_shape=[message] * 3 + [page],
-        in_specs=specs(*[VMEM] * 4),
-        out_specs=specs(*[VMEM] * 4),
-        scratch_shapes=[VMEM((SUBLANES, LANES), jnp.int32)] * 2,
-        cost_estimate=pl.CostEstimate(flops=0, bytes_accessed=40_000_000, transcendentals=0),
+        out_shape=[message] * 3
+        + [page]
+        + [struct(state.shape), struct(terrain.shape, jnp.int32), struct(block_weight.shape)],
+        in_specs=specs(*[VMEM] * 3, *[pl.ANY] * 4),
+        out_specs=specs(*[VMEM] * 7),
+        scratch_shapes=[
+            VMEM(page.shape, jnp.int32),
+            VMEM((SUBLANES, LANES), jnp.int32),
+            VMEM((SUBLANES, LANES), jnp.int32),
+            pltpu.SemaphoreType.DMA((4,)),
+        ],
         compiler_params=params(),
         name="lists",
     )(
@@ -382,6 +457,9 @@
         block_owner.reshape(1, blocks),
         block_row.reshape(1, blocks),
         panel_cell.reshape(page.shape),
+        in_hbm(state),
+        in_hbm(terrain),
+        in_hbm(block_weight),
     )
 
     def towards(number_of, cross):
@@ -408,13 +486,12 @@
         ],
         compiler_params=params(),
         name="produce",
-    )(own, *lists, state, terrain, block_weight)
+    )(own, *lists, state, terrain, weight)
     arrived = [parts[0]] + [
         lax.ppermute(parts[distance], "lev", [(rank, rank ^ distance) for rank in range(partners)])
         for distance in range(partners - 1, 0, -1)
     ]
-    section_rows = lev_dev * fields * quarters + quarters
-    section_rows += -section_rows % SUBLANES
+    section_rows = HELD_ROWS * quarters
     sections = pl.pallas_call(
         functools.partial(sum_kernel, lev_dev, fields, partners),
         out_shape=[struct((section_rows, LANES))] * 3,
@@ -427,17 +504,32 @@
         lax.ppermute(sections[number], ("grid", "side"), towards(lambda side: number, 1))
         for number in range(ROUNDS - 1, -1, -1)
     ][::-1]
-    stride = lev_dev * fields + 1
-    stride += -stride % SUBLANES
+    held_shape = ((tiles + 1) * HELD_ROWS, LANES)
+    held = jnp.zeros(held_shape, jnp.float32)
+    sizes = (lev_dev, fields, coarse, groups, tiles)
+    for number in range(ROUNDS - 1, 0, -1):
+        held = pl.pallas_call(
+            functools.partial(place_kernel, *sizes, [number]),
+            out_shape=struct(held_shape),
+            in_specs=specs(VMEM, SMEM, VMEM, VMEM),
+            out_specs=pl.BlockSpec(memory_space=VMEM),
+            input_output_aliases={3: 0},
+            compiler_params=params(),
+            name="place",
+        )(sections[number], lists[number], slots, held)
     result = pl.pallas_call(
-        functools.partial(finish_kernel, lev_dev, fields, coarse, groups),
-        out_shape=struct(state.shape),
-        in_specs=specs(*[VMEM] * 3, *[SMEM] * 3, VMEM, VMEM),
-        out_specs=pl.BlockSpec(memory_space=VMEM),
-        scratch_shapes=[VMEM(((tiles + 1) * stride, LANES), jnp.float32)],
+        functools.partial(finish_kernel, *sizes, [0]),
+        out_shape=pltpu.HBM(state.shape, jnp.float32),
+        in_specs=specs(VMEM, SMEM, VMEM, VMEM, VMEM),
+        out_specs=pl.BlockSpec(memory_space=pltpu.HBM),
+        scratch_shapes=[
+            VMEM(held_shape, jnp.float32),
+            VMEM(state.shape, jnp.float32),
+            pltpu.SemaphoreType.DMA((fields,)),
+        ],
         compiler_params=params(),
         name="finish",
-    )(*sections, *lists, slots, state)
+    )(sections[0], lists[0], slots, held, state)
     return (
         result.reshape(fields, tiles, lev_dev, LANES)
         .transpose(2, 0, 1, 3)

time: 34.1 us -> 29.2 us (0.86)
  local copies, waits for them, and re-layouts: 4.37 us -> 0.74 us
  waiting for transfers between devices: 10.5 us -> 7.83 us
  Pallas kernels: 5.79 us -> 7.42 us
    unnamed x16 -> x8, local copies, waits for them, and re-layouts: 4.37 us -> 0.7 us
    ppermute x3, waiting for transfers between devices: 4.23 us -> 1.66 us  [on_device(): lax.ppermute(sections[number], ('grid', 'side'), towards(lambda side: num...]
    pallas_call x1 -> x3, Pallas kernels: 2.61 us -> 3.69 us  [the longest x2 1.88 us: on_device(): pl.pallas_call(functools.partial(place_kernel, *sizes, [number]), out_sha...]
    pallas_call x1, Pallas kernels: 1.05 us -> 1.56 us  [on_device(): pl.pallas_call(functools.partial(list_kernel, groups), out_shape=[message...]
  transfers between devices with their start and end apart: 9 -> 9, of which waited for: 6 -> 5; matrix products, arithmetic and copies ran while one was open for 0% -> 0% of each run, Pallas kernels for 0% -> 6%
where the time goes in v3:
time: 29.2 us; the launch traced here: 29 us
  starting transfers between devices  13 us (45%)
  waiting for transfers between devices  7.83 us (27%)
  Pallas kernels  7.42 us (25%)
  local copies, waits for them, and re-layouts  0.74 us (3%)
    ppermute x3, waiting for transfers between devices, on_device(): lax.ppermute(parts[distance], 'lev', [(rank, rank ^ distance) for rank in...  4.26 us
    ppermute x3, starting transfers between devices, on_device(): lax.ppermute(sections[number], ('grid', 'side'), towards(lambda side: num...  3.76 us
    ppermute x3, starting transfers between devices, on_device(): lax.ppermute(parts[distance], 'lev', [(rank, rank ^ distance) for rank in...  3.55 us
    ppermute x1, starting transfers between devices, on_device(): lax.ppermute(first, ('grid', 'side'), towards(lambda side: 2 * side, 0))  3.09 us
    ppermute x1, starting transfers between devices, on_device(): second = lax.ppermute(second, ('grid', 'side'), towards(lambda side: 1, 0))  2.59 us
    pallas_call x1, Pallas kernels, on_device(): pl.pallas_call(functools.partial(produce_kernel, lev_dev, fields, partner...  2.15 us
    ppermute x1, waiting for transfers between devices, on_device(): second = lax.ppermute(second, ('grid', 'side'), towards(lambda side: 1, 0))  1.91 us
    pallas_call x2, Pallas kernels, on_device(): pl.pallas_call(functools.partial(place_kernel, *sizes, [number]), out_sha...  1.88 us
  transfers between devices with their start and end apart: 9, of which 5 were waited for; matrix products, arithmetic and copies ran while one was open for 0% of the time, Pallas kernels for 6%

profile of v3, /device:TPU:0, one launch (start us, length us, event | category | flops | bytes accessed | tf_op | source)
XLA Modules:
  0.0 29.0 jit_solution(3094255488922519466)
XLA Ops:
  0.0 0.0 copy-start.1
  0.0 0.0 copy-start
  0.0 0.0 copy-start.2
  0.0 0.0 copy-start.3
  0.0 0.7 %copy-done.1 = s32[1024]{0:T(1024)S(1)} copy-done((s32[1024]{0:T(1024)S(1)}, s32[1024]{0:T(1024)}, u32[]{:S(2)}) %copy-start.1) | copy-done | bytes 4120
  0.7 0.0 copy-done
  0.7 0.0 copy-done.2
  0.7 0.0 copy-done.3
  0.7 1.6 %lists.1 = (s32[8,128]{1,0:T(8,128)S(1)}, s32[8,128]{1,0:T(8,128)S(1)}, s32[8,128]{1,0:T(8,128)S(1)}, s32[8,128]{1,0:T(8,128)S(1)}, f32[768,128]{1,0:T(8,128)S(1...) custom-call(s32[8,128]{1,0:T(8,128)S(1)} %bitcast.19, s32[1,64]{1,0:T(1,128)S(1)} %bitcast.21, ...), custom_call_target="tpu_custom_call" | custom-call | tf_op jit(solution)/shard_map/lists/pallas_call | solution.py:440
  2.3 3.1 %collective-permute-start = (s32[8,128]{1,0:T(8,128)S(1)}, s32[8,128]{1,0:T(8,128)S(1)}, u32[]{:S(2)}, u32[]{:S(2)}) collective-permute-start(s32[8,128]{1,0:T(8,128)S(1)} %get-tuple-element.21), channel_id=1, source_target_pairs={{0,8},{1,25},{8,0},{9,17},{16,24},{17,9},{24,16},{25,1},{2,10},{3,... | collective-permute-start | bytes 12296 | tf_op jit(solution)/shard_map/ppermute | solution.py:472
  5.4 2.6 %collective-permute-start.1 = (s32[8,128]{1,0:T(8,128)S(1)}, s32[8,128]{1,0:T(8,128)S(1)}, u32[]{:S(2)}, u32[]{:S(2)}) collective-permute-start(s32[8,128]{1,0:T(8,128)S(1)} %get-tuple-element.22), channel_id=1, source_target_pairs={{0,16},{1,17},{8,24},{9,25},{16,0},{17,1},{24,8},{25,9},{2,18},{3,... | collective-permute-start | bytes 12296 | tf_op jit(solution)/shard_map/ppermute | solution.py:473
  8.0 0.0 collective-permute-done.refs_0_.refs_1_
  8.0 0.0 collective-permute-start.2
  8.0 1.9 %collective-permute-done.1.refs_1_ = s32[8,128]{1,0:T(8,128)S(1)} collective-permute-done((s32[8,128]{1,0:T(8,128)S(1)}, s32[8,128]{1,0:T(8,128)S(1)}, u32[]{:S(2)}, u32[]{:S(2)}) %collective-permute-start.1) | collective-permute-done | bytes 4128 | tf_op jit(solution)/shard_map/ppermute | solution.py:473
  9.9 0.0 collective-permute-done.2.refs_2_.refs_1_
  9.9 2.1 %produce.1 = (f32[144,128]{1,0:T(8,128)S(1)}, f32[144,128]{1,0:T(8,128)S(1)}, f32[144,128]{1,0:T(8,128)S(1)}, f32[144,128]{1,0:T(8,128)S(1)}, f32[16,128]{1,0:T(8,128)S(1)}) custom-call(s32[8,128]{1,0:T(8,128)S(1)} %get-tuple-element.20.own, s32[8,128]{1,0:T(8,128)S(1)} %collective-permute-done.refs_0_.refs_1_, s32[8,128]{1,0:T(8,128)S(1)} %collective-permute-done.1.refs_1_, ...), custom_call_target="tpu_custom_call" | custom-call | tf_op jit(solution)/shard_map/produce/pallas_call | solution.py:478
  12.0 2.5 %collective-permute-start.3 = (f32[144,128]{1,0:T(8,128)S(1)}, f32[144,128]{1,0:T(8,128)S(1)}, u32[]{:S(2)}, u32[]{:S(2)}) collective-permute-start(f32[144,128]{1,0:T(8,128)S(1)} %get-tuple-element.27), channel_id=1, source_target_pairs={{0,6},{2,4},{4,2},{6,0},{1,7},{3,5},{5,3},{7,1},{8,14},{10,12},{12... | collective-permute-start | bytes 221192 | tf_op jit(solution)/shard_map/ppermute | solution.py:491
  14.5 0.5 %collective-permute-start.4 = (f32[144,128]{1,0:T(8,128)S(1)}, f32[144,128]{1,0:T(8,128)S(1)}, u32[]{:S(2)}, u32[]{:S(2)}) collective-permute-start(f32[144,128]{1,0:T(8,128)S(1)} %get-tuple-element.28), channel_id=1, source_target_pairs={{0,4},{2,6},{4,0},{6,2},{1,5},{3,7},{5,1},{7,3},{8,12},{10,14},{12... | collective-permute-start | bytes 221192 | tf_op jit(solution)/shard_map/ppermute | solution.py:491
  15.1 0.5 %collective-permute-start.5 = (f32[144,128]{1,0:T(8,128)S(1)}, f32[144,128]{1,0:T(8,128)S(1)}, u32[]{:S(2)}, u32[]{:S(2)}) collective-permute-start(f32[144,128]{1,0:T(8,128)S(1)} %get-tuple-element.29), channel_id=1, source_target_pairs={{0,2},{2,0},{4,6},{6,4},{1,3},{3,1},{5,7},{7,5},{8,10},{10,8},{12,... | collective-permute-start | bytes 221192 | tf_op jit(solution)/shard_map/ppermute | solution.py:491
  15.6 2.3 %collective-permute-done.3.refs_1_ = f32[144,128]{1,0:T(8,128)S(1)} collective-permute-done((f32[144,128]{1,0:T(8,128)S(1)}, f32[144,128]{1,0:T(8,128)S(1)}, u32[]{:S(2)}, u32[]{:S(2)}) %collective-permute-start.3) | collective-permute-done | bytes 73760 | tf_op jit(solution)/shard_map/ppermute | solution.py:491
  17.9 1.8 %collective-permute-done.4.refs_2_ = f32[144,128]{1,0:T(8,128)S(1)} collective-permute-done((f32[144,128]{1,0:T(8,128)S(1)}, f32[144,128]{1,0:T(8,128)S(1)}, u32[]{:S(2)}, u32[]{:S(2)}) %collective-permute-start.4) | collective-permute-done | bytes 73760 | tf_op jit(solution)/shard_map/ppermute | solution.py:491
  19.7 0.1 collective-permute-done.5.refs_3_
  19.9 2.1 %collective-permute-start.8 = (f32[64,128]{1,0:T(8,128)S(1)}, f32[64,128]{1,0:T(8,128)S(1)}, u32[]{:S(2)}, u32[]{:S(2)}) collective-permute-start(f32[64,128]{1,0:T(8,128)S(1)} %get-tuple-element.34), channel_id=1, source_target_pairs={{0,25},{1,24},{8,17},{9,16},{16,9},{17,8},{24,1},{25,0},{2,27},{3,... | collective-permute-start | bytes 98312 | tf_op jit(solution)/shard_map/ppermute | solution.py:504
  22.0 0.0 collective-permute-start.7
  22.0 1.6 %collective-permute-start.6 = (f32[64,128]{1,0:T(8,128)S(1)}, f32[64,128]{1,0:T(8,128)S(1)}, u32[]{:S(2)}, u32[]{:S(2)}) collective-permute-start(f32[64,128]{1,0:T(8,128)S(1)} %get-tuple-element.31), channel_id=1, source_target_pairs={{0,9},{1,8},{8,1},{9,0},{16,25},{17,24},{24,17},{25,16},{2,11},{3,... | collective-permute-start | bytes 98312 | tf_op jit(solution)/shard_map/ppermute | solution.py:504
  23.6 1.7 %collective-permute-done.8.refs_0_ = f32[64,128]{1,0:T(8,128)S(1)} collective-permute-done((f32[64,128]{1,0:T(8,128)S(1)}, f32[64,128]{1,0:T(8,128)S(1)}, u32[]{:S(2)}, u32[]{:S(2)}) %collective-permute-start.8) | collective-permute-done | bytes 32800 | tf_op jit(solution)/shard_map/ppermute | solution.py:504
  25.3 0.9 %place.2.refs_3_ = f32[1040,128]{1,0:T(8,128)S(1)} custom-call(f32[64,128]{1,0:T(8,128)S(1)} %collective-permute-done.8.refs_0_, s32[8,128]{1,0:T(8,128)S(1)} %collective-permute-done.2.refs_2_.refs_1_, s32[8,128]{1,0:T(8,128)S(1)} %get-tuple-element.32.refs_2_, f32[1040,128]{1,0:T(8,128)S(1)} %broadcast_in_dim.3.refs_3_), custom_call_target="tpu_custom_call", output_to_operand_aliasing={{}: (3, {})} | custom-call | tf_op jit(solution)/shard_map/place/pallas_call | solution.py:511
  26.3 0.0 collective-permute-done.7.refs_0_
  26.3 0.9 %place.3.refs_3_ = f32[1040,128]{1,0:T(8,128)S(1)} custom-call(f32[64,128]{1,0:T(8,128)S(1)} %collective-permute-done.7.refs_0_, s32[8,128]{1,0:T(8,128)S(1)} %collective-permute-done.1.refs_1_, s32[8,128]{1,0:T(8,128)S(1)} %get-tuple-element.32.refs_2_, f32[1040,128]{1,0:T(8,128)S(1)} %place.2.refs_3_), custom_call_target="tpu_custom_call", output_to_operand_aliasing={{}: (3, {})} | custom-call | tf_op jit(solution)/shard_map/place/pallas_call | solution.py:511
  27.2 0.0 collective-permute-done.6.refs_0_
  27.2 1.8 %finish.1 = f32[768,128]{1,0:T(8,128)} custom-call(f32[64,128]{1,0:T(8,128)S(1)} %collective-permute-done.6.refs_0_, s32[8,128]{1,0:T(8,128)S(1)} %collective-permute-done.refs_0_.refs_1_, s32[8,128]{1,0:T(8,128)S(1)} %get-tuple-element.32.refs_2_, f32[1040,128]{1,0:T(8,128)S(1)} %place.3.refs_3_, f32[768,128]{1,0:T(8,128)S(1)} %get-tuple-element.23.refs_3_.refs_4_), custom_call_target="tpu_custom_call" | custom-call | tf_op jit(solution)/shard_map/finish/pallas_call | solution.py:520
  (2 shorter events, 0.1 us)
Async XLA Ops:
  0.0 0.7 %copy-start.1 = (s32[1024]{0:T(1024)S(1)}, s32[1024]{0:T(1024)}, u32[]{:S(2)}) copy-start(s32[1024]{0:T(1024)} %param.10) | copy-start | bytes 12292
  0.0 0.7 %copy-start = (s32[1024,1]{0,1:T(1,128)S(1)}, s32[1024,1]{0,1:T(1,128)}, u32[]{:S(2)}) copy-start(s32[1024,1]{0,1:T(1,128)} %param.9) | copy-start | bytes 12292
  0.0 0.7 %copy-start.2 = (s32[64,1]{0,1:T(1,128)S(1)}, s32[64,1]{0,1:T(1,128)}, u32[]{:S(2)}) copy-start(s32[64,1]{0,1:T(1,128)} %param.12) | copy-start | bytes 772
  0.0 0.7 %copy-start.3 = (s32[64]{0:T(128)S(1)}, s32[64]{0:T(128)}, u32[]{:S(2)}) copy-start(s32[64]{0:T(128)} %param.13) | copy-start | bytes 772
  2.3 5.7 %collective-permute-start = (s32[8,128]{1,0:T(8,128)S(1)}, s32[8,128]{1,0:T(8,128)S(1)}, u32[]{:S(2)}, u32[]{:S(2)}) collective-permute-start(s32[8,128]{1,0:T(8,128)S(1)} %get-tuple-element.21), channel_id=1, source_target_pairs={{0,8},{1,25},{8,0},{9,17},{16,24},{17,9},{24,16},{25,1},{2,10},{3,... | collective-permute-start | bytes 12296 | tf_op jit(solution)/shard_map/ppermute | solution.py:472
  5.4 4.5 %collective-permute-start.1 = (s32[8,128]{1,0:T(8,128)S(1)}, s32[8,128]{1,0:T(8,128)S(1)}, u32[]{:S(2)}, u32[]{:S(2)}) collective-permute-start(s32[8,128]{1,0:T(8,128)S(1)} %get-tuple-element.22), channel_id=1, source_target_pairs={{0,16},{1,17},{8,24},{9,25},{16,0},{17,1},{24,8},{25,9},{2,18},{3,... | collective-permute-start | bytes 12296 | tf_op jit(solution)/shard_map/ppermute | solution.py:473
  8.0 1.9 %collective-permute-start.2 = (s32[8,128]{1,0:T(8,128)S(1)}, s32[8,128]{1,0:T(8,128)S(1)}, u32[]{:S(2)}, u32[]{:S(2)}) collective-permute-start(s32[8,128]{1,0:T(8,128)S(1)} %collective-permute-done.refs_0_.refs_1_), channel_id=1, source_target_pairs={{0,1},{1,0},{2,3},{3,2},{4,5},{5,4},{6,7},{7,6},{8,9},{9,8},{10,11... | collective-permute-start | bytes 12296 | tf_op jit(solution)/shard_map/ppermute | solution.py:474
  12.0 5.9 %collective-permute-start.3 = (f32[144,128]{1,0:T(8,128)S(1)}, f32[144,128]{1,0:T(8,128)S(1)}, u32[]{:S(2)}, u32[]{:S(2)}) collective-permute-start(f32[144,128]{1,0:T(8,128)S(1)} %get-tuple-element.27), channel_id=1, source_target_pairs={{0,6},{2,4},{4,2},{6,0},{1,7},{3,5},{5,3},{7,1},{8,14},{10,12},{12... | collective-permute-start | bytes 221192 | tf_op jit(solution)/shard_map/ppermute | solution.py:491
  14.5 5.2 %collective-permute-start.4 = (f32[144,128]{1,0:T(8,128)S(1)}, f32[144,128]{1,0:T(8,128)S(1)}, u32[]{:S(2)}, u32[]{:S(2)}) collective-permute-start(f32[144,128]{1,0:T(8,128)S(1)} %get-tuple-element.28), channel_id=1, source_target_pairs={{0,4},{2,6},{4,0},{6,2},{1,5},{3,7},{5,1},{7,3},{8,12},{10,14},{12... | collective-permute-start | bytes 221192 | tf_op jit(solution)/shard_map/ppermute | solution.py:491
  15.1 4.8 %collective-permute-start.5 = (f32[144,128]{1,0:T(8,128)S(1)}, f32[144,128]{1,0:T(8,128)S(1)}, u32[]{:S(2)}, u32[]{:S(2)}) collective-permute-start(f32[144,128]{1,0:T(8,128)S(1)} %get-tuple-element.29), channel_id=1, source_target_pairs={{0,2},{2,0},{4,6},{6,4},{1,3},{3,1},{5,7},{7,5},{8,10},{10,8},{12,... | collective-permute-start | bytes 221192 | tf_op jit(solution)/shard_map/ppermute | solution.py:491
  19.9 5.4 %collective-permute-start.8 = (f32[64,128]{1,0:T(8,128)S(1)}, f32[64,128]{1,0:T(8,128)S(1)}, u32[]{:S(2)}, u32[]{:S(2)}) collective-permute-start(f32[64,128]{1,0:T(8,128)S(1)} %get-tuple-element.34), channel_id=1, source_target_pairs={{0,25},{1,24},{8,17},{9,16},{16,9},{17,8},{24,1},{25,0},{2,27},{3,... | collective-permute-start | bytes 98312 | tf_op jit(solution)/shard_map/ppermute | solution.py:504
  22.0 4.3 %collective-permute-start.7 = (f32[64,128]{1,0:T(8,128)S(1)}, f32[64,128]{1,0:T(8,128)S(1)}, u32[]{:S(2)}, u32[]{:S(2)}) collective-permute-start(f32[64,128]{1,0:T(8,128)S(1)} %get-tuple-element.33), channel_id=1, source_target_pairs={{0,17},{1,16},{8,25},{9,24},{16,1},{17,0},{24,9},{25,8},{2,19},{3,... | collective-permute-start | bytes 98312 | tf_op jit(solution)/shard_map/ppermute | solution.py:504
  22.0 5.2 %collective-permute-start.6 = (f32[64,128]{1,0:T(8,128)S(1)}, f32[64,128]{1,0:T(8,128)S(1)}, u32[]{:S(2)}, u32[]{:S(2)}) collective-permute-start(f32[64,128]{1,0:T(8,128)S(1)} %get-tuple-element.31), channel_id=1, source_target_pairs={{0,9},{1,8},{8,1},{9,0},{16,25},{17,24},{24,17},{25,16},{2,11},{3,... | collective-permute-start | bytes 98312 | tf_op jit(solution)/shard_map/ppermute | solution.py:504

commit v4 on v3

--- a/solution.py
+++ b/solution.py
@@ -235,10 +235,12 @@
     lax.fori_loop(0, ROUNDS * quarters // TOGETHER, some_tiles, 0)
 
 
-def produce_kernel(lev_dev, fields, partners, groups, own, *refs):
+def produce_kernel(lev_dev, fields, partners, groups, own_ref, *refs):
     lists, state, terrain, weight = refs[:3], refs[3], refs[4], refs[5]
     parts = refs[6 : 6 + partners]
-    mass, scratch, packed = refs[6 + partners :]
+    mass, scratch, packed, own, sem = refs[6 + partners :]
+    copy = pltpu.make_async_copy(own_ref, own, sem)
+    copy.start()
     tiles = terrain.shape[0] // SUBLANES
     side, group = lax.axis_index("side"), lax.axis_index("lev")
 
@@ -246,9 +248,11 @@
     def _():
         mass[...] = jnp.zeros_like(mass)
         panel_rows(lev_dev, fields, tiles, groups, lists, group, state, terrain, packed, scratch)
+        copy.wait()
 
     @pl.when(side == 1)
     def _():
+        copy.wait()
         block_rows(lev_dev, fields, tiles, own, group, state, terrain, weight, scratch, mass)
 
     rows = scratch.shape[0] // SUBLANES
@@ -279,7 +283,7 @@
         section[tail:, :] = jnp.zeros((section.shape[0] - tail, LANES), jnp.float32)
 
 
-def place_panel(lev_dev, fields, number, section, slots, held):
+def place_panel(lev_dev, fields, number, fresh, section, slots, found):
     shape = (SUBLANES, LANES)
     sub = iota(shape, 0)
     panel_tiles = slots.shape[0]
@@ -288,48 +292,56 @@
     for tile in range(panel_tiles):
         place = jnp.broadcast_to(slots[tile : tile + 1, :], shape)
         here = place >> LANE_BITS == number * quarters + sub % quarters
+        low = place & (LANES - 1)
         for chunk in range(chunks):
-            got = gather_lanes(
-                section[chunk * SUBLANES : (chunk + 1) * SUBLANES, :], place & (LANES - 1)
-            )
+            got = gather_lanes(section[chunk * SUBLANES : (chunk + 1) * SUBLANES, :], low)
             row = (tile * chunks + chunk) * SUBLANES
-            held[row : row + SUBLANES, :] = jnp.where(here, got, held[row : row + SUBLANES, :])
-
-
-def place_blocks(coarse, spare, section, runs, held):
-    per = LANES // coarse
-    quarters = section.shape[0] // HELD_ROWS
-    lane = iota((HELD_ROWS, LANES), 1)
+            before = 0.0 if fresh else found[row : row + SUBLANES, :]
+            found[row : row + SUBLANES, :] = jnp.where(here, got, before)
+
+
+def place_blocks(coarse, number, section, page, spread_high, spread_low):
+    shape = (SUBLANES, LANES)
+    lane, sub = iota(shape, 1), iota(shape, 0)
+    quarters = page.shape[0] // 2
+    kinds = spread_high.shape[1] // LANES
+    runs = jnp.broadcast_to(page[quarters : quarters + 1, :], shape)
+    indices, heres = [], []
     for quarter in range(quarters):
-        chunk = section[pl.ds(quarter, HELD_ROWS, stride=quarters), :]
-        for place in range(per):
-            run = runs[quarters, quarter * per + place]
-            run = jnp.where(run < 0, spare * per, run)
-            turn = (run + (per - place)) % per * coarse
-            start = pl.multiple_of(run // per * HELD_ROWS, SUBLANES)
-            piece = pltpu.roll(jnp.where(lane // coarse == place, chunk, 0.0), turn, 1)
-            held[pl.ds(start, HELD_ROWS), :] = held[pl.ds(start, HELD_ROWS), :] + piece
-
-
-def place_kernel(lev_dev, fields, coarse, groups, spare, numbers, *refs):
-    count = len(numbers)
-    sections, runs = refs[:count], refs[count : 2 * count]
-    slots, held_in, held = refs[2 * count], refs[2 * count + 1], refs[-1]
-    del held_in
+        run = jnp.where(lane == quarter * SUBLANES + sub, runs, 0)
+        run = jnp.broadcast_to(jnp.sum(run, axis=1, keepdims=True), shape)
+        shift = lane - (run & (LANES // coarse - 1)) * coarse
+        indices.append((shift + sub * coarse) & (LANES - 1))
+        heres.append((shift >= 0) & (shift < coarse) & (run >= 0))
+    for pair in range(0, quarters, 2):
+        for kind in range(kinds):
+            both = []
+            for quarter in (pair, pair + 1):
+                row = kind * quarters + quarter
+                line = jnp.broadcast_to(section[row : row + 1, :], shape)
+                both.append(jnp.where(heres[quarter], gather_lanes(line, indices[quarter]), 0.0))
+            both = jnp.concatenate(both, axis=0)
+            high = both.astype(jnp.bfloat16)
+            start = (number * quarters + pair) * SUBLANES
+            here = (slice(start, start + 2 * SUBLANES), slice(kind * LANES, (kind + 1) * LANES))
+            spread_high[here] = high
+            spread_low[here] = (both - high.astype(jnp.float32)).astype(jnp.bfloat16)
+
+
+def place_kernel(lev_dev, fields, coarse, groups, number, fresh, section, page, slots, *refs):
+    spread_high, spread_low, found = refs[-3:]
     side = lax.axis_index("side")
 
     @pl.when(side == 0)
     def _():
-        for section, run in zip(sections, runs):
-            place_blocks(coarse, spare, section, run, held)
+        place_blocks(coarse, number, section, page, spread_high, spread_low)
 
     @pl.when(side == 1)
     def _():
-        for section, number in zip(sections, numbers):
-            place_panel(lev_dev, fields, answer_round(number, groups), section, slots, held)
-
-
-def finish_panel(lev_dev, fields, tiles, panel_tiles, held, state, staged, send):
+        place_panel(lev_dev, fields, answer_round(number, groups), fresh, section, slots, found)
+
+
+def finish_panel(lev_dev, fields, tiles, panel_tiles, found, state, staged, send):
     shape = (SUBLANES, LANES)
     sub = iota(shape, 0)
     quarters = panel_tiles // 2
@@ -344,7 +356,7 @@
                 chunk = (level * fields + field) // share
                 row = (tile * chunks + chunk) * SUBLANES
                 rim = jnp.sum(
-                    jnp.where(sub // quarters == part, held[row : row + SUBLANES, :], 0.0),
+                    jnp.where(sub // quarters == part, found[row : row + SUBLANES, :], 0.0),
                     axis=0,
                     keepdims=True,
                 )
@@ -355,24 +367,38 @@
         send(field)
 
 
-def finish_coarse(lev_dev, fields, tiles, held, state, staged, send):
-    weight_sum = held[pl.ds(lev_dev * fields, tiles, stride=HELD_ROWS), :]
-    scale = 1.0 / (1.0 + weight_sum)
+def finish_coarse(lev_dev, fields, tiles, coarse, pages, spread_high, spread_low, state, staged, send):
+    quarters = pages[0].shape[0] // 2
+    width = quarters * SUBLANES
+    shift = (LANES // coarse).bit_length() - 1
+    tile = iota((tiles, LANES), 0)
+    lane = iota((1, LANES), 1)
+    runs = jnp.full((1, LANES), -1, jnp.int32)
+    for number, page in enumerate(pages):
+        turned = page[quarters : quarters + 1, :]
+        if number:
+            turned = pltpu.roll(jnp.broadcast_to(turned, (SUBLANES, LANES)), number * width, 1)[0:1]
+        runs = jnp.where(lane // width == number, turned, runs)
+    lands = (tile == jnp.broadcast_to(runs >> shift, tile.shape)).astype(jnp.bfloat16)
+    lands = lands[:, : ROUNDS * width]
+
+    def landed(kind):
+        here = (slice(None), slice(kind * LANES, (kind + 1) * LANES))
+        high = jnp.dot(lands, spread_high[here], preferred_element_type=jnp.float32)
+        return high + jnp.dot(lands, spread_low[here], preferred_element_type=jnp.float32)
+
+    scale = 1.0 / (1.0 + landed(lev_dev * fields))
     for field in range(fields):
         for level in range(lev_dev):
             here = pl.ds(field * tiles * lev_dev + level, tiles, stride=lev_dev)
-            feedback = held[pl.ds(level * fields + field, tiles, stride=HELD_ROWS), :]
-            staged[here, :] = (state[here, :] + feedback) * scale
+            staged[here, :] = (state[here, :] + landed(level * fields + field)) * scale
         send(field)
 
 
-def finish_kernel(lev_dev, fields, coarse, groups, spare, numbers, *refs):
-    count = len(numbers)
-    slots, state = refs[2 * count], refs[2 * count + 2]
-    out, held, staged, sems = refs[2 * count + 3 :]
-    held[...] = refs[2 * count + 1][...]
-    place_kernel(lev_dev, fields, coarse, groups, spare, numbers, *refs[: 2 * count + 2], held)
-    tiles = spare
+def finish_kernel(lev_dev, fields, coarse, groups, number, section, *refs):
+    pages, slots, kept, state = refs[:3], refs[3], refs[4:7], refs[7]
+    out, spread_high, spread_low, found, staged, sems = refs[8:]
+    tiles = state.shape[0] // (fields * lev_dev)
     rows = tiles * lev_dev
     copies = [
         pltpu.make_async_copy(
@@ -384,17 +410,23 @@
     ]
     side = lax.axis_index("side")
 
+    def send(field):
+        copies[field].start()
+
     @pl.when(side == 0)
     def _():
+        spread_high[...] = kept[0][...]
+        spread_low[...] = kept[1][...]
+        place_blocks(coarse, number, section, pages[number], spread_high, spread_low)
         finish_coarse(
-            lev_dev, fields, tiles, held, state, staged, lambda field: copies[field].start()
+            lev_dev, fields, tiles, coarse, pages, spread_high, spread_low, state, staged, send
         )
 
     @pl.when(side == 1)
     def _():
-        finish_panel(
-            lev_dev, fields, tiles, slots.shape[0], held, state, staged, lambda field: copies[field].start()
-        )
+        found[...] = kept[2][...]
+        place_panel(lev_dev, fields, answer_round(number, groups), False, section, slots, found)
+        finish_panel(lev_dev, fields, tiles, slots.shape[0], found, state, staged, send)
 
     for copy in copies:
         copy.wait()
@@ -478,11 +510,13 @@
     *parts, mass = pl.pallas_call(
         functools.partial(produce_kernel, lev_dev, fields, partners, groups),
         out_shape=[part] * partners + [struct((2 * SUBLANES, LANES))],
-        in_specs=specs(SMEM, *[VMEM] * 6),
+        in_specs=specs(*[VMEM] * 7),
         out_specs=specs(*[VMEM] * (partners + 1)),
         scratch_shapes=[
             VMEM((scratch_rows * SUBLANES, LANES), jnp.float32),
             VMEM((tiles, LANES), jnp.int32),
+            SMEM((MESSAGE_ROWS, LANES), jnp.int32),
+            pltpu.SemaphoreType.DMA,
         ],
         compiler_params=params(),
         name="produce",
@@ -504,32 +538,31 @@
         lax.ppermute(sections[number], ("grid", "side"), towards(lambda side: number, 1))
         for number in range(ROUNDS - 1, -1, -1)
     ][::-1]
-    held_shape = ((tiles + 1) * HELD_ROWS, LANES)
-    held = jnp.zeros(held_shape, jnp.float32)
-    sizes = (lev_dev, fields, coarse, groups, tiles)
+    kinds = lev_dev * fields + 1
+    spread = struct((ROUNDS * quarters * SUBLANES, kinds * LANES), jnp.bfloat16)
+    kept = [spread, spread, struct((panel_tiles * lev_dev * fields * quarters, LANES))]
+    sizes = (lev_dev, fields, coarse, groups)
+    held = []
     for number in range(ROUNDS - 1, 0, -1):
         held = pl.pallas_call(
-            functools.partial(place_kernel, *sizes, [number]),
-            out_shape=struct(held_shape),
-            in_specs=specs(VMEM, SMEM, VMEM, VMEM),
-            out_specs=pl.BlockSpec(memory_space=VMEM),
-            input_output_aliases={3: 0},
+            functools.partial(place_kernel, *sizes, number, not held),
+            out_shape=kept,
+            in_specs=specs(*[VMEM] * (3 + len(held))),
+            out_specs=specs(*[VMEM] * 3),
+            input_output_aliases={3 + index: index for index in range(len(held))},
             compiler_params=params(),
             name="place",
-        )(sections[number], lists[number], slots, held)
+        )(sections[number], lists[number], slots, *held)
     result = pl.pallas_call(
-        functools.partial(finish_kernel, *sizes, [0]),
+        functools.partial(finish_kernel, *sizes, 0),
         out_shape=pltpu.HBM(state.shape, jnp.float32),
-        in_specs=specs(VMEM, SMEM, VMEM, VMEM, VMEM),
+        in_specs=specs(*[VMEM] * 9),
         out_specs=pl.BlockSpec(memory_space=pltpu.HBM),
-        scratch_shapes=[
-            VMEM(held_shape, jnp.float32),
-            VMEM(state.shape, jnp.float32),
-            pltpu.SemaphoreType.DMA((fields,)),
-        ],
+        scratch_shapes=[VMEM(one.shape, one.dtype) for one in kept]
+        + [VMEM(state.shape, jnp.float32), pltpu.SemaphoreType.DMA((fields,))],
         compiler_params=params(),
         name="finish",
-    )(sections[0], lists[0], slots, held, state)
+    )(sections[0], *lists, slots, *held, state)
     return (
         result.reshape(fields, tiles, lev_dev, LANES)
         .transpose(2, 0, 1, 3)

time: 29.2 us -> 28.1 us (0.962)
  Pallas kernels: 7.42 us -> 4.88 us
  waiting for transfers between devices: 7.83 us -> 9.2 us
    pallas_call x3, Pallas kernels: 3.69 us -> 1.73 us  [the longest x1 1.21 us: on_device(): pl.pallas_call(functools.partial(finish_kernel, *sizes, 0), out_shape=plt...]
    ppermute x3, waiting for transfers between devices: 1.66 us -> 2.91 us  [on_device(): lax.ppermute(sections[number], ('grid', 'side'), towards(lambda side: num...]
    pallas_call x1, Pallas kernels: 2.15 us -> 1.56 us  [on_device(): pl.pallas_call(functools.partial(produce_kernel, lev_dev, fields, partner...]
  transfers between devices with their start and end apart: 9 -> 9, of which waited for: 5 -> 6; matrix products, arithmetic and copies ran while one was open for 0% -> 0% of each run, Pallas kernels for 6% -> 2%
where the time goes in v4:
time: 28.1 us; the launch traced here: 28 us
  starting transfers between devices  13.1 us (47%)
  waiting for transfers between devices  9.2 us (33%)
  Pallas kernels  4.88 us (17%)
  local copies, waits for them, and re-layouts  0.7 us (2%)
    ppermute x3, waiting for transfers between devices, on_device(): lax.ppermute(parts[distance], 'lev', [(rank, rank ^ distance) for rank in...  4.37 us
    ppermute x3, starting transfers between devices, on_device(): lax.ppermute(sections[number], ('grid', 'side'), towards(lambda side: num...  3.89 us
    ppermute x3, starting transfers between devices, on_device(): lax.ppermute(parts[distance], 'lev', [(rank, rank ^ distance) for rank in...  3.55 us
    ppermute x1, starting transfers between devices, on_device(): lax.ppermute(first, ('grid', 'side'), towards(lambda side: 2 * side, 0))  3.09 us
    ppermute x3, waiting for transfers between devices, on_device(): lax.ppermute(sections[number], ('grid', 'side'), towards(lambda side: num...  2.91 us
    ppermute x1, starting transfers between devices, on_device(): second = lax.ppermute(second, ('grid', 'side'), towards(lambda side: 1, 0))  2.59 us
    ppermute x1, waiting for transfers between devices, on_device(): second = lax.ppermute(second, ('grid', 'side'), towards(lambda side: 1, 0))  1.91 us
    pallas_call x1, Pallas kernels, on_device(): pl.pallas_call(functools.partial(list_kernel, groups), out_shape=[message...  1.56 us
  transfers between devices with their start and end apart: 9, of which 6 were waited for; matrix products, arithmetic and copies ran while one was open for 0% of the time, Pallas kernels for 2%

profile of v4, /device:TPU:0, one launch (start us, length us, event | category | flops | bytes accessed | tf_op | source)
XLA Modules:
  0.0 28.0 jit_solution(12825493843321934715)
XLA Ops:
  0.0 0.0 copy-start.1
  0.0 0.0 copy-start
  0.0 0.0 copy-start.2
  0.0 0.0 copy-start.3
  0.0 0.7 %copy-done.1 = s32[1024]{0:T(1024)S(1)} copy-done((s32[1024]{0:T(1024)S(1)}, s32[1024]{0:T(1024)}, u32[]{:S(2)}) %copy-start.1) | copy-done | bytes 4120
  0.7 0.0 copy-done
  0.7 0.0 copy-done.2
  0.7 0.0 copy-done.3
  0.7 1.6 %lists.1 = (s32[8,128]{1,0:T(8,128)S(1)}, s32[8,128]{1,0:T(8,128)S(1)}, s32[8,128]{1,0:T(8,128)S(1)}, s32[8,128]{1,0:T(8,128)S(1)}, f32[768,128]{1,0:T(8,128)S(1...) custom-call(s32[8,128]{1,0:T(8,128)S(1)} %bitcast.19, s32[1,64]{1,0:T(1,128)S(1)} %bitcast.21, ...), custom_call_target="tpu_custom_call" | custom-call | tf_op jit(solution)/shard_map/lists/pallas_call | solution.py:472
  2.3 3.1 %collective-permute-start = (s32[8,128]{1,0:T(8,128)S(1)}, s32[8,128]{1,0:T(8,128)S(1)}, u32[]{:S(2)}, u32[]{:S(2)}) collective-permute-start(s32[8,128]{1,0:T(8,128)S(1)} %get-tuple-element.27), channel_id=1, source_target_pairs={{0,8},{1,25},{8,0},{9,17},{16,24},{17,9},{24,16},{25,1},{2,10},{3,... | collective-permute-start | bytes 12296 | tf_op jit(solution)/shard_map/ppermute | solution.py:504
  5.4 2.6 %collective-permute-start.1 = (s32[8,128]{1,0:T(8,128)S(1)}, s32[8,128]{1,0:T(8,128)S(1)}, u32[]{:S(2)}, u32[]{:S(2)}) collective-permute-start(s32[8,128]{1,0:T(8,128)S(1)} %get-tuple-element.28), channel_id=1, source_target_pairs={{0,16},{1,17},{8,24},{9,25},{16,0},{17,1},{24,8},{25,9},{2,18},{3,... | collective-permute-start | bytes 12296 | tf_op jit(solution)/shard_map/ppermute | solution.py:505
  8.0 0.0 collective-permute-done.refs_0_
  8.0 0.0 collective-permute-start.2
  8.0 1.9 %collective-permute-done.1.refs_1_.page = s32[8,128]{1,0:T(8,128)S(1)} collective-permute-done((s32[8,128]{1,0:T(8,128)S(1)}, s32[8,128]{1,0:T(8,128)S(1)}, u32[]{:S(2)}, u32[]{:S(2)}) %collective-permute-start.1) | collective-permute-done | bytes 4128 | tf_op jit(solution)/shard_map/ppermute | solution.py:505
  9.9 0.0 collective-permute-done.2.refs_2_.page
  9.9 1.6 %produce.1 = (f32[144,128]{1,0:T(8,128)S(1)}, f32[144,128]{1,0:T(8,128)S(1)}, f32[144,128]{1,0:T(8,128)S(1)}, f32[144,128]{1,0:T(8,128)S(1)}, f32[16,128]{1,0:T(8,128)S(1)}) custom-call(s32[8,128]{1,0:T(8,128)S(1)} %get-tuple-element.26.own_ref, s32[8,128]{1,0:T(8,128)S(1)} %collective-permute-done.refs_0_, ...), custom_call_target="tpu_custom_call" | custom-call | tf_op jit(solution)/shard_map/produce/pallas_call | solution.py:510
  11.4 2.5 %collective-permute-start.3 = (f32[144,128]{1,0:T(8,128)S(1)}, f32[144,128]{1,0:T(8,128)S(1)}, u32[]{:S(2)}, u32[]{:S(2)}) collective-permute-start(f32[144,128]{1,0:T(8,128)S(1)} %get-tuple-element.33), channel_id=1, source_target_pairs={{0,6},{2,4},{4,2},{6,0},{1,7},{3,5},{5,3},{7,1},{8,14},{10,12},{12... | collective-permute-start | bytes 221192 | tf_op jit(solution)/shard_map/ppermute | solution.py:525
  14.0 0.5 %collective-permute-start.4 = (f32[144,128]{1,0:T(8,128)S(1)}, f32[144,128]{1,0:T(8,128)S(1)}, u32[]{:S(2)}, u32[]{:S(2)}) collective-permute-start(f32[144,128]{1,0:T(8,128)S(1)} %get-tuple-element.34), channel_id=1, source_target_pairs={{0,4},{2,6},{4,0},{6,2},{1,5},{3,7},{5,1},{7,3},{8,12},{10,14},{12... | collective-permute-start | bytes 221192 | tf_op jit(solution)/shard_map/ppermute | solution.py:525
  14.5 0.5 %collective-permute-start.5 = (f32[144,128]{1,0:T(8,128)S(1)}, f32[144,128]{1,0:T(8,128)S(1)}, u32[]{:S(2)}, u32[]{:S(2)}) collective-permute-start(f32[144,128]{1,0:T(8,128)S(1)} %get-tuple-element.35), channel_id=1, source_target_pairs={{0,2},{2,0},{4,6},{6,4},{1,3},{3,1},{5,7},{7,5},{8,10},{10,8},{12,... | collective-permute-start | bytes 221192 | tf_op jit(solution)/shard_map/ppermute | solution.py:525
  15.0 1.8 %collective-permute-done.3.refs_1_ = f32[144,128]{1,0:T(8,128)S(1)} collective-permute-done((f32[144,128]{1,0:T(8,128)S(1)}, f32[144,128]{1,0:T(8,128)S(1)}, u32[]{:S(2)}, u32[]{:S(2)}) %collective-permute-start.3) | collective-permute-done | bytes 73760 | tf_op jit(solution)/shard_map/ppermute | solution.py:525
  16.8 2.0 %collective-permute-done.4.refs_2_ = f32[144,128]{1,0:T(8,128)S(1)} collective-permute-done((f32[144,128]{1,0:T(8,128)S(1)}, f32[144,128]{1,0:T(8,128)S(1)}, u32[]{:S(2)}, u32[]{:S(2)}) %collective-permute-start.4) | collective-permute-done | bytes 73760 | tf_op jit(solution)/shard_map/ppermute | solution.py:525
  18.7 0.6 %collective-permute-done.5.refs_3_ = f32[144,128]{1,0:T(8,128)S(1)} collective-permute-done((f32[144,128]{1,0:T(8,128)S(1)}, f32[144,128]{1,0:T(8,128)S(1)}, u32[]{:S(2)}, u32[]{:S(2)}) %collective-permute-start.5) | collective-permute-done | bytes 73760 | tf_op jit(solution)/shard_map/ppermute | solution.py:525
  19.4 2.4 %collective-permute-start.8 = (f32[64,128]{1,0:T(8,128)S(1)}, f32[64,128]{1,0:T(8,128)S(1)}, u32[]{:S(2)}, u32[]{:S(2)}) collective-permute-start(f32[64,128]{1,0:T(8,128)S(1)} %get-tuple-element.40), channel_id=1, source_target_pairs={{0,25},{1,24},{8,17},{9,16},{16,9},{17,8},{24,1},{25,0},{2,27},{3,... | collective-permute-start | bytes 98312 | tf_op jit(solution)/shard_map/ppermute | solution.py:538
  21.8 0.0 collective-permute-start.7
  21.8 1.5 %collective-permute-start.6 = (f32[64,128]{1,0:T(8,128)S(1)}, f32[64,128]{1,0:T(8,128)S(1)}, u32[]{:S(2)}, u32[]{:S(2)}) collective-permute-start(f32[64,128]{1,0:T(8,128)S(1)} %get-tuple-element.37), channel_id=1, source_target_pairs={{0,9},{1,8},{8,1},{9,0},{16,25},{17,24},{24,17},{25,16},{2,11},{3,... | collective-permute-start | bytes 98312 | tf_op jit(solution)/shard_map/ppermute | solution.py:538
  23.3 1.4 %collective-permute-done.8.section = f32[64,128]{1,0:T(8,128)S(1)} collective-permute-done((f32[64,128]{1,0:T(8,128)S(1)}, f32[64,128]{1,0:T(8,128)S(1)}, u32[]{:S(2)}, u32[]{:S(2)}) %collective-permute-start.8) | collective-permute-done | bytes 32800 | tf_op jit(solution)/shard_map/ppermute | solution.py:538
  24.7 0.3 place.2
  24.9 1.5 %collective-permute-done.7.section = f32[64,128]{1,0:T(8,128)S(1)} collective-permute-done((f32[64,128]{1,0:T(8,128)S(1)}, f32[64,128]{1,0:T(8,128)S(1)}, u32[]{:S(2)}, u32[]{:S(2)}) %collective-permute-start.7) | collective-permute-done | bytes 32800 | tf_op jit(solution)/shard_map/ppermute | solution.py:538
  26.5 0.3 place.3
  26.7 0.0 collective-permute-done.6.section
  26.7 1.2 %finish.1 = f32[768,128]{1,0:T(8,128)} custom-call(f32[64,128]{1,0:T(8,128)S(1)} %collective-permute-done.6.section, s32[8,128]{1,0:T(8,128)S(1)} %collective-permute-done.refs_0_, s32[8,128]{1,0:T(8,128)S(1)} %collective-permute-done.1.refs_1_.page, s32[8,128]{1,0:T(8,128)S(1)} %collective-permute-done.2.refs_2_.page, ...), custom_call_target="tpu_custom_call" | custom-call | tf_op jit(solution)/shard_map/finish/pallas_call | solution.py:556
  (1 shorter events, 0.0 us)
Async XLA Ops:
  0.0 0.7 %copy-start.1 = (s32[1024]{0:T(1024)S(1)}, s32[1024]{0:T(1024)}, u32[]{:S(2)}) copy-start(s32[1024]{0:T(1024)} %param.10) | copy-start | bytes 12292
  0.0 0.7 %copy-start = (s32[1024,1]{0,1:T(1,128)S(1)}, s32[1024,1]{0,1:T(1,128)}, u32[]{:S(2)}) copy-start(s32[1024,1]{0,1:T(1,128)} %param.9) | copy-start | bytes 12292
  0.0 0.7 %copy-start.2 = (s32[64,1]{0,1:T(1,128)S(1)}, s32[64,1]{0,1:T(1,128)}, u32[]{:S(2)}) copy-start(s32[64,1]{0,1:T(1,128)} %param.12) | copy-start | bytes 772
  0.0 0.7 %copy-start.3 = (s32[64]{0:T(128)S(1)}, s32[64]{0:T(128)}, u32[]{:S(2)}) copy-start(s32[64]{0:T(128)} %param.13) | copy-start | bytes 772
  2.3 5.7 %collective-permute-start = (s32[8,128]{1,0:T(8,128)S(1)}, s32[8,128]{1,0:T(8,128)S(1)}, u32[]{:S(2)}, u32[]{:S(2)}) collective-permute-start(s32[8,128]{1,0:T(8,128)S(1)} %get-tuple-element.27), channel_id=1, source_target_pairs={{0,8},{1,25},{8,0},{9,17},{16,24},{17,9},{24,16},{25,1},{2,10},{3,... | collective-permute-start | bytes 12296 | tf_op jit(solution)/shard_map/ppermute | solution.py:504
  5.4 4.5 %collective-permute-start.1 = (s32[8,128]{1,0:T(8,128)S(1)}, s32[8,128]{1,0:T(8,128)S(1)}, u32[]{:S(2)}, u32[]{:S(2)}) collective-permute-start(s32[8,128]{1,0:T(8,128)S(1)} %get-tuple-element.28), channel_id=1, source_target_pairs={{0,16},{1,17},{8,24},{9,25},{16,0},{17,1},{24,8},{25,9},{2,18},{3,... | collective-permute-start | bytes 12296 | tf_op jit(solution)/shard_map/ppermute | solution.py:505
  8.0 1.9 %collective-permute-start.2 = (s32[8,128]{1,0:T(8,128)S(1)}, s32[8,128]{1,0:T(8,128)S(1)}, u32[]{:S(2)}, u32[]{:S(2)}) collective-permute-start(s32[8,128]{1,0:T(8,128)S(1)} %collective-permute-done.refs_0_), channel_id=1, source_target_pairs={{0,1},{1,0},{2,3},{3,2},{4,5},{5,4},{6,7},{7,6},{8,9},{9,8},{10,11... | collective-permute-start | bytes 12296 | tf_op jit(solution)/shard_map/ppermute | solution.py:506
  11.4 5.3 %collective-permute-start.3 = (f32[144,128]{1,0:T(8,128)S(1)}, f32[144,128]{1,0:T(8,128)S(1)}, u32[]{:S(2)}, u32[]{:S(2)}) collective-permute-start(f32[144,128]{1,0:T(8,128)S(1)} %get-tuple-element.33), channel_id=1, source_target_pairs={{0,6},{2,4},{4,2},{6,0},{1,7},{3,5},{5,3},{7,1},{8,14},{10,12},{12... | collective-permute-start | bytes 221192 | tf_op jit(solution)/shard_map/ppermute | solution.py:525
  14.0 4.8 %collective-permute-start.4 = (f32[144,128]{1,0:T(8,128)S(1)}, f32[144,128]{1,0:T(8,128)S(1)}, u32[]{:S(2)}, u32[]{:S(2)}) collective-permute-start(f32[144,128]{1,0:T(8,128)S(1)} %get-tuple-element.34), channel_id=1, source_target_pairs={{0,4},{2,6},{4,0},{6,2},{1,5},{3,7},{5,1},{7,3},{8,12},{10,14},{12... | collective-permute-start | bytes 221192 | tf_op jit(solution)/shard_map/ppermute | solution.py:525
  14.5 4.9 %collective-permute-start.5 = (f32[144,128]{1,0:T(8,128)S(1)}, f32[144,128]{1,0:T(8,128)S(1)}, u32[]{:S(2)}, u32[]{:S(2)}) collective-permute-start(f32[144,128]{1,0:T(8,128)S(1)} %get-tuple-element.35), channel_id=1, source_target_pairs={{0,2},{2,0},{4,6},{6,4},{1,3},{3,1},{5,7},{7,5},{8,10},{10,8},{12,... | collective-permute-start | bytes 221192 | tf_op jit(solution)/shard_map/ppermute | solution.py:525
  19.4 5.3 %collective-permute-start.8 = (f32[64,128]{1,0:T(8,128)S(1)}, f32[64,128]{1,0:T(8,128)S(1)}, u32[]{:S(2)}, u32[]{:S(2)}) collective-permute-start(f32[64,128]{1,0:T(8,128)S(1)} %get-tuple-element.40), channel_id=1, source_target_pairs={{0,25},{1,24},{8,17},{9,16},{16,9},{17,8},{24,1},{25,0},{2,27},{3,... | collective-permute-start | bytes 98312 | tf_op jit(solution)/shard_map/ppermute | solution.py:538
  21.8 4.7 %collective-permute-start.7 = (f32[64,128]{1,0:T(8,128)S(1)}, f32[64,128]{1,0:T(8,128)S(1)}, u32[]{:S(2)}, u32[]{:S(2)}) collective-permute-start(f32[64,128]{1,0:T(8,128)S(1)} %get-tuple-element.39), channel_id=1, source_target_pairs={{0,17},{1,16},{8,25},{9,24},{16,1},{17,0},{24,9},{25,8},{2,19},{3,... | collective-permute-start | bytes 98312 | tf_op jit(solution)/shard_map/ppermute | solution.py:538
  21.8 4.9 %collective-permute-start.6 = (f32[64,128]{1,0:T(8,128)S(1)}, f32[64,128]{1,0:T(8,128)S(1)}, u32[]{:S(2)}, u32[]{:S(2)}) collective-permute-start(f32[64,128]{1,0:T(8,128)S(1)} %get-tuple-element.37), channel_id=1, source_target_pairs={{0,9},{1,8},{8,1},{9,0},{16,25},{17,24},{24,17},{25,16},{2,11},{3,... | collective-permute-start | bytes 98312 | tf_op jit(solution)/shard_map/ppermute | solution.py:538

commit v5 on v4

--- a/solution.py
+++ b/solution.py
@@ -10,9 +10,9 @@
 LANES = 128
 LANE_BITS = 7
 SUBLANES = 8
-VALUE_BITS = 16
-ID_BITS = 8
-MESSAGE_ROWS = 8
+VALUE_BITS = 24
+ROW_BITS = 16
+SECTION_ORDER = (2, 0, 1)
 HELD_ROWS = 16
 ROUNDS = 3
 TOGETHER = 2
@@ -34,90 +34,78 @@
     return lax.broadcasted_iota(jnp.int32, shape, dimension)
 
 
-def rank_of(hit):
-    rows, lanes = hit.shape
-    lane, row = iota(hit.shape, 1), iota(hit.shape, 0)
-    ones = hit.astype(jnp.int32)
-    running = ones
-    step = 1
-    while step < lanes:
-        running = running + jnp.where(lane >= step, pltpu.roll(running, step, 1), 0)
-        step *= 2
-    total = jnp.broadcast_to(jnp.sum(ones, axis=1, keepdims=True), hit.shape)
-    above = jnp.where(row >= 1, pltpu.roll(total, 1, 0), 0)
-    step = 1
-    while step < rows:
-        above = above + jnp.where(row >= step, pltpu.roll(above, step, 0), 0)
-        step *= 2
-    return running - ones + above
-
-
-def squeeze(hit, rank, value, value_bits):
-    rows, lanes = hit.shape
-    lane, row = iota(hit.shape, 1), iota(hit.shape, 0)
-    held = jnp.where(hit, ((row * lanes + lane - rank) << value_bits) | value, -1)
-    bit = 0
-    while 1 << bit < rows * lanes:
-        step = 1 << bit
-        if step < lanes:
-            turned = pltpu.roll(held, lanes - step, 1)
-            coming = jnp.where(lane < lanes - step, turned, pltpu.roll(turned, rows - 1, 0))
-        else:
-            coming = pltpu.roll(held, rows - step // lanes, 0)
-        comes = (coming >= 0) & ((coming >> (value_bits + bit)) & 1 == 1)
-        stays = (held >= 0) & ((held >> (value_bits + bit)) & 1 == 0)
-        held = jnp.where(comes, coming, jnp.where(stays, held, -1))
-        bit += 1
-    return jnp.where(held >= 0, held & ((1 << value_bits) - 1), -1)
-
-
-def list_kernel(groups, owner_ref, block_ref, row_ref, *refs):
-    sources, (first, second, own_ref, slot_ref, *kept) = refs[:4], refs[4:11]
-    cell_ref, block_pad, row_pad, sems = refs[11:]
+def gather_lanes(values, index):
+    return jnp.take_along_axis(values, index, axis=1, mode="promise_in_bounds")
+
+
+def compact(hits, values, pages):
+    rows, lanes = hits[0].shape
+    shape = (rows, lanes)
+    lane, row = iota(shape, 1), iota(shape, 0)
+    ones, above = [], []
+    for hit in hits:
+        one = hit.astype(jnp.int32)
+        upper = one
+        step = 1
+        while step < rows:
+            upper = upper + jnp.where(row >= step, pltpu.roll(upper, step, 0), 0)
+            step *= 2
+        ones.append(one.astype(jnp.float32))
+        above.append((upper - one).astype(jnp.float32))
+    blank = [jnp.zeros(shape, jnp.float32)] * (-len(hits) % 2)
+    left = jnp.concatenate(ones + blank + above + blank, axis=0).astype(jnp.bfloat16)
+    square = (lanes, lanes)
+    earlier = (iota(square, 0) < iota(square, 1)).astype(jnp.bfloat16)
+    right = jnp.concatenate([earlier, jnp.ones(square, jnp.bfloat16)], axis=1)
+    sums = jnp.dot(left, right, preferred_element_type=jnp.float32).astype(jnp.int32)
+    results, places = [], []
+    for number, hit in enumerate(hits):
+        start = number * rows
+        rank, count = sums[start : start + rows, :lanes], sums[start : start + rows, lanes:]
+        start += (len(hits) + len(blank)) * rows
+        before = sums[start : start + rows, lanes:]
+        held = jnp.where(hit, ((lane - rank) << VALUE_BITS) | values, -1)
+        bit = 0
+        while 1 << bit < lanes:
+            coming = pltpu.roll(held, lanes - (1 << bit), 1)
+            comes = (coming >= 0) & ((coming >> (VALUE_BITS + bit)) & 1 == 1)
+            stays = (held >= 0) & ((held >> (VALUE_BITS + bit)) & 1 == 0)
+            held = jnp.where(comes, coming, jnp.where(stays, held, -1))
+            bit += 1
+        held = held & ((1 << VALUE_BITS) - 1)
+        lines = []
+        for page in range(pages):
+            offset = page * lanes + lane - before
+            inside = (offset >= 0) & (offset < count)
+            got = jnp.where(inside, gather_lanes(held, offset & (lanes - 1)), 0)
+            lines.append(jnp.sum(got, axis=0, keepdims=True))
+        results.append(lines)
+        places.append(rank + before)
+    return results, places
+
+
+def list_kernel(groups, owner_any, cell_any, first, second, slot_ref, owner_ref, cell_ref, sems):
     copies = [
         pltpu.make_async_copy(source, target, sems.at[index])
-        for index, (source, target) in enumerate(zip(sources, (cell_ref, *kept)))
+        for index, (source, target) in enumerate(((owner_any, owner_ref), (cell_any, cell_ref)))
     ]
     for copy in copies:
         copy.start()
-    blocks = block_ref.shape[1]
-    block_pad[...] = jnp.full(block_pad.shape, -1, jnp.int32)
-    row_pad[...] = jnp.zeros(row_pad.shape, jnp.int32)
-    block_pad[0:1, 0:blocks] = block_ref[...]
-    row_pad[0:1, 0:blocks] = row_ref[...]
     tile, side = lax.axis_index("grid"), lax.axis_index("side")
+    for copy in copies:
+        copy.wait()
     owners = owner_ref[...]
-    landing = block_pad[...]
-    marked = row_pad[...] | (iota(landing.shape, 1) << VALUE_BITS)
     half = owners.shape[0] // 2
     hits = [owners == partner_of(tile, number, groups) for number in range(ROUNDS)]
-    ranks = [rank_of(hit) for hit in hits]
-    copies[0].wait()
-    cells = cell_ref[...]
+    pages, ranks = compact(hits, cell_ref[...], half)
     slots = jnp.zeros_like(owners)
-    own_ref[...] = jnp.full(own_ref.shape, -1, jnp.int32)
-    pages = []
-    for number in range(ROUNDS):
-        partner = partner_of(tile, number, groups)
-        hit, rank = hits[number], ranks[number]
+    for number, (hit, rank) in enumerate(zip(hits, ranks)):
         slots = jnp.where(hit, number * half * LANES + rank, slots)
-        wanted = squeeze(hit, rank, cells, VALUE_BITS)
-        lands = landing == partner
-        block = squeeze(lands, rank_of(lands), marked, VALUE_BITS + ID_BITS)
-        rows = jnp.where(block >= 0, block & ((1 << VALUE_BITS) - 1), -1)
-        pages.append((jnp.maximum(wanted[0:half], 0), rows[0:1]))
-        own_ref[number : number + 1, :] = jnp.where(block >= 0, block >> VALUE_BITS, -1)[0:1]
     slot_ref[...] = slots
-    for target, (here, there) in ((first, (pages[0], pages[2])), (second, (pages[1], pages[1]))):
-        target[...] = jnp.full(target.shape, -1, jnp.int32)
-        target[0:half, :] = jnp.where(side == 0, here[0], there[0])
-        target[half : half + 1, :] = jnp.where(side == 0, here[1], there[1])
-    for copy in copies[1:]:
-        copy.wait()
-
-
-def gather_lanes(values, index):
-    return jnp.take_along_axis(values, index, axis=1, mode="promise_in_bounds")
+    for target, here, there in ((first, 0, 2), (second, 1, 1)):
+        target[...] = jnp.zeros(target.shape, jnp.int32)
+        for line in range(half):
+            target[line : line + 1, :] = jnp.where(side == 0, pages[here][line], pages[there][line])
 
 
 def fold(values, least):
@@ -128,13 +116,9 @@
     return values
 
 
-def panel_rows(lev_dev, fields, tiles, groups, lists, group, state, terrain, packed, scratch):
+def panel_rows(lev_dev, fields, tiles, groups, lists, group, state, packed, scratch):
     levels = SUBLANES
     bits = (levels - 1).bit_length()
-    total = jnp.zeros((tiles, LANES), jnp.int32)
-    for level in range(levels):
-        total = total | (terrain[pl.ds(level, tiles, stride=levels), :] << (bits * level))
-    packed[...] = total
     shape = (SUBLANES, LANES)
     sub = iota(shape, 0)
     per = SUBLANES // lev_dev
@@ -235,52 +219,100 @@
     lax.fori_loop(0, ROUNDS * quarters // TOGETHER, some_tiles, 0)
 
 
-def produce_kernel(lev_dev, fields, partners, groups, own_ref, *refs):
-    lists, state, terrain, weight = refs[:3], refs[3], refs[4], refs[5]
-    parts = refs[6 : 6 + partners]
-    mass, scratch, packed, own, sem = refs[6 + partners :]
-    copy = pltpu.make_async_copy(own_ref, own, sem)
-    copy.start()
-    tiles = terrain.shape[0] // SUBLANES
+def prepare_kernel(lev_dev, fields, groups, block_owner, block_row, *refs):
+    sources, (state, packed, table, facts) = refs[:3], refs[3:7]
+    terrain, weight, owner_pad, row_pad, own_page, own, sems = refs[7:]
+    state_copy, terrain_copy, weight_copy = [
+        pltpu.make_async_copy(source, target, sems.at[index])
+        for index, (source, target) in enumerate(zip(sources, (state, terrain, weight)))
+    ]
+    own_copy = pltpu.make_async_copy(own_page, own, sems.at[3])
+    tile, side, group = lax.axis_index("grid"), lax.axis_index("side"), lax.axis_index("lev")
+    tiles = packed.shape[0]
+    terrain_copy.start()
+    state_copy.start()
+
+    @pl.when(side == 0)
+    def _():
+        levels = SUBLANES
+        bits = (levels - 1).bit_length()
+        terrain_copy.wait()
+        total = jnp.zeros((tiles, LANES), jnp.int32)
+        for level in range(levels):
+            total = total | (terrain[pl.ds(level, tiles, stride=levels), :] << (bits * level))
+        packed[...] = total
+        state_copy.wait()
+
+    @pl.when(side == 1)
+    def _():
+        weight_copy.start()
+        blocks = block_owner.shape[1]
+        owner_pad[...] = jnp.full(owner_pad.shape, -1, jnp.int32)
+        row_pad[...] = jnp.zeros(row_pad.shape, jnp.int32)
+        owner_pad[0:1, 0:blocks] = block_owner[...]
+        row_pad[0:1, 0:blocks] = block_row[...]
+        owners = owner_pad[...]
+        hits = [owners == partner_of(tile, number, groups) for number in range(ROUNDS)]
+        marked = ((iota(owners.shape, 1) + 1) << ROW_BITS) | row_pad[...]
+        pages, _ = compact(hits, marked, 1)
+        own_page[...] = jnp.zeros(own_page.shape, jnp.int32)
+        count = facts.shape[0] - SUBLANES
+        facts[count:, :] = jnp.zeros((SUBLANES, LANES), jnp.float32)
+        for number, (line,) in enumerate(pages):
+            name = line >> ROW_BITS
+            own_page[number : number + 1, :] = name - 1
+            run = jnp.where(name > 0, line & ((1 << ROW_BITS) - 1), -1)
+            facts[count + number : count + number + 1, :] = run.astype(jnp.float32)
+        own_copy.start()
+        own_copy.wait()
+        terrain_copy.wait()
+        state_copy.wait()
+        weight_copy.wait()
+        block_rows(lev_dev, fields, tiles, own, group, state, terrain, weight, table, facts)
+
+
+def produce_kernel(lev_dev, fields, partners, groups, *refs):
+    lists, state, packed, table = refs[:3], refs[3], refs[4], refs[5]
+    parts, scratch = refs[6 : 6 + partners], refs[6 + partners]
+    tiles = packed.shape[0]
     side, group = lax.axis_index("side"), lax.axis_index("lev")
 
+    def emit(source):
+        rows = source.shape[0] // SUBLANES
+        for distance in range(partners):
+            target = group ^ distance
+            for level in range(lev_dev):
+                parts[distance][level * rows : (level + 1) * rows, :] = source[
+                    pl.ds(target * lev_dev + level, rows, stride=SUBLANES), :
+                ]
+
     @pl.when(side == 0)
     def _():
-        mass[...] = jnp.zeros_like(mass)
-        panel_rows(lev_dev, fields, tiles, groups, lists, group, state, terrain, packed, scratch)
-        copy.wait()
+        panel_rows(lev_dev, fields, tiles, groups, lists, group, state, packed, scratch)
+        emit(scratch)
 
     @pl.when(side == 1)
     def _():
-        copy.wait()
-        block_rows(lev_dev, fields, tiles, own, group, state, terrain, weight, scratch, mass)
-
-    rows = scratch.shape[0] // SUBLANES
-    for distance in range(partners):
-        target = group ^ distance
-        for level in range(lev_dev):
-            parts[distance][level * rows : (level + 1) * rows, :] = scratch[
-                pl.ds(target * lev_dev + level, rows, stride=SUBLANES), :
-            ]
+        emit(table)
 
 
 def sum_kernel(lev_dev, fields, partners, *refs):
-    parts, mass, sections = refs[:partners], refs[partners], refs[partners + 1 :]
+    parts, facts, sections = refs[:partners], refs[partners], refs[partners + 1 :]
     total = parts[0][...]
     for part in parts[1:]:
         total = total + part[...]
     rows = total.shape[0] // lev_dev
-    span = rows // 3
+    span = rows // ROUNDS
     quarters = span // fields
+    masses = facts.shape[0] - SUBLANES
     for number, section in enumerate(sections):
         for level in range(lev_dev):
             start = level * rows + number * span
             section[level * span : (level + 1) * span, :] = total[start : start + span]
-        section[lev_dev * span : lev_dev * span + quarters, :] = mass[
-            number * quarters : (number + 1) * quarters, :
-        ]
-        tail = lev_dev * span + quarters
-        section[tail:, :] = jnp.zeros((section.shape[0] - tail, LANES), jnp.float32)
+        last = lev_dev * span + quarters
+        section[last - quarters : last, :] = facts[number * quarters : (number + 1) * quarters, :]
+        section[last:, :] = jnp.zeros((section.shape[0] - last, LANES), jnp.float32)
+        section[last : last + 1, :] = facts[masses + number : masses + number + 1, :]
 
 
 def place_panel(lev_dev, fields, number, fresh, section, slots, found):
@@ -300,12 +332,16 @@
             found[row : row + SUBLANES, :] = jnp.where(here, got, before)
 
 
-def place_blocks(coarse, number, section, page, spread_high, spread_low):
+def runs_of(section, quarters, kinds):
+    row = quarters * kinds
+    return section[row : row + 1, :].astype(jnp.int32)
+
+
+def place_blocks(coarse, quarters, number, section, spread_high, spread_low):
     shape = (SUBLANES, LANES)
     lane, sub = iota(shape, 1), iota(shape, 0)
-    quarters = page.shape[0] // 2
     kinds = spread_high.shape[1] // LANES
-    runs = jnp.broadcast_to(page[quarters : quarters + 1, :], shape)
+    runs = jnp.broadcast_to(runs_of(section, quarters, kinds), shape)
     indices, heres = [], []
     for quarter in range(quarters):
         run = jnp.where(lane == quarter * SUBLANES + sub, runs, 0)
@@ -328,13 +364,13 @@
             spread_low[here] = (both - high.astype(jnp.float32)).astype(jnp.bfloat16)
 
 
-def place_kernel(lev_dev, fields, coarse, groups, number, fresh, section, page, slots, *refs):
+def place_kernel(lev_dev, fields, coarse, groups, number, fresh, section, slots, *refs):
     spread_high, spread_low, found = refs[-3:]
     side = lax.axis_index("side")
 
     @pl.when(side == 0)
     def _():
-        place_blocks(coarse, number, section, page, spread_high, spread_low)
+        place_blocks(coarse, slots.shape[0] // 2, number, section, spread_high, spread_low)
 
     @pl.when(side == 1)
     def _():
@@ -367,15 +403,16 @@
         send(field)
 
 
-def finish_coarse(lev_dev, fields, tiles, coarse, pages, spread_high, spread_low, state, staged, send):
-    quarters = pages[0].shape[0] // 2
+def finish_coarse(
+    lev_dev, fields, tiles, coarse, quarters, sections, spread_high, spread_low, state, staged, send
+):
     width = quarters * SUBLANES
     shift = (LANES // coarse).bit_length() - 1
     tile = iota((tiles, LANES), 0)
     lane = iota((1, LANES), 1)
     runs = jnp.full((1, LANES), -1, jnp.int32)
-    for number, page in enumerate(pages):
-        turned = page[quarters : quarters + 1, :]
+    for number, section in enumerate(sections):
+        turned = runs_of(section, quarters, lev_dev * fields + 1)
         if number:
             turned = pltpu.roll(jnp.broadcast_to(turned, (SUBLANES, LANES)), number * width, 1)[0:1]
         runs = jnp.where(lane // width == number, turned, runs)
@@ -395,9 +432,10 @@
         send(field)
 
 
-def finish_kernel(lev_dev, fields, coarse, groups, number, section, *refs):
-    pages, slots, kept, state = refs[:3], refs[3], refs[4:7], refs[7]
+def finish_kernel(lev_dev, fields, coarse, groups, number, *refs):
+    sections, slots, kept, state = refs[:3], refs[3], refs[4:7], refs[7]
     out, spread_high, spread_low, found, staged, sems = refs[8:]
+    quarters = slots.shape[0] // 2
     tiles = state.shape[0] // (fields * lev_dev)
     rows = tiles * lev_dev
     copies = [
@@ -417,15 +455,15 @@
     def _():
         spread_high[...] = kept[0][...]
         spread_low[...] = kept[1][...]
-        place_blocks(coarse, number, section, pages[number], spread_high, spread_low)
+        place_blocks(coarse, quarters, number, sections[number], spread_high, spread_low)
         finish_coarse(
-            lev_dev, fields, tiles, coarse, pages, spread_high, spread_low, state, staged, send
+            lev_dev, fields, tiles, coarse, quarters, sections, spread_high, spread_low, state, staged, send
         )
 
     @pl.when(side == 1)
     def _():
         found[...] = kept[2][...]
-        place_panel(lev_dev, fields, answer_round(number, groups), False, section, slots, found)
+        place_panel(lev_dev, fields, answer_round(number, groups), False, sections[number], slots, found)
         finish_panel(lev_dev, fields, tiles, slots.shape[0], found, state, staged, send)
 
     for copy in copies:
@@ -467,32 +505,20 @@
     terrain = (
         terrain_level.reshape(levels, tiles, LANES).transpose(1, 0, 2).reshape(tiles * levels, LANES)
     )
-    message = struct((MESSAGE_ROWS, LANES), jnp.int32)
     page = struct((panel_tiles, LANES), jnp.int32)
-    first, second, own, slots, state, terrain, weight = pl.pallas_call(
+    first, second, slots = pl.pallas_call(
         functools.partial(list_kernel, groups),
-        out_shape=[message] * 3
-        + [page]
-        + [struct(state.shape), struct(terrain.shape, jnp.int32), struct(block_weight.shape)],
-        in_specs=specs(*[VMEM] * 3, *[pl.ANY] * 4),
-        out_specs=specs(*[VMEM] * 7),
+        out_shape=[page] * 3,
+        in_specs=specs(*[pl.ANY] * 2),
+        out_specs=specs(*[VMEM] * 3),
         scratch_shapes=[
             VMEM(page.shape, jnp.int32),
-            VMEM((SUBLANES, LANES), jnp.int32),
-            VMEM((SUBLANES, LANES), jnp.int32),
-            pltpu.SemaphoreType.DMA((4,)),
+            VMEM(page.shape, jnp.int32),
+            pltpu.SemaphoreType.DMA((2,)),
         ],
         compiler_params=params(),
         name="lists",
-    )(
-        panel_owner.reshape(page.shape),
-        block_owner.reshape(1, blocks),
-        block_row.reshape(1, blocks),
-        panel_cell.reshape(page.shape),
-        in_hbm(state),
-        in_hbm(terrain),
-        in_hbm(block_weight),
-    )
+    )(in_hbm(panel_owner.reshape(page.shape)), in_hbm(panel_cell.reshape(page.shape)))
 
     def towards(number_of, cross):
         return [
@@ -506,21 +532,44 @@
     third = lax.ppermute(first, "side", [(0, 1), (1, 0)])
     lists = [first, second, third]
     scratch_rows = ROUNDS * fields * quarters
+    table_shape = (scratch_rows * SUBLANES, LANES)
+    state, packed, table, facts = pl.pallas_call(
+        functools.partial(prepare_kernel, lev_dev, fields, groups),
+        out_shape=[
+            struct(state.shape),
+            struct((tiles, LANES), jnp.int32),
+            struct(table_shape),
+            struct((ROUNDS * quarters + SUBLANES, LANES)),
+        ],
+        in_specs=specs(*[VMEM] * 2, *[pl.ANY] * 3),
+        out_specs=specs(*[VMEM] * 4),
+        scratch_shapes=[
+            VMEM(terrain.shape, jnp.int32),
+            VMEM(block_weight.shape, jnp.float32),
+            *[VMEM((SUBLANES, LANES), jnp.int32)] * 3,
+            SMEM((SUBLANES, LANES), jnp.int32),
+            pltpu.SemaphoreType.DMA((4,)),
+        ],
+        cost_estimate=pl.CostEstimate(flops=0, bytes_accessed=8_000_000, transcendentals=0),
+        compiler_params=params(),
+        name="prepare",
+    )(
+        block_owner.reshape(1, blocks),
+        block_row.reshape(1, blocks),
+        in_hbm(state),
+        in_hbm(terrain),
+        in_hbm(block_weight),
+    )
     part = struct((lev_dev * scratch_rows, LANES))
-    *parts, mass = pl.pallas_call(
+    parts = pl.pallas_call(
         functools.partial(produce_kernel, lev_dev, fields, partners, groups),
-        out_shape=[part] * partners + [struct((2 * SUBLANES, LANES))],
-        in_specs=specs(*[VMEM] * 7),
-        out_specs=specs(*[VMEM] * (partners + 1)),
-        scratch_shapes=[
-            VMEM((scratch_rows * SUBLANES, LANES), jnp.float32),
-            VMEM((tiles, LANES), jnp.int32),
-            SMEM((MESSAGE_ROWS, LANES), jnp.int32),
-            pltpu.SemaphoreType.DMA,
-        ],
+        out_shape=[part] * partners,
+        in_specs=specs(*[VMEM] * 6),
+        out_specs=specs(*[VMEM] * partners),
+        scratch_shapes=[VMEM(table_shape, jnp.float32)],
         compiler_params=params(),
         name="produce",
-    )(own, *lists, state, terrain, weight)
+    )(*lists, state, packed, table)
     arrived = [parts[0]] + [
         lax.ppermute(parts[distance], "lev", [(rank, rank ^ distance) for rank in range(partners)])
         for distance in range(partners - 1, 0, -1)
@@ -533,36 +582,37 @@
         out_specs=specs(*[VMEM] * 3),
         compiler_params=params(),
         name="sections",
-    )(*arrived, mass)
+    )(*arrived, facts)
     sections = [
         lax.ppermute(sections[number], ("grid", "side"), towards(lambda side: number, 1))
-        for number in range(ROUNDS - 1, -1, -1)
-    ][::-1]
+        for number in SECTION_ORDER
+    ]
+    sections = [sections[SECTION_ORDER.index(number)] for number in range(ROUNDS)]
     kinds = lev_dev * fields + 1
     spread = struct((ROUNDS * quarters * SUBLANES, kinds * LANES), jnp.bfloat16)
     kept = [spread, spread, struct((panel_tiles * lev_dev * fields * quarters, LANES))]
     sizes = (lev_dev, fields, coarse, groups)
     held = []
-    for number in range(ROUNDS - 1, 0, -1):
+    for number in SECTION_ORDER[:-1]:
         held = pl.pallas_call(
             functools.partial(place_kernel, *sizes, number, not held),
             out_shape=kept,
-            in_specs=specs(*[VMEM] * (3 + len(held))),
+            in_specs=specs(*[VMEM] * (2 + len(held))),
             out_specs=specs(*[VMEM] * 3),
-            input_output_aliases={3 + index: index for index in range(len(held))},
+            input_output_aliases={2 + index: index for index in range(len(held))},
             compiler_params=params(),
             name="place",
-        )(sections[number], lists[number], slots, *held)
+        )(sections[number], slots, *held)
     result = pl.pallas_call(
-        functools.partial(finish_kernel, *sizes, 0),
+        functools.partial(finish_kernel, *sizes, SECTION_ORDER[-1]),
         out_shape=pltpu.HBM(state.shape, jnp.float32),
-        in_specs=specs(*[VMEM] * 9),
+        in_specs=specs(*[VMEM] * 8),
         out_specs=pl.BlockSpec(memory_space=pltpu.HBM),
         scratch_shapes=[VMEM(one.shape, one.dtype) for one in kept]
         + [VMEM(state.shape, jnp.float32), pltpu.SemaphoreType.DMA((fields,))],
         compiler_params=params(),
         name="finish",
-    )(sections[0], *lists, slots, *held, state)
+    )(*sections, slots, *held, state)
     return (
         result.reshape(fields, tiles, lev_dev, LANES)
         .transpose(2, 0, 1, 3)

time: 28.1 us -> 27.3 us (0.972)
  waiting for transfers between devices: 9.2 us -> 7.42 us
  Pallas kernels: 4.88 us -> 5.88 us
    ppermute x1, waiting for transfers between devices: 1.91 us -> 0.12 us  [on_device(): second = lax.ppermute(second, ('grid', 'side'), towards(lambda side: 1, 0))]
    pallas_call x2 -> x3, Pallas kernels: 2.78 us -> 3.77 us  [the longest x1 1.46 us: on_device(): pl.pallas_call(functools.partial(list_kernel, groups), out_shape=[page] *...]
    unnamed x8 -> x4, local copies, waits for them, and re-layouts: 0.7 us -> 0.66 us
  transfers between devices with their start and end apart: 9 -> 9, of which waited for: 6 -> 7; matrix products, arithmetic and copies ran while one was open for 0% -> 0% of each run, Pallas kernels for 2% -> 6%
where the time goes in v5:
time: 27.3 us; the launch traced here: 27 us
  starting transfers between devices  13 us (48%)
  waiting for transfers between devices  7.42 us (27%)
  Pallas kernels  5.88 us (22%)
  local copies, waits for them, and re-layouts  0.66 us (2%)
    ppermute x3, waiting for transfers between devices, on_device(): lax.ppermute(parts[distance], 'lev', [(rank, rank ^ distance) for rank in...  4.5 us
    ppermute x3, starting transfers between devices, on_device(): lax.ppermute(sections[number], ('grid', 'side'), towards(lambda side: num...  3.79 us
    ppermute x3, starting transfers between devices, on_device(): lax.ppermute(parts[distance], 'lev', [(rank, rank ^ distance) for rank in...  3.55 us
    ppermute x1, starting transfers between devices, on_device(): lax.ppermute(first, ('grid', 'side'), towards(lambda side: 2 * side, 0))  3.09 us
    ppermute x3, waiting for transfers between devices, on_device(): lax.ppermute(sections[number], ('grid', 'side'), towards(lambda side: num...  2.79 us
    ppermute x1, starting transfers between devices, on_device(): second = lax.ppermute(second, ('grid', 'side'), towards(lambda side: 1, 0))  2.59 us
    pallas_call x1, Pallas kernels, on_device(): pl.pallas_call(functools.partial(produce_kernel, lev_dev, fields, partner...  1.52 us
    pallas_call x1, Pallas kernels, on_device(): pl.pallas_call(functools.partial(list_kernel, groups), out_shape=[page] *...  1.46 us
  transfers between devices with their start and end apart: 9, of which 7 were waited for; matrix products, arithmetic and copies ran while one was open for 0% of the time, Pallas kernels for 6%

profile of v5, /device:TPU:0, one launch (start us, length us, event | category | flops | bytes accessed | tf_op | source)
XLA Modules:
  0.0 27.0 jit_solution(6012101345438762690)
XLA Ops:
  0.0 1.5 %lists.1 = (s32[8,128]{1,0:T(8,128)S(1)}, s32[8,128]{1,0:T(8,128)S(1)}, s32[8,128]{1,0:T(8,128)S(1)}) custom-call(s32[8,128]{1,0:T(8,128)} %bitcast.23, s32[8,128]{1,0:T(8,128)} %bitcast.24), custom_call_target="tpu_custom_call" | custom-call | tf_op jit(solution)/shard_map/lists/pallas_call | solution.py:509
  1.5 3.1 %collective-permute-start = (s32[8,128]{1,0:T(8,128)S(1)}, s32[8,128]{1,0:T(8,128)S(1)}, u32[]{:S(2)}, u32[]{:S(2)}) collective-permute-start(s32[8,128]{1,0:T(8,128)S(1)} %get-tuple-element.25), channel_id=1, source_target_pairs={{0,8},{1,25},{8,0},{9,17},{16,24},{17,9},{24,16},{25,1},{2,10},{3,... | collective-permute-start | bytes 12296 | tf_op jit(solution)/shard_map/ppermute | solution.py:530
  4.6 2.6 %collective-permute-start.1 = (s32[8,128]{1,0:T(8,128)S(1)}, s32[8,128]{1,0:T(8,128)S(1)}, u32[]{:S(2)}, u32[]{:S(2)}) collective-permute-start(s32[8,128]{1,0:T(8,128)S(1)} %get-tuple-element.26), channel_id=1, source_target_pairs={{0,16},{1,17},{8,24},{9,25},{16,0},{17,1},{24,8},{25,9},{2,18},{3,... | collective-permute-start | bytes 12296 | tf_op jit(solution)/shard_map/ppermute | solution.py:531
  7.1 0.0 collective-permute-done.refs_0_
  7.2 0.0 collective-permute-start.2
  7.2 0.0 copy-start
  7.2 0.0 copy-start.1
  7.2 0.6 %copy-done = s32[64,1]{0,1:T(1,128)S(1)} copy-done((s32[64,1]{0,1:T(1,128)S(1)}, s32[64,1]{0,1:T(1,128)}, u32[]{:S(2)}) %copy-start) | copy-done | bytes 280
  7.8 0.0 copy-done.1
  7.8 1.1 %prepare.1 = (f32[768,128]{1,0:T(8,128)S(1)}, s32[64,128]{1,0:T(8,128)S(1)}, f32[576,128]{1,0:T(8,128)S(1)}, f32[20,128]{1,0:T(8,128)S(1)}) custom-call(s32[1,64]{1,0:T(1,128)S(1)} %bitcast.19, s32[1,64]{1,0:T(1,128)S(1)} %bitcast.20, f32[768,128]{1,0:T(8,128)} %bitcast.21, s32[512,128]{1,0:T(8,128)} %bitcast.22, f32[64,16,128]{2,1,0:T(8,128)} %refs_2_.1), custom_call_target="tpu_custom_call" | custom-call | bytes 8000000 | tf_op jit(solution)/shard_map/prepare/pallas_call | solution.py:536
  8.9 0.1 collective-permute-done.1.refs_1_
  9.1 0.0 collective-permute-done.2.refs_2_
  9.1 1.5 %produce.1 = (f32[144,128]{1,0:T(8,128)S(1)}, f32[144,128]{1,0:T(8,128)S(1)}, f32[144,128]{1,0:T(8,128)S(1)}, f32[144,128]{1,0:T(8,128)S(1)}) custom-call(s32[8,128]{1,0:T(8,128)S(1)} %collective-permute-done.refs_0_, s32[8,128]{1,0:T(8,128)S(1)} %collective-permute-done.1.refs_1_, s32[8,128]{1,0:T(8,128)S(1)} %collective-permute-done.2.refs_2_, ...), custom_call_target="tpu_custom_call" | custom-call | tf_op jit(solution)/shard_map/produce/pallas_call | solution.py:564
  10.6 2.5 %collective-permute-start.3 = (f32[144,128]{1,0:T(8,128)S(1)}, f32[144,128]{1,0:T(8,128)S(1)}, u32[]{:S(2)}, u32[]{:S(2)}) collective-permute-start(f32[144,128]{1,0:T(8,128)S(1)} %get-tuple-element.31), channel_id=1, source_target_pairs={{0,6},{2,4},{4,2},{6,0},{1,7},{3,5},{5,3},{7,1},{8,14},{10,12},{12... | collective-permute-start | bytes 221192 | tf_op jit(solution)/shard_map/ppermute | solution.py:574
  13.1 0.5 %collective-permute-start.4 = (f32[144,128]{1,0:T(8,128)S(1)}, f32[144,128]{1,0:T(8,128)S(1)}, u32[]{:S(2)}, u32[]{:S(2)}) collective-permute-start(f32[144,128]{1,0:T(8,128)S(1)} %get-tuple-element.32), channel_id=1, source_target_pairs={{0,4},{2,6},{4,0},{6,2},{1,5},{3,7},{5,1},{7,3},{8,12},{10,14},{12... | collective-permute-start | bytes 221192 | tf_op jit(solution)/shard_map/ppermute | solution.py:574
  13.6 0.5 %collective-permute-start.5 = (f32[144,128]{1,0:T(8,128)S(1)}, f32[144,128]{1,0:T(8,128)S(1)}, u32[]{:S(2)}, u32[]{:S(2)}) collective-permute-start(f32[144,128]{1,0:T(8,128)S(1)} %get-tuple-element.33), channel_id=1, source_target_pairs={{0,2},{2,0},{4,6},{6,4},{1,3},{3,1},{5,7},{7,5},{8,10},{10,8},{12,... | collective-permute-start | bytes 221192 | tf_op jit(solution)/shard_map/ppermute | solution.py:574
  14.2 2.2 %collective-permute-done.3.refs_1_ = f32[144,128]{1,0:T(8,128)S(1)} collective-permute-done((f32[144,128]{1,0:T(8,128)S(1)}, f32[144,128]{1,0:T(8,128)S(1)}, u32[]{:S(2)}, u32[]{:S(2)}) %collective-permute-start.3) | collective-permute-done | bytes 73760 | tf_op jit(solution)/shard_map/ppermute | solution.py:574
  16.3 1.8 %collective-permute-done.4.refs_2_ = f32[144,128]{1,0:T(8,128)S(1)} collective-permute-done((f32[144,128]{1,0:T(8,128)S(1)}, f32[144,128]{1,0:T(8,128)S(1)}, u32[]{:S(2)}, u32[]{:S(2)}) %collective-permute-start.4) | collective-permute-done | bytes 73760 | tf_op jit(solution)/shard_map/ppermute | solution.py:574
  18.1 0.5 %collective-permute-done.5.refs_3_ = f32[144,128]{1,0:T(8,128)S(1)} collective-permute-done((f32[144,128]{1,0:T(8,128)S(1)}, f32[144,128]{1,0:T(8,128)S(1)}, u32[]{:S(2)}, u32[]{:S(2)}) %collective-permute-start.5) | collective-permute-done | bytes 73760 | tf_op jit(solution)/shard_map/ppermute | solution.py:574
  18.7 2.8 %collective-permute-start.8 = (f32[64,128]{1,0:T(8,128)S(1)}, f32[64,128]{1,0:T(8,128)S(1)}, u32[]{:S(2)}, u32[]{:S(2)}) collective-permute-start(f32[64,128]{1,0:T(8,128)S(1)} %get-tuple-element.37), channel_id=1, source_target_pairs={{0,25},{1,24},{8,17},{9,16},{16,9},{17,8},{24,1},{25,0},{2,27},{3,... | collective-permute-start | bytes 98312 | tf_op jit(solution)/shard_map/ppermute | solution.py:587
  21.5 0.0 collective-permute-start.6
  21.5 1.0 %collective-permute-start.7 = (f32[64,128]{1,0:T(8,128)S(1)}, f32[64,128]{1,0:T(8,128)S(1)}, u32[]{:S(2)}, u32[]{:S(2)}) collective-permute-start(f32[64,128]{1,0:T(8,128)S(1)} %get-tuple-element.36), channel_id=1, source_target_pairs={{0,17},{1,16},{8,25},{9,24},{16,1},{17,0},{24,9},{25,8},{2,19},{3,... | collective-permute-start | bytes 98312 | tf_op jit(solution)/shard_map/ppermute | solution.py:587
  22.5 1.6 %collective-permute-done.8.section.refs_2_ = f32[64,128]{1,0:T(8,128)S(1)} collective-permute-done((f32[64,128]{1,0:T(8,128)S(1)}, f32[64,128]{1,0:T(8,128)S(1)}, u32[]{:S(2)}, u32[]{:S(2)}) %collective-permute-start.8) | collective-permute-done | bytes 32800 | tf_op jit(solution)/shard_map/ppermute | solution.py:587
  24.0 0.3 %place.2 = (bf16[96,1664]{1,0:T(8,128)(2,1)S(1)}, bf16[96,1664]{1,0:T(8,128)(2,1)S(1)}, f32[384,128]{1,0:T(8,128)S(1)}) custom-call(f32[64,128]{1,0:T(8,128)S(1)} %collective-permute-done.8.section.refs_2_, s32[8,128]{1,0:T(8,128)S(1)} %get-tuple-element.38.slots.refs_3_), custom_call_target="tpu_custom_call" | custom-call | tf_op jit(solution)/shard_map/place/pallas_call | solution.py:597
  24.3 0.5 %collective-permute-done.6.section.refs_0_ = f32[64,128]{1,0:T(8,128)S(1)} collective-permute-done((f32[64,128]{1,0:T(8,128)S(1)}, f32[64,128]{1,0:T(8,128)S(1)}, u32[]{:S(2)}, u32[]{:S(2)}) %collective-permute-start.6) | collective-permute-done | bytes 32800 | tf_op jit(solution)/shard_map/ppermute | solution.py:587
  24.9 0.3 %place.3 = (bf16[96,1664]{1,0:T(8,128)(2,1)S(1)}, bf16[96,1664]{1,0:T(8,128)(2,1)S(1)}, f32[384,128]{1,0:T(8,128)S(1)}) custom-call(f32[64,128]{1,0:T(8,128)S(1)} %collective-permute-done.6.section.refs_0_, s32[8,128]{1,0:T(8,128)S(1)} %get-tuple-element.38.slots.refs_3_, ...), custom_call_target="tpu_custom_call", output_to_operand_aliasing={{0}: (2, {}), {1}: (3, {}), {2}: (4, {})} | custom-call | tf_op jit(solution)/shard_map/place/pallas_call | solution.py:597
  25.1 0.7 %collective-permute-done.7.refs_1_ = f32[64,128]{1,0:T(8,128)S(1)} collective-permute-done((f32[64,128]{1,0:T(8,128)S(1)}, f32[64,128]{1,0:T(8,128)S(1)}, u32[]{:S(2)}, u32[]{:S(2)}) %collective-permute-start.7) | collective-permute-done | bytes 32800 | tf_op jit(solution)/shard_map/ppermute | solution.py:587
  25.8 1.2 %finish.1 = f32[768,128]{1,0:T(8,128)} custom-call(f32[64,128]{1,0:T(8,128)S(1)} %collective-permute-done.6.section.refs_0_, f32[64,128]{1,0:T(8,128)S(1)} %collective-permute-done.7.refs_1_, f32[64,128]{1,0:T(8,128)S(1)} %collective-permute-done.8.section.refs_2_, s32[8,128]{1,0:T(8,128)S(1)} %get-tuple-element.38.slots.refs_3_, ...), custom_call_target="tpu_custom_call" | custom-call | tf_op jit(solution)/shard_map/finish/pallas_call | solution.py:606
  (1 shorter events, 0.0 us)
Async XLA Ops:
  1.5 5.7 %collective-permute-start = (s32[8,128]{1,0:T(8,128)S(1)}, s32[8,128]{1,0:T(8,128)S(1)}, u32[]{:S(2)}, u32[]{:S(2)}) collective-permute-start(s32[8,128]{1,0:T(8,128)S(1)} %get-tuple-element.25), channel_id=1, source_target_pairs={{0,8},{1,25},{8,0},{9,17},{16,24},{17,9},{24,16},{25,1},{2,10},{3,... | collective-permute-start | bytes 12296 | tf_op jit(solution)/shard_map/ppermute | solution.py:530
  4.6 4.5 %collective-permute-start.1 = (s32[8,128]{1,0:T(8,128)S(1)}, s32[8,128]{1,0:T(8,128)S(1)}, u32[]{:S(2)}, u32[]{:S(2)}) collective-permute-start(s32[8,128]{1,0:T(8,128)S(1)} %get-tuple-element.26), channel_id=1, source_target_pairs={{0,16},{1,17},{8,24},{9,25},{16,0},{17,1},{24,8},{25,9},{2,18},{3,... | collective-permute-start | bytes 12296 | tf_op jit(solution)/shard_map/ppermute | solution.py:531
  7.2 1.9 %collective-permute-start.2 = (s32[8,128]{1,0:T(8,128)S(1)}, s32[8,128]{1,0:T(8,128)S(1)}, u32[]{:S(2)}, u32[]{:S(2)}) collective-permute-start(s32[8,128]{1,0:T(8,128)S(1)} %collective-permute-done.refs_0_), channel_id=1, source_target_pairs={{0,1},{1,0},{2,3},{3,2},{4,5},{5,4},{6,7},{7,6},{8,9},{9,8},{10,11... | collective-permute-start | bytes 12296 | tf_op jit(solution)/shard_map/ppermute | solution.py:532
  7.2 0.7 %copy-start = (s32[64,1]{0,1:T(1,128)S(1)}, s32[64,1]{0,1:T(1,128)}, u32[]{:S(2)}) copy-start(s32[64,1]{0,1:T(1,128)} %param.12) | copy-start | bytes 772
  7.2 0.7 %copy-start.1 = (s32[64]{0:T(128)S(1)}, s32[64]{0:T(128)}, u32[]{:S(2)}) copy-start(s32[64]{0:T(128)} %param.13) | copy-start | bytes 772
  10.6 5.7 %collective-permute-start.3 = (f32[144,128]{1,0:T(8,128)S(1)}, f32[144,128]{1,0:T(8,128)S(1)}, u32[]{:S(2)}, u32[]{:S(2)}) collective-permute-start(f32[144,128]{1,0:T(8,128)S(1)} %get-tuple-element.31), channel_id=1, source_target_pairs={{0,6},{2,4},{4,2},{6,0},{1,7},{3,5},{5,3},{7,1},{8,14},{10,12},{12... | collective-permute-start | bytes 221192 | tf_op jit(solution)/shard_map/ppermute | solution.py:574
  13.1 5.0 %collective-permute-start.4 = (f32[144,128]{1,0:T(8,128)S(1)}, f32[144,128]{1,0:T(8,128)S(1)}, u32[]{:S(2)}, u32[]{:S(2)}) collective-permute-start(f32[144,128]{1,0:T(8,128)S(1)} %get-tuple-element.32), channel_id=1, source_target_pairs={{0,4},{2,6},{4,0},{6,2},{1,5},{3,7},{5,1},{7,3},{8,12},{10,14},{12... | collective-permute-start | bytes 221192 | tf_op jit(solution)/shard_map/ppermute | solution.py:574
  13.6 5.0 %collective-permute-start.5 = (f32[144,128]{1,0:T(8,128)S(1)}, f32[144,128]{1,0:T(8,128)S(1)}, u32[]{:S(2)}, u32[]{:S(2)}) collective-permute-start(f32[144,128]{1,0:T(8,128)S(1)} %get-tuple-element.33), channel_id=1, source_target_pairs={{0,2},{2,0},{4,6},{6,4},{1,3},{3,1},{5,7},{7,5},{8,10},{10,8},{12,... | collective-permute-start | bytes 221192 | tf_op jit(solution)/shard_map/ppermute | solution.py:574
  18.7 5.4 %collective-permute-start.8 = (f32[64,128]{1,0:T(8,128)S(1)}, f32[64,128]{1,0:T(8,128)S(1)}, u32[]{:S(2)}, u32[]{:S(2)}) collective-permute-start(f32[64,128]{1,0:T(8,128)S(1)} %get-tuple-element.37), channel_id=1, source_target_pairs={{0,25},{1,24},{8,17},{9,16},{16,9},{17,8},{24,1},{25,0},{2,27},{3,... | collective-permute-start | bytes 98312 | tf_op jit(solution)/shard_map/ppermute | solution.py:587
  21.5 3.3 %collective-permute-start.6 = (f32[64,128]{1,0:T(8,128)S(1)}, f32[64,128]{1,0:T(8,128)S(1)}, u32[]{:S(2)}, u32[]{:S(2)}) collective-permute-start(f32[64,128]{1,0:T(8,128)S(1)} %get-tuple-element.35), channel_id=1, source_target_pairs={{0,9},{1,8},{8,1},{9,0},{16,25},{17,24},{24,17},{25,16},{2,11},{3,... | collective-permute-start | bytes 98312 | tf_op jit(solution)/shard_map/ppermute | solution.py:587
  21.5 4.3 %collective-permute-start.7 = (f32[64,128]{1,0:T(8,128)S(1)}, f32[64,128]{1,0:T(8,128)S(1)}, u32[]{:S(2)}, u32[]{:S(2)}) collective-permute-start(f32[64,128]{1,0:T(8,128)S(1)} %get-tuple-element.36), channel_id=1, source_target_pairs={{0,17},{1,16},{8,25},{9,24},{16,1},{17,0},{24,9},{25,8},{2,19},{3,... | collective-permute-start | bytes 98312 | tf_op jit(solution)/shard_map/ppermute | solution.py:587

commit v6 on v5

--- a/solution.py
+++ b/solution.py
@@ -15,7 +15,8 @@
 SECTION_ORDER = (2, 0, 1)
 HELD_ROWS = 16
 ROUNDS = 3
-TOGETHER = 2
+TOGETHER = 4
+DIGIT_BITS = 3
 VMEM = pltpu.VMEM
 SMEM = pltpu.SMEM
 
@@ -45,13 +46,9 @@
     ones, above = [], []
     for hit in hits:
         one = hit.astype(jnp.int32)
-        upper = one
-        step = 1
-        while step < rows:
-            upper = upper + jnp.where(row >= step, pltpu.roll(upper, step, 0), 0)
-            step *= 2
+        uppers = [jnp.where(row >= step, pltpu.roll(one, step, 0), 0) for step in range(1, rows)]
         ones.append(one.astype(jnp.float32))
-        above.append((upper - one).astype(jnp.float32))
+        above.append(sum(uppers).astype(jnp.float32))
     blank = [jnp.zeros(shape, jnp.float32)] * (-len(hits) % 2)
     left = jnp.concatenate(ones + blank + above + blank, axis=0).astype(jnp.bfloat16)
     square = (lanes, lanes)
@@ -65,13 +62,16 @@
         start += (len(hits) + len(blank)) * rows
         before = sums[start : start + rows, lanes:]
         held = jnp.where(hit, ((lane - rank) << VALUE_BITS) | values, -1)
-        bit = 0
-        while 1 << bit < lanes:
-            coming = pltpu.roll(held, lanes - (1 << bit), 1)
-            comes = (coming >= 0) & ((coming >> (VALUE_BITS + bit)) & 1 == 1)
-            stays = (held >= 0) & ((held >> (VALUE_BITS + bit)) & 1 == 0)
-            held = jnp.where(comes, coming, jnp.where(stays, held, -1))
-            bit += 1
+        bit, bits = 0, (lanes - 1).bit_length()
+        while bit < bits:
+            wide = min(DIGIT_BITS, bits - bit)
+            moved = jnp.full(shape, -1, jnp.int32)
+            for digit in range(1 << wide):
+                coming = pltpu.roll(held, lanes - (digit << bit), 1) if digit else held
+                comes = (coming >> (VALUE_BITS + bit)) & ((1 << wide) - 1) == digit
+                moved = jnp.where(comes & (coming >= 0), coming, moved)
+            held = moved
+            bit += wide
         held = held & ((1 << VALUE_BITS) - 1)
         lines = []
         for page in range(pages):
@@ -221,12 +221,13 @@
 
 def prepare_kernel(lev_dev, fields, groups, block_owner, block_row, *refs):
     sources, (state, packed, table, facts) = refs[:3], refs[3:7]
-    terrain, weight, owner_pad, row_pad, own_page, own, sems = refs[7:]
+    terrain, weight, own, owners, rows, sems = refs[7:]
     state_copy, terrain_copy, weight_copy = [
         pltpu.make_async_copy(source, target, sems.at[index])
         for index, (source, target) in enumerate(zip(sources, (state, terrain, weight)))
     ]
-    own_copy = pltpu.make_async_copy(own_page, own, sems.at[3])
+    owner_copy = pltpu.make_async_copy(block_owner, owners, sems.at[3])
+    row_copy = pltpu.make_async_copy(block_row, rows, sems.at[4])
     tile, side, group = lax.axis_index("grid"), lax.axis_index("side"), lax.axis_index("lev")
     tiles = packed.shape[0]
     terrain_copy.start()
@@ -246,25 +247,40 @@
     @pl.when(side == 1)
     def _():
         weight_copy.start()
-        blocks = block_owner.shape[1]
-        owner_pad[...] = jnp.full(owner_pad.shape, -1, jnp.int32)
-        row_pad[...] = jnp.zeros(row_pad.shape, jnp.int32)
-        owner_pad[0:1, 0:blocks] = block_owner[...]
-        row_pad[0:1, 0:blocks] = block_row[...]
-        owners = owner_pad[...]
-        hits = [owners == partner_of(tile, number, groups) for number in range(ROUNDS)]
-        marked = ((iota(owners.shape, 1) + 1) << ROW_BITS) | row_pad[...]
-        pages, _ = compact(hits, marked, 1)
-        own_page[...] = jnp.zeros(own_page.shape, jnp.int32)
+        owner_copy.start()
+        row_copy.start()
+        blocks = owners.shape[1]
         count = facts.shape[0] - SUBLANES
+        lane = iota((1, LANES), 1)
+        partners = [partner_of(tile, number, groups) for number in range(ROUNDS)]
+
+        def clear(place, carry):
+            for number in range(ROUNDS):
+                own[number, place] = -1
+            return carry
+
+        def enter(block, carry):
+            counts, runs = list(carry[:ROUNDS]), list(carry[ROUNDS:])
+            owner, row = owners[0, block], rows[0, block]
+            for number in range(ROUNDS):
+                mine = owner == partners[number]
+                own[number, counts[number]] = jnp.where(mine, block, -1)
+                runs[number] = jnp.where(
+                    (lane == counts[number]) & mine, row.astype(jnp.float32), runs[number]
+                )
+                counts[number] = counts[number] + mine.astype(jnp.int32)
+            return (*counts, *runs)
+
+        lax.fori_loop(0, blocks // 2 + 1, clear, 0, unroll=True)
+        owner_copy.wait()
+        row_copy.wait()
+        empty = jnp.full((1, LANES), -1.0, jnp.float32)
+        carry = lax.fori_loop(
+            0, blocks, enter, (jnp.int32(0),) * ROUNDS + (empty,) * ROUNDS, unroll=True
+        )
         facts[count:, :] = jnp.zeros((SUBLANES, LANES), jnp.float32)
-        for number, (line,) in enumerate(pages):
-            name = line >> ROW_BITS
-            own_page[number : number + 1, :] = name - 1
-            run = jnp.where(name > 0, line & ((1 << ROW_BITS) - 1), -1)
-            facts[count + number : count + number + 1, :] = run.astype(jnp.float32)
-        own_copy.start()
-        own_copy.wait()
+        for number in range(ROUNDS):
+            facts[count + number : count + number + 1, :] = carry[ROUNDS + number]
         terrain_copy.wait()
         state_copy.wait()
         weight_copy.wait()
@@ -541,21 +557,22 @@
             struct(table_shape),
             struct((ROUNDS * quarters + SUBLANES, LANES)),
         ],
-        in_specs=specs(*[VMEM] * 2, *[pl.ANY] * 3),
+        in_specs=specs(*[pl.ANY] * 5),
         out_specs=specs(*[VMEM] * 4),
         scratch_shapes=[
             VMEM(terrain.shape, jnp.int32),
             VMEM(block_weight.shape, jnp.float32),
-            *[VMEM((SUBLANES, LANES), jnp.int32)] * 3,
-            SMEM((SUBLANES, LANES), jnp.int32),
-            pltpu.SemaphoreType.DMA((4,)),
+            SMEM((ROUNDS, LANES), jnp.int32),
+            SMEM((1, blocks), jnp.int32),
+            SMEM((1, blocks), jnp.int32),
+            pltpu.SemaphoreType.DMA((5,)),
         ],
         cost_estimate=pl.CostEstimate(flops=0, bytes_accessed=8_000_000, transcendentals=0),
         compiler_params=params(),
         name="prepare",
     )(
-        block_owner.reshape(1, blocks),
-        block_row.reshape(1, blocks),
+        in_hbm(block_owner.reshape(1, blocks)),
+        in_hbm(block_row.reshape(1, blocks)),
         in_hbm(state),
         in_hbm(terrain),
         in_hbm(block_weight),

time: 27.3 us -> 26.4 us (0.967)
  local copies, waits for them, and re-layouts: 0.66 us -> 0 us
    ppermute x1, waiting for transfers between devices: 0.12 us -> 0.78 us  [on_device(): second = lax.ppermute(second, ('grid', 'side'), towards(lambda side: 1, 0))]
    unnamed x4 -> x0, local copies, waits for them, and re-layouts: 0.66 us -> none
    ppermute x3, waiting for transfers between devices: 4.5 us -> 4.14 us  [on_device(): lax.ppermute(parts[distance], 'lev', [(rank, rank ^ distance) for rank in...]
where the time goes in v6:
time: 26.4 us; the launch traced here: 26.2 us
  starting transfers between devices  13.1 us (50%)
  waiting for transfers between devices  7.49 us (28%)
  Pallas kernels  5.63 us (21%)
    ppermute x3, waiting for transfers between devices, on_device(): lax.ppermute(parts[distance], 'lev', [(rank, rank ^ distance) for rank in...  4.14 us
    ppermute x3, starting transfers between devices, on_device(): lax.ppermute(sections[number], ('grid', 'side'), towards(lambda side: num...  3.81 us
    ppermute x3, starting transfers between devices, on_device(): lax.ppermute(parts[distance], 'lev', [(rank, rank ^ distance) for rank in...  3.57 us
    ppermute x1, starting transfers between devices, on_device(): lax.ppermute(first, ('grid', 'side'), towards(lambda side: 2 * side, 0))  3.09 us
    ppermute x1, starting transfers between devices, on_device(): second = lax.ppermute(second, ('grid', 'side'), towards(lambda side: 1, 0))  2.59 us
    ppermute x3, waiting for transfers between devices, on_device(): lax.ppermute(sections[number], ('grid', 'side'), towards(lambda side: num...  2.56 us
    pallas_call x1, Pallas kernels, on_device(): pl.pallas_call(functools.partial(produce_kernel, lev_dev, fields, partner...  1.52 us
    pallas_call x1, Pallas kernels, on_device(): pl.pallas_call(functools.partial(finish_kernel, *sizes, SECTION_ORDER[-1]...  1.2 us
  transfers between devices with their start and end apart: 9, of which 7 were waited for; matrix products, arithmetic and copies ran while one was open for 0% of the time, Pallas kernels for 6%

profile of v6, /device:TPU:0, one launch (start us, length us, event | category | flops | bytes accessed | tf_op | source)
XLA Modules:
  0.0 26.2 jit_solution(16184851599330456928)
XLA Ops:
  0.0 1.2 %lists.1 = (s32[8,128]{1,0:T(8,128)S(1)}, s32[8,128]{1,0:T(8,128)S(1)}, s32[8,128]{1,0:T(8,128)S(1)}) custom-call(s32[8,128]{1,0:T(8,128)} %bitcast.21, s32[8,128]{1,0:T(8,128)} %bitcast.22), custom_call_target="tpu_custom_call" | custom-call | tf_op jit(solution)/shard_map/lists/pallas_call | solution.py:525
  1.2 3.1 %collective-permute-start = (s32[8,128]{1,0:T(8,128)S(1)}, s32[8,128]{1,0:T(8,128)S(1)}, u32[]{:S(2)}, u32[]{:S(2)}) collective-permute-start(s32[8,128]{1,0:T(8,128)S(1)} %get-tuple-element.25), channel_id=1, source_target_pairs={{0,8},{1,25},{8,0},{9,17},{16,24},{17,9},{24,16},{25,1},{2,10},{3,... | collective-permute-start | bytes 12296 | tf_op jit(solution)/shard_map/ppermute | solution.py:546
  4.3 2.6 %collective-permute-start.1 = (s32[8,128]{1,0:T(8,128)S(1)}, s32[8,128]{1,0:T(8,128)S(1)}, u32[]{:S(2)}, u32[]{:S(2)}) collective-permute-start(s32[8,128]{1,0:T(8,128)S(1)} %get-tuple-element.26), channel_id=1, source_target_pairs={{0,16},{1,17},{8,24},{9,25},{16,0},{17,1},{24,8},{25,9},{2,18},{3,... | collective-permute-start | bytes 12296 | tf_op jit(solution)/shard_map/ppermute | solution.py:547
  6.9 0.0 collective-permute-done.refs_0_
  6.9 0.0 collective-permute-start.2
  6.9 1.1 %prepare.1 = (f32[768,128]{1,0:T(8,128)S(1)}, s32[64,128]{1,0:T(8,128)S(1)}, f32[576,128]{1,0:T(8,128)S(1)}, f32[20,128]{1,0:T(8,128)S(1)}) custom-call(s32[1,64]{1,0:T(1,128)} %bitcast.23, s32[1,64]{1,0:T(1,128)} %bitcast.24, f32[768,128]{1,0:T(8,128)} %bitcast.19, s32[512,128]{1,0:T(8,128)} %bitcast.20, f32[64,16,128]{2,1,0:T(8,128)} %refs_2_.1), custom_call_target="tpu_custom_call" | custom-call | bytes 8000000 | tf_op jit(solution)/shard_map/prepare/pallas_call | solution.py:552
  8.0 0.8 %collective-permute-done.1.refs_1_ = s32[8,128]{1,0:T(8,128)S(1)} collective-permute-done((s32[8,128]{1,0:T(8,128)S(1)}, s32[8,128]{1,0:T(8,128)S(1)}, u32[]{:S(2)}, u32[]{:S(2)}) %collective-permute-start.1) | collective-permute-done | bytes 4128 | tf_op jit(solution)/shard_map/ppermute | solution.py:547
  8.8 0.0 collective-permute-done.2.refs_2_
  8.8 1.5 %produce.1 = (f32[144,128]{1,0:T(8,128)S(1)}, f32[144,128]{1,0:T(8,128)S(1)}, f32[144,128]{1,0:T(8,128)S(1)}, f32[144,128]{1,0:T(8,128)S(1)}) custom-call(s32[8,128]{1,0:T(8,128)S(1)} %collective-permute-done.refs_0_, s32[8,128]{1,0:T(8,128)S(1)} %collective-permute-done.1.refs_1_, s32[8,128]{1,0:T(8,128)S(1)} %collective-permute-done.2.refs_2_, ...), custom_call_target="tpu_custom_call" | custom-call | tf_op jit(solution)/shard_map/produce/pallas_call | solution.py:581
  10.3 2.5 %collective-permute-start.3 = (f32[144,128]{1,0:T(8,128)S(1)}, f32[144,128]{1,0:T(8,128)S(1)}, u32[]{:S(2)}, u32[]{:S(2)}) collective-permute-start(f32[144,128]{1,0:T(8,128)S(1)} %get-tuple-element.31), channel_id=1, source_target_pairs={{0,6},{2,4},{4,2},{6,0},{1,7},{3,5},{5,3},{7,1},{8,14},{10,12},{12... | collective-permute-start | bytes 221192 | tf_op jit(solution)/shard_map/ppermute | solution.py:591
  12.8 0.5 %collective-permute-start.4 = (f32[144,128]{1,0:T(8,128)S(1)}, f32[144,128]{1,0:T(8,128)S(1)}, u32[]{:S(2)}, u32[]{:S(2)}) collective-permute-start(f32[144,128]{1,0:T(8,128)S(1)} %get-tuple-element.32), channel_id=1, source_target_pairs={{0,4},{2,6},{4,0},{6,2},{1,5},{3,7},{5,1},{7,3},{8,12},{10,14},{12... | collective-permute-start | bytes 221192 | tf_op jit(solution)/shard_map/ppermute | solution.py:591
  13.4 0.6 %collective-permute-start.5 = (f32[144,128]{1,0:T(8,128)S(1)}, f32[144,128]{1,0:T(8,128)S(1)}, u32[]{:S(2)}, u32[]{:S(2)}) collective-permute-start(f32[144,128]{1,0:T(8,128)S(1)} %get-tuple-element.33), channel_id=1, source_target_pairs={{0,2},{2,0},{4,6},{6,4},{1,3},{3,1},{5,7},{7,5},{8,10},{10,8},{12,... | collective-permute-start | bytes 221192 | tf_op jit(solution)/shard_map/ppermute | solution.py:591
  13.9 2.5 %collective-permute-done.3.refs_1_ = f32[144,128]{1,0:T(8,128)S(1)} collective-permute-done((f32[144,128]{1,0:T(8,128)S(1)}, f32[144,128]{1,0:T(8,128)S(1)}, u32[]{:S(2)}, u32[]{:S(2)}) %collective-permute-start.3) | collective-permute-done | bytes 73760 | tf_op jit(solution)/shard_map/ppermute | solution.py:591
  16.4 1.5 %collective-permute-done.4.refs_2_ = f32[144,128]{1,0:T(8,128)S(1)} collective-permute-done((f32[144,128]{1,0:T(8,128)S(1)}, f32[144,128]{1,0:T(8,128)S(1)}, u32[]{:S(2)}, u32[]{:S(2)}) %collective-permute-start.4) | collective-permute-done | bytes 73760 | tf_op jit(solution)/shard_map/ppermute | solution.py:591
  18.0 0.1 collective-permute-done.5.refs_3_
  18.1 2.5 %collective-permute-start.8 = (f32[64,128]{1,0:T(8,128)S(1)}, f32[64,128]{1,0:T(8,128)S(1)}, u32[]{:S(2)}, u32[]{:S(2)}) collective-permute-start(f32[64,128]{1,0:T(8,128)S(1)} %get-tuple-element.37), channel_id=1, source_target_pairs={{0,25},{1,24},{8,17},{9,16},{16,9},{17,8},{24,1},{25,0},{2,27},{3,... | collective-permute-start | bytes 98312 | tf_op jit(solution)/shard_map/ppermute | solution.py:604
  20.6 0.1 collective-permute-start.6
  20.7 1.2 %collective-permute-start.7 = (f32[64,128]{1,0:T(8,128)S(1)}, f32[64,128]{1,0:T(8,128)S(1)}, u32[]{:S(2)}, u32[]{:S(2)}) collective-permute-start(f32[64,128]{1,0:T(8,128)S(1)} %get-tuple-element.36), channel_id=1, source_target_pairs={{0,17},{1,16},{8,25},{9,24},{16,1},{17,0},{24,9},{25,8},{2,19},{3,... | collective-permute-start | bytes 98312 | tf_op jit(solution)/shard_map/ppermute | solution.py:604
  21.9 1.5 %collective-permute-done.8.section.refs_2_ = f32[64,128]{1,0:T(8,128)S(1)} collective-permute-done((f32[64,128]{1,0:T(8,128)S(1)}, f32[64,128]{1,0:T(8,128)S(1)}, u32[]{:S(2)}, u32[]{:S(2)}) %collective-permute-start.8) | collective-permute-done | bytes 32800 | tf_op jit(solution)/shard_map/ppermute | solution.py:604
  23.4 0.3 %place.2 = (bf16[96,1664]{1,0:T(8,128)(2,1)S(1)}, bf16[96,1664]{1,0:T(8,128)(2,1)S(1)}, f32[384,128]{1,0:T(8,128)S(1)}) custom-call(f32[64,128]{1,0:T(8,128)S(1)} %collective-permute-done.8.section.refs_2_, s32[8,128]{1,0:T(8,128)S(1)} %get-tuple-element.38.slots.refs_3_), custom_call_target="tpu_custom_call" | custom-call | tf_op jit(solution)/shard_map/place/pallas_call | solution.py:614
  23.7 0.4 %collective-permute-done.6.section.refs_0_ = f32[64,128]{1,0:T(8,128)S(1)} collective-permute-done((f32[64,128]{1,0:T(8,128)S(1)}, f32[64,128]{1,0:T(8,128)S(1)}, u32[]{:S(2)}, u32[]{:S(2)}) %collective-permute-start.6) | collective-permute-done | bytes 32800 | tf_op jit(solution)/shard_map/ppermute | solution.py:604
  24.1 0.3 %place.3 = (bf16[96,1664]{1,0:T(8,128)(2,1)S(1)}, bf16[96,1664]{1,0:T(8,128)(2,1)S(1)}, f32[384,128]{1,0:T(8,128)S(1)}) custom-call(f32[64,128]{1,0:T(8,128)S(1)} %collective-permute-done.6.section.refs_0_, s32[8,128]{1,0:T(8,128)S(1)} %get-tuple-element.38.slots.refs_3_, ...), custom_call_target="tpu_custom_call", output_to_operand_aliasing={{0}: (2, {}), {1}: (3, {}), {2}: (4, {})} | custom-call | tf_op jit(solution)/shard_map/place/pallas_call | solution.py:614
  24.4 0.7 %collective-permute-done.7.refs_1_ = f32[64,128]{1,0:T(8,128)S(1)} collective-permute-done((f32[64,128]{1,0:T(8,128)S(1)}, f32[64,128]{1,0:T(8,128)S(1)}, u32[]{:S(2)}, u32[]{:S(2)}) %collective-permute-start.7) | collective-permute-done | bytes 32800 | tf_op jit(solution)/shard_map/ppermute | solution.py:604
  25.0 1.2 %finish.1 = f32[768,128]{1,0:T(8,128)} custom-call(f32[64,128]{1,0:T(8,128)S(1)} %collective-permute-done.6.section.refs_0_, f32[64,128]{1,0:T(8,128)S(1)} %collective-permute-done.7.refs_1_, f32[64,128]{1,0:T(8,128)S(1)} %collective-permute-done.8.section.refs_2_, s32[8,128]{1,0:T(8,128)S(1)} %get-tuple-element.38.slots.refs_3_, ...), custom_call_target="tpu_custom_call" | custom-call | tf_op jit(solution)/shard_map/finish/pallas_call | solution.py:623
  (1 shorter events, 0.0 us)
Async XLA Ops:
  1.2 5.7 %collective-permute-start = (s32[8,128]{1,0:T(8,128)S(1)}, s32[8,128]{1,0:T(8,128)S(1)}, u32[]{:S(2)}, u32[]{:S(2)}) collective-permute-start(s32[8,128]{1,0:T(8,128)S(1)} %get-tuple-element.25), channel_id=1, source_target_pairs={{0,8},{1,25},{8,0},{9,17},{16,24},{17,9},{24,16},{25,1},{2,10},{3,... | collective-permute-start | bytes 12296 | tf_op jit(solution)/shard_map/ppermute | solution.py:546
  4.3 4.5 %collective-permute-start.1 = (s32[8,128]{1,0:T(8,128)S(1)}, s32[8,128]{1,0:T(8,128)S(1)}, u32[]{:S(2)}, u32[]{:S(2)}) collective-permute-start(s32[8,128]{1,0:T(8,128)S(1)} %get-tuple-element.26), channel_id=1, source_target_pairs={{0,16},{1,17},{8,24},{9,25},{16,0},{17,1},{24,8},{25,9},{2,18},{3,... | collective-permute-start | bytes 12296 | tf_op jit(solution)/shard_map/ppermute | solution.py:547
  6.9 1.9 %collective-permute-start.2 = (s32[8,128]{1,0:T(8,128)S(1)}, s32[8,128]{1,0:T(8,128)S(1)}, u32[]{:S(2)}, u32[]{:S(2)}) collective-permute-start(s32[8,128]{1,0:T(8,128)S(1)} %collective-permute-done.refs_0_), channel_id=1, source_target_pairs={{0,1},{1,0},{2,3},{3,2},{4,5},{5,4},{6,7},{7,6},{8,9},{9,8},{10,11... | collective-permute-start | bytes 12296 | tf_op jit(solution)/shard_map/ppermute | solution.py:548
  10.3 6.1 %collective-permute-start.3 = (f32[144,128]{1,0:T(8,128)S(1)}, f32[144,128]{1,0:T(8,128)S(1)}, u32[]{:S(2)}, u32[]{:S(2)}) collective-permute-start(f32[144,128]{1,0:T(8,128)S(1)} %get-tuple-element.31), channel_id=1, source_target_pairs={{0,6},{2,4},{4,2},{6,0},{1,7},{3,5},{5,3},{7,1},{8,14},{10,12},{12... | collective-permute-start | bytes 221192 | tf_op jit(solution)/shard_map/ppermute | solution.py:591
  12.8 5.1 %collective-permute-start.4 = (f32[144,128]{1,0:T(8,128)S(1)}, f32[144,128]{1,0:T(8,128)S(1)}, u32[]{:S(2)}, u32[]{:S(2)}) collective-permute-start(f32[144,128]{1,0:T(8,128)S(1)} %get-tuple-element.32), channel_id=1, source_target_pairs={{0,4},{2,6},{4,0},{6,2},{1,5},{3,7},{5,1},{7,3},{8,12},{10,14},{12... | collective-permute-start | bytes 221192 | tf_op jit(solution)/shard_map/ppermute | solution.py:591
  13.4 4.7 %collective-permute-start.5 = (f32[144,128]{1,0:T(8,128)S(1)}, f32[144,128]{1,0:T(8,128)S(1)}, u32[]{:S(2)}, u32[]{:S(2)}) collective-permute-start(f32[144,128]{1,0:T(8,128)S(1)} %get-tuple-element.33), channel_id=1, source_target_pairs={{0,2},{2,0},{4,6},{6,4},{1,3},{3,1},{5,7},{7,5},{8,10},{10,8},{12,... | collective-permute-start | bytes 221192 | tf_op jit(solution)/shard_map/ppermute | solution.py:591
  18.1 5.3 %collective-permute-start.8 = (f32[64,128]{1,0:T(8,128)S(1)}, f32[64,128]{1,0:T(8,128)S(1)}, u32[]{:S(2)}, u32[]{:S(2)}) collective-permute-start(f32[64,128]{1,0:T(8,128)S(1)} %get-tuple-element.37), channel_id=1, source_target_pairs={{0,25},{1,24},{8,17},{9,16},{16,9},{17,8},{24,1},{25,0},{2,27},{3,... | collective-permute-start | bytes 98312 | tf_op jit(solution)/shard_map/ppermute | solution.py:604
  20.6 3.5 %collective-permute-start.6 = (f32[64,128]{1,0:T(8,128)S(1)}, f32[64,128]{1,0:T(8,128)S(1)}, u32[]{:S(2)}, u32[]{:S(2)}) collective-permute-start(f32[64,128]{1,0:T(8,128)S(1)} %get-tuple-element.35), channel_id=1, source_target_pairs={{0,9},{1,8},{8,1},{9,0},{16,25},{17,24},{24,17},{25,16},{2,11},{3,... | collective-permute-start | bytes 98312 | tf_op jit(solution)/shard_map/ppermute | solution.py:604
  20.7 4.3 %collective-permute-start.7 = (f32[64,128]{1,0:T(8,128)S(1)}, f32[64,128]{1,0:T(8,128)S(1)}, u32[]{:S(2)}, u32[]{:S(2)}) collective-permute-start(f32[64,128]{1,0:T(8,128)S(1)} %get-tuple-element.36), channel_id=1, source_target_pairs={{0,17},{1,16},{8,25},{9,24},{16,1},{17,0},{24,9},{25,8},{2,19},{3,... | collective-permute-start | bytes 98312 | tf_op jit(solution)/shard_map/ppermute | solution.py:604

commit v7 on v6

--- a/solution.py
+++ b/solution.py
@@ -15,7 +15,6 @@
 SECTION_ORDER = (2, 0, 1)
 HELD_ROWS = 16
 ROUNDS = 3
-TOGETHER = 4
 DIGIT_BITS = 3
 VMEM = pltpu.VMEM
 SMEM = pltpu.SMEM
@@ -84,7 +83,9 @@
     return results, places
 
 
-def list_kernel(groups, owner_any, cell_any, first, second, slot_ref, owner_ref, cell_ref, sems):
+def list_kernel(groups, *refs):
+    owner_any, cell_any, state_any, terrain_any, first, second, slot_ref, state, terrain = refs[:9]
+    owner_ref, cell_ref, sems = refs[9:]
     copies = [
         pltpu.make_async_copy(source, target, sems.at[index])
         for index, (source, target) in enumerate(((owner_any, owner_ref), (cell_any, cell_ref)))
@@ -92,6 +93,14 @@
     for copy in copies:
         copy.start()
     tile, side = lax.axis_index("grid"), lax.axis_index("side")
+    state_copy = pltpu.make_async_copy(state_any, state, sems.at[2])
+    terrain_copy = pltpu.make_async_copy(terrain_any, terrain, sems.at[3])
+
+    @pl.when(side == 0)
+    def _():
+        terrain_copy.start()
+        state_copy.start()
+
     for copy in copies:
         copy.wait()
     owners = owner_ref[...]
@@ -102,10 +111,15 @@
     for number, (hit, rank) in enumerate(zip(hits, ranks)):
         slots = jnp.where(hit, number * half * LANES + rank, slots)
     slot_ref[...] = slots
-    for target, here, there in ((first, 0, 2), (second, 1, 1)):
+    for target, here, there in ((first, 0, 1), (second, 2, 2)):
         target[...] = jnp.zeros(target.shape, jnp.int32)
         for line in range(half):
             target[line : line + 1, :] = jnp.where(side == 0, pages[here][line], pages[there][line])
+
+    @pl.when(side == 0)
+    def _():
+        terrain_copy.wait()
+        state_copy.wait()
 
 
 def fold(values, least):
@@ -152,33 +166,21 @@
                 scratch[row : row + levels, :] = placed
 
 
-def block_rows(lev_dev, fields, tiles, own, group, state, terrain, weight, scratch, mass):
+def block_rows(lev_dev, fields, tiles, group, state, terrain, weight, table, mass):
     levels = SUBLANES
-    coarse = weight.shape[1]
+    blocks, coarse, _ = weight.shape
     per = LANES // coarse
-    quarters = tiles // 2 // per
-
-    def some_tiles(index, carry):
-        number, quarter = index // (quarters // TOGETHER), index % (quarters // TOGETHER) * TOGETHER
-
-        @pl.when(own[number, quarter * per] >= 0)
-        def _():
-            for more in range(TOGETHER):
-                fill_tile(number * quarters + quarter + more, number, quarter + more)
-
-        return carry
-
-    def fill_tile(index, number, quarter):
+    for index in range(blocks // per):
         lefts, rights = [], []
         for place in range(per):
-            name = own[number, quarter * per + place]
-            block = jnp.maximum(name, 0)
-            source = terrain[pl.ds(pl.multiple_of(block * levels, levels), levels), :]
+            block = index * per + place
+            source = terrain[block * levels : (block + 1) * levels, :]
             parts = []
             for field in range(fields):
                 placed = jnp.zeros((levels, LANES), jnp.float32)
                 for level in range(lev_dev):
-                    line = state[pl.ds((field * tiles + block) * lev_dev + level, 1), :]
+                    row = (field * tiles + block) * lev_dev + level
+                    line = state[row : row + 1, :]
                     placed = jnp.where(source == group * lev_dev + level, line, placed)
                 parts.append(placed)
             moved = jnp.concatenate(parts, axis=0)
@@ -189,7 +191,7 @@
                     [moved_high, moved_low, jnp.ones((2 * SUBLANES, LANES), jnp.bfloat16)], axis=0
                 )
             )
-            dense = jnp.where(name >= 0, weight[block], 0.0)
+            dense = weight[block]
             dense_high = dense.astype(jnp.bfloat16)
             dense_low = (dense - dense_high.astype(jnp.float32)).astype(jnp.bfloat16)
             blank = jnp.zeros((coarse, LANES), jnp.bfloat16)
@@ -210,81 +212,66 @@
         rows = fields * levels
         result = product[:rows] + product[rows : 2 * rows]
         for field in range(fields):
-            row = ((number * fields + field) * quarters + quarter) * levels
-            scratch[pl.ds(pl.multiple_of(row, levels), levels), :] = result[
-                field * levels : (field + 1) * levels
-            ]
-        mass[pl.ds(index, 1), :] = product[2 * rows : 2 * rows + 1]
-
-    lax.fori_loop(0, ROUNDS * quarters // TOGETHER, some_tiles, 0)
-
-
-def prepare_kernel(lev_dev, fields, groups, block_owner, block_row, *refs):
+            row = (field * (blocks // per) + index) * levels
+            table[row : row + levels, :] = result[field * levels : (field + 1) * levels]
+        mass[index : index + 1, :] = product[2 * rows : 2 * rows + 1]
+
+
+def prepare_kernel(lev_dev, fields, groups, terrain_0, block_owner, block_row, *refs):
     sources, (state, packed, table, facts) = refs[:3], refs[3:7]
-    terrain, weight, own, owners, rows, sems = refs[7:]
-    state_copy, terrain_copy, weight_copy = [
-        pltpu.make_async_copy(source, target, sems.at[index])
+    terrain, weight, owners, rows, sems = refs[7:]
+    copies = [
+        pltpu.make_async_copy(source, target, sems.at[2 + index])
         for index, (source, target) in enumerate(zip(sources, (state, terrain, weight)))
     ]
-    owner_copy = pltpu.make_async_copy(block_owner, owners, sems.at[3])
-    row_copy = pltpu.make_async_copy(block_row, rows, sems.at[4])
+    owner_copy = pltpu.make_async_copy(block_owner, owners, sems.at[0])
+    row_copy = pltpu.make_async_copy(block_row, rows, sems.at[1])
     tile, side, group = lax.axis_index("grid"), lax.axis_index("side"), lax.axis_index("lev")
     tiles = packed.shape[0]
-    terrain_copy.start()
-    state_copy.start()
 
     @pl.when(side == 0)
     def _():
         levels = SUBLANES
         bits = (levels - 1).bit_length()
-        terrain_copy.wait()
         total = jnp.zeros((tiles, LANES), jnp.int32)
         for level in range(levels):
-            total = total | (terrain[pl.ds(level, tiles, stride=levels), :] << (bits * level))
+            total = total | (terrain_0[pl.ds(level, tiles, stride=levels), :] << (bits * level))
         packed[...] = total
-        state_copy.wait()
 
     @pl.when(side == 1)
     def _():
-        weight_copy.start()
+        for copy in copies:
+            copy.start()
         owner_copy.start()
         row_copy.start()
         blocks = owners.shape[1]
-        count = facts.shape[0] - SUBLANES
         lane = iota((1, LANES), 1)
         partners = [partner_of(tile, number, groups) for number in range(ROUNDS)]
 
-        def clear(place, carry):
-            for number in range(ROUNDS):
-                own[number, place] = -1
-            return carry
-
         def enter(block, carry):
-            counts, runs = list(carry[:ROUNDS]), list(carry[ROUNDS:])
-            owner, row = owners[0, block], rows[0, block]
+            counts, names, runs = [list(carry[at : at + ROUNDS]) for at in range(0, 3 * ROUNDS, ROUNDS)]
+            owner, run = owners[0, block], rows[0, block].astype(jnp.float32)
+            name = block.astype(jnp.float32)
             for number in range(ROUNDS):
                 mine = owner == partners[number]
-                own[number, counts[number]] = jnp.where(mine, block, -1)
-                runs[number] = jnp.where(
-                    (lane == counts[number]) & mine, row.astype(jnp.float32), runs[number]
-                )
+                here = (lane == counts[number]) & mine
+                names[number] = jnp.where(here, name, names[number])
+                runs[number] = jnp.where(here, run, runs[number])
                 counts[number] = counts[number] + mine.astype(jnp.int32)
-            return (*counts, *runs)
-
-        lax.fori_loop(0, blocks // 2 + 1, clear, 0, unroll=True)
+            return (*counts, *names, *runs)
+
         owner_copy.wait()
         row_copy.wait()
         empty = jnp.full((1, LANES), -1.0, jnp.float32)
         carry = lax.fori_loop(
-            0, blocks, enter, (jnp.int32(0),) * ROUNDS + (empty,) * ROUNDS, unroll=True
+            0, blocks, enter, (jnp.int32(0),) * ROUNDS + (empty,) * (2 * ROUNDS), unroll=True
         )
-        facts[count:, :] = jnp.zeros((SUBLANES, LANES), jnp.float32)
-        for number in range(ROUNDS):
-            facts[count + number : count + number + 1, :] = carry[ROUNDS + number]
-        terrain_copy.wait()
-        state_copy.wait()
-        weight_copy.wait()
-        block_rows(lev_dev, fields, tiles, own, group, state, terrain, weight, table, facts)
+        facts[SUBLANES:, :] = jnp.zeros((SUBLANES, LANES), jnp.float32)
+        for number in range(2 * ROUNDS):
+            facts[SUBLANES + number : SUBLANES + number + 1, :] = carry[ROUNDS + number]
+        for copy in copies:
+            copy.wait()
+        block_rows(lev_dev, fields, tiles, group, state, terrain, weight, table, facts)
 
 
 def produce_kernel(lev_dev, fields, partners, groups, *refs):
@@ -295,10 +282,11 @@
 
     def emit(source):
         rows = source.shape[0] // SUBLANES
+        span = parts[0].shape[0] // lev_dev
         for distance in range(partners):
             target = group ^ distance
             for level in range(lev_dev):
-                parts[distance][level * rows : (level + 1) * rows, :] = source[
+                parts[distance][level * span : level * span + rows, :] = source[
                     pl.ds(target * lev_dev + level, rows, stride=SUBLANES), :
                 ]
 
@@ -312,7 +300,7 @@
         emit(table)
 
 
-def sum_kernel(lev_dev, fields, partners, *refs):
+def sum_kernel(lev_dev, fields, coarse, partners, *refs):
     parts, facts, sections = refs[:partners], refs[partners], refs[partners + 1 :]
     total = parts[0][...]
     for part in parts[1:]:
@@ -320,15 +308,43 @@
     rows = total.shape[0] // lev_dev
     span = rows // ROUNDS
     quarters = span // fields
-    masses = facts.shape[0] - SUBLANES
-    for number, section in enumerate(sections):
-        for level in range(lev_dev):
-            start = level * rows + number * span
-            section[level * span : (level + 1) * span, :] = total[start : start + span]
-        last = lev_dev * span + quarters
-        section[last - quarters : last, :] = facts[number * quarters : (number + 1) * quarters, :]
-        section[last:, :] = jnp.zeros((section.shape[0] - last, LANES), jnp.float32)
-        section[last : last + 1, :] = facts[masses + number : masses + number + 1, :]
+    side = lax.axis_index("side")
+    kinds = lev_dev * fields + 1
+
+    @pl.when(side == 0)
+    def _():
+        for number, section in enumerate(sections):
+            for level in range(lev_dev):
+                start = level * rows + number * span
+                section[level * span : (level + 1) * span, :] = total[start : start + span]
+            rest = section.shape[0] - lev_dev * span
+            section[lev_dev * span :, :] = jnp.zeros((rest, LANES), jnp.float32)
+
+    @pl.when(side == 1)
+    def _():
+        shape = (SUBLANES, LANES)
+        lane, sub = iota(shape, 1), iota(shape, 0)
+        per = LANES // coarse
+        sources = [
+            total[level * rows + field * SUBLANES : level * rows + (field + 1) * SUBLANES]
+            for level in range(lev_dev)
+            for field in range(fields)
+        ] + [facts[0:SUBLANES, :]]
+        for number, section in enumerate(sections):
+            names = facts[SUBLANES + number : SUBLANES + number + 1, :].astype(jnp.int32)
+            names = jnp.broadcast_to(names, shape)
+            for quarter in range(quarters):
+                name = gather_lanes(names, quarter * per + lane // coarse)
+                low = (name & (per - 1)) * coarse + lane % coarse
+                here = (sub == name // per) & (name >= 0)
+                for kind, source in enumerate(sources):
+                    got = jnp.where(here, gather_lanes(source, low), 0.0)
+                    row = kind * quarters + quarter
+                    section[row : row + 1, :] = jnp.sum(got, axis=0, keepdims=True)
+            last = kinds * quarters
+            section[last:, :] = jnp.zeros((section.shape[0] - last, LANES), jnp.float32)
+            run = SUBLANES + ROUNDS + number
+            section[last : last + 1, :] = facts[run : run + 1, :]
 
 
 def place_panel(lev_dev, fields, number, fresh, section, slots, found):
@@ -449,8 +465,8 @@
 
 
 def finish_kernel(lev_dev, fields, coarse, groups, number, *refs):
-    sections, slots, kept, state = refs[:3], refs[3], refs[4:7], refs[7]
-    out, spread_high, spread_low, found, staged, sems = refs[8:]
+    sections, slots, kept, state, state_1 = refs[:3], refs[3], refs[4:7], refs[7], refs[8]
+    out, spread_high, spread_low, found, staged, sems = refs[9:]
     quarters = slots.shape[0] // 2
     tiles = state.shape[0] // (fields * lev_dev)
     rows = tiles * lev_dev
@@ -480,7 +496,7 @@
     def _():
         found[...] = kept[2][...]
         place_panel(lev_dev, fields, answer_round(number, groups), False, sections[number], slots, found)
-        finish_panel(lev_dev, fields, tiles, slots.shape[0], found, state, staged, send)
+        finish_panel(lev_dev, fields, tiles, slots.shape[0], found, state_1, staged, send)
 
     for copy in copies:
         copy.wait()
@@ -522,19 +538,24 @@
         terrain_level.reshape(levels, tiles, LANES).transpose(1, 0, 2).reshape(tiles * levels, LANES)
     )
     page = struct((panel_tiles, LANES), jnp.int32)
-    first, second, slots = pl.pallas_call(
+    sources = [in_hbm(state), in_hbm(terrain), in_hbm(block_weight)]
+    first, second, slots, state_0, terrain_0 = pl.pallas_call(
         functools.partial(list_kernel, groups),
-        out_shape=[page] * 3,
-        in_specs=specs(*[pl.ANY] * 2),
-        out_specs=specs(*[VMEM] * 3),
+        out_shape=[page] * 3 + [struct(state.shape), struct(terrain.shape, jnp.int32)],
+        in_specs=specs(*[pl.ANY] * 4),
+        out_specs=specs(*[VMEM] * 5),
         scratch_shapes=[
             VMEM(page.shape, jnp.int32),
             VMEM(page.shape, jnp.int32),
-            pltpu.SemaphoreType.DMA((2,)),
+            pltpu.SemaphoreType.DMA((4,)),
         ],
         compiler_params=params(),
         name="lists",
-    )(in_hbm(panel_owner.reshape(page.shape)), in_hbm(panel_cell.reshape(page.shape)))
+    )(
+        in_hbm(panel_owner.reshape(page.shape)),
+        in_hbm(panel_cell.reshape(page.shape)),
+        *sources[:2],
+    )
 
     def towards(number_of, cross):
         return [
@@ -543,26 +564,25 @@
             for side in range(sides)
         ]
 
-    first = lax.ppermute(first, ("grid", "side"), towards(lambda side: 2 * side, 0))
-    second = lax.ppermute(second, ("grid", "side"), towards(lambda side: 1, 0))
+    first = lax.ppermute(first, ("grid", "side"), towards(lambda side: side, 0))
+    second = lax.ppermute(second, ("grid", "side"), towards(lambda side: 2, 1))
     third = lax.ppermute(first, "side", [(0, 1), (1, 0)])
-    lists = [first, second, third]
+    lists = [first, third, second]
     scratch_rows = ROUNDS * fields * quarters
     table_shape = (scratch_rows * SUBLANES, LANES)
-    state, packed, table, facts = pl.pallas_call(
+    state_1, packed, table, facts = pl.pallas_call(
         functools.partial(prepare_kernel, lev_dev, fields, groups),
         out_shape=[
             struct(state.shape),
             struct((tiles, LANES), jnp.int32),
-            struct(table_shape),
-            struct((ROUNDS * quarters + SUBLANES, LANES)),
+            struct((fields * blocks * coarse // LANES * levels, LANES)),
+            struct((2 * SUBLANES, LANES)),
         ],
-        in_specs=specs(*[pl.ANY] * 5),
+        in_specs=specs(VMEM, *[pl.ANY] * 5),
         out_specs=specs(*[VMEM] * 4),
         scratch_shapes=[
             VMEM(terrain.shape, jnp.int32),
             VMEM(block_weight.shape, jnp.float32),
-            SMEM((ROUNDS, LANES), jnp.int32),
             SMEM((1, blocks), jnp.int32),
             SMEM((1, blocks), jnp.int32),
             pltpu.SemaphoreType.DMA((5,)),
@@ -571,11 +591,10 @@
         compiler_params=params(),
         name="prepare",
     )(
+        terrain_0,
         in_hbm(block_owner.reshape(1, blocks)),
         in_hbm(block_row.reshape(1, blocks)),
-        in_hbm(state),
-        in_hbm(terrain),
-        in_hbm(block_weight),
+        *sources,
     )
     part = struct((lev_dev * scratch_rows, LANES))
     parts = pl.pallas_call(
@@ -586,14 +605,14 @@
         scratch_shapes=[VMEM(table_shape, jnp.float32)],
         compiler_params=params(),
         name="produce",
-    )(*lists, state, packed, table)
+    )(*lists, state_0, packed, table)
     arrived = [parts[0]] + [
         lax.ppermute(parts[distance], "lev", [(rank, rank ^ distance) for rank in range(partners)])
         for distance in range(partners - 1, 0, -1)
     ]
     section_rows = HELD_ROWS * quarters
     sections = pl.pallas_call(
-        functools.partial(sum_kernel, lev_dev, fields, partners),
+        functools.partial(sum_kernel, lev_dev, fields, coarse, partners),
         out_shape=[struct((section_rows, LANES))] * 3,
         in_specs=specs(*[VMEM] * (partners + 1)),
         out_specs=specs(*[VMEM] * 3),
@@ -623,13 +642,13 @@
     result = pl.pallas_call(
         functools.partial(finish_kernel, *sizes, SECTION_ORDER[-1]),
         out_shape=pltpu.HBM(state.shape, jnp.float32),
-        in_specs=specs(*[VMEM] * 8),
+        in_specs=specs(*[VMEM] * 9),
         out_specs=pl.BlockSpec(memory_space=pltpu.HBM),
         scratch_shapes=[VMEM(one.shape, one.dtype) for one in kept]
         + [VMEM(state.shape, jnp.float32), pltpu.SemaphoreType.DMA((fields,))],
         compiler_params=params(),
         name="finish",
-    )(*sections, slots, *held, state)
+    )(*sections, slots, *held, state_0, state_1)
     return (
         result.reshape(fields, tiles, lev_dev, LANES)
         .transpose(2, 0, 1, 3)

time: 26.4 us -> 25.6 us (0.970)
  Pallas kernels: 5.63 us -> 4.62 us
  starting transfers between devices: 13.1 us -> 12.1 us
  waiting for transfers between devices: 7.49 us -> 8.48 us
    ppermute x2, waiting for transfers between devices: 0.78 us -> 2.18 us  [the longest x1 2.13 us: on_device(): second = lax.ppermute(second, ('grid', 'side'), towards(lambda side: 2, 1))]
    ppermute x2, starting transfers between devices: 5.68 us -> 4.63 us  [the longest x1 3.09 us: on_device(): first = lax.ppermute(first, ('grid', 'side'), towards(lambda side: side, 0))]
    pallas_call x1, Pallas kernels: 1.12 us -> 0.1 us  [on_device(): pl.pallas_call(functools.partial(prepare_kernel, lev_dev, fields, groups)...]
    ppermute x1, starting transfers between devices: 0.01 us -> 1.01 us  [on_device(): third = lax.ppermute(first, 'side', [(0, 1), (1, 0)])]
    ppermute x3, starting transfers between devices: 3.81 us -> 2.9 us  [on_device(): lax.ppermute(sections[number], ('grid', 'side'), towards(lambda side: num...]
    ppermute x3, waiting for transfers between devices: 4.14 us -> 3.82 us  [on_device(): lax.ppermute(parts[distance], 'lev', [(rank, rank ^ distance) for rank in...]
  transfers between devices with their start and end apart: 9 -> 9, of which waited for: 7 -> 6; matrix products, arithmetic and copies ran while one was open for 0% -> 0% of each run, Pallas kernels for 6% -> 3%
where the time goes in v7:
time: 25.6 us; the launch traced here: 25.3 us
  starting transfers between devices  12.1 us (47%)
  waiting for transfers between devices  8.48 us (33%)
  Pallas kernels  4.62 us (18%)
    ppermute x3, waiting for transfers between devices, on_device(): lax.ppermute(parts[distance], 'lev', [(rank, rank ^ distance) for rank in...  3.82 us
    ppermute x3, starting transfers between devices, on_device(): lax.ppermute(parts[distance], 'lev', [(rank, rank ^ distance) for rank in...  3.55 us
    ppermute x1, starting transfers between devices, on_device(): first = lax.ppermute(first, ('grid', 'side'), towards(lambda side: side, 0))  3.09 us
    ppermute x3, starting transfers between devices, on_device(): lax.ppermute(sections[number], ('grid', 'side'), towards(lambda side: num...  2.9 us
    ppermute x3, waiting for transfers between devices, on_device(): lax.ppermute(sections[number], ('grid', 'side'), towards(lambda side: num...  2.48 us
    ppermute x1, waiting for transfers between devices, on_device(): second = lax.ppermute(second, ('grid', 'side'), towards(lambda side: 2, 1))  2.13 us
    ppermute x1, starting transfers between devices, on_device(): second = lax.ppermute(second, ('grid', 'side'), towards(lambda side: 2, 1))  1.54 us
    pallas_call x1, Pallas kernels, on_device(): pl.pallas_call(functools.partial(produce_kernel, lev_dev, fields, partner...  1.52 us
  transfers between devices with their start and end apart: 9, of which 6 were waited for; matrix products, arithmetic and copies ran while one was open for 0% of the time, Pallas kernels for 3%

profile of v7, /device:TPU:0, one launch (start us, length us, event | category | flops | bytes accessed | tf_op | source)
XLA Modules:
  0.0 25.3 jit_solution(7914004395119935715)
XLA Ops:
  0.0 1.2 %lists.1 = (s32[8,128]{1,0:T(8,128)S(1)}, s32[8,128]{1,0:T(8,128)S(1)}, s32[8,128]{1,0:T(8,128)S(1)}, f32[768,128]{1,0:T(8,128)S(1)}, s32[512,128]{1,0:T(8,128)S(1)}) custom-call(s32[8,128]{1,0:T(8,128)} %bitcast.23, s32[8,128]{1,0:T(8,128)} %bitcast.24, f32[768,128]{1,0:T(8,128)} %bitcast.19, s32[512,128]{1,0:T(8,128)} %bitcast.21), custom_call_target="tpu_custom_call" | custom-call | tf_op jit(solution)/shard_map/lists/pallas_call | solution.py:542
  1.2 3.1 %collective-permute-start = (s32[8,128]{1,0:T(8,128)S(1)}, s32[8,128]{1,0:T(8,128)S(1)}, u32[]{:S(2)}, u32[]{:S(2)}) collective-permute-start(s32[8,128]{1,0:T(8,128)S(1)} %get-tuple-element.27), channel_id=1, source_target_pairs={{0,8},{1,17},{8,0},{9,25},{16,24},{17,1},{24,16},{25,9},{2,10},{3,... | collective-permute-start | bytes 12296 | tf_op jit(solution)/shard_map/ppermute | solution.py:567
  4.3 1.5 %collective-permute-start.2 = (s32[8,128]{1,0:T(8,128)S(1)}, s32[8,128]{1,0:T(8,128)S(1)}, u32[]{:S(2)}, u32[]{:S(2)}) collective-permute-start(s32[8,128]{1,0:T(8,128)S(1)} %get-tuple-element.28), channel_id=1, source_target_pairs={{0,25},{1,24},{8,17},{9,16},{16,9},{17,8},{24,1},{25,0},{2,27},{3,... | collective-permute-start | bytes 12296 | tf_op jit(solution)/shard_map/ppermute | solution.py:568
  5.9 0.0 collective-permute-done.refs_0_
  5.9 1.0 %collective-permute-start.1 = (s32[8,128]{1,0:T(8,128)S(1)}, s32[8,128]{1,0:T(8,128)S(1)}, u32[]{:S(2)}, u32[]{:S(2)}) collective-permute-start(s32[8,128]{1,0:T(8,128)S(1)} %collective-permute-done.refs_0_), channel_id=1, source_target_pairs={{0,1},{1,0},{2,3},{3,2},{4,5},{5,4},{6,7},{7,6},{8,9},{9,8},{10,11... | collective-permute-start | bytes 12296 | tf_op jit(solution)/shard_map/ppermute | solution.py:569
  6.9 0.1 prepare.1
  7.0 2.1 %collective-permute-done.2.refs_2_ = s32[8,128]{1,0:T(8,128)S(1)} collective-permute-done((s32[8,128]{1,0:T(8,128)S(1)}, s32[8,128]{1,0:T(8,128)S(1)}, u32[]{:S(2)}, u32[]{:S(2)}) %collective-permute-start.2) | collective-permute-done | bytes 4128 | tf_op jit(solution)/shard_map/ppermute | solution.py:568
  9.1 0.0 collective-permute-done.1.refs_1_
  9.2 1.5 %produce.1 = (f32[144,128]{1,0:T(8,128)S(1)}, f32[144,128]{1,0:T(8,128)S(1)}, f32[144,128]{1,0:T(8,128)S(1)}, f32[144,128]{1,0:T(8,128)S(1)}) custom-call(s32[8,128]{1,0:T(8,128)S(1)} %collective-permute-done.refs_0_, s32[8,128]{1,0:T(8,128)S(1)} %collective-permute-done.1.refs_1_, s32[8,128]{1,0:T(8,128)S(1)} %collective-permute-done.2.refs_2_, ...), custom_call_target="tpu_custom_call" | custom-call | tf_op jit(solution)/shard_map/produce/pallas_call | solution.py:600
  10.7 2.5 %collective-permute-start.3 = (f32[144,128]{1,0:T(8,128)S(1)}, f32[144,128]{1,0:T(8,128)S(1)}, u32[]{:S(2)}, u32[]{:S(2)}) collective-permute-start(f32[144,128]{1,0:T(8,128)S(1)} %get-tuple-element.34), channel_id=1, source_target_pairs={{0,6},{2,4},{4,2},{6,0},{1,7},{3,5},{5,3},{7,1},{8,14},{10,12},{12... | collective-permute-start | bytes 221192 | tf_op jit(solution)/shard_map/ppermute | solution.py:610
  13.2 0.5 %collective-permute-start.4 = (f32[144,128]{1,0:T(8,128)S(1)}, f32[144,128]{1,0:T(8,128)S(1)}, u32[]{:S(2)}, u32[]{:S(2)}) collective-permute-start(f32[144,128]{1,0:T(8,128)S(1)} %get-tuple-element.35), channel_id=1, source_target_pairs={{0,4},{2,6},{4,0},{6,2},{1,5},{3,7},{5,1},{7,3},{8,12},{10,14},{12... | collective-permute-start | bytes 221192 | tf_op jit(solution)/shard_map/ppermute | solution.py:610
  13.7 0.5 %collective-permute-start.5 = (f32[144,128]{1,0:T(8,128)S(1)}, f32[144,128]{1,0:T(8,128)S(1)}, u32[]{:S(2)}, u32[]{:S(2)}) collective-permute-start(f32[144,128]{1,0:T(8,128)S(1)} %get-tuple-element.36), channel_id=1, source_target_pairs={{0,2},{2,0},{4,6},{6,4},{1,3},{3,1},{5,7},{7,5},{8,10},{10,8},{12,... | collective-permute-start | bytes 221192 | tf_op jit(solution)/shard_map/ppermute | solution.py:610
  14.2 2.1 %collective-permute-done.3.refs_1_ = f32[144,128]{1,0:T(8,128)S(1)} collective-permute-done((f32[144,128]{1,0:T(8,128)S(1)}, f32[144,128]{1,0:T(8,128)S(1)}, u32[]{:S(2)}, u32[]{:S(2)}) %collective-permute-start.3) | collective-permute-done | bytes 73760 | tf_op jit(solution)/shard_map/ppermute | solution.py:610
  16.3 1.3 %collective-permute-done.4.refs_2_ = f32[144,128]{1,0:T(8,128)S(1)} collective-permute-done((f32[144,128]{1,0:T(8,128)S(1)}, f32[144,128]{1,0:T(8,128)S(1)}, u32[]{:S(2)}, u32[]{:S(2)}) %collective-permute-start.4) | collective-permute-done | bytes 73760 | tf_op jit(solution)/shard_map/ppermute | solution.py:610
  17.5 0.5 %collective-permute-done.5.refs_3_ = f32[144,128]{1,0:T(8,128)S(1)} collective-permute-done((f32[144,128]{1,0:T(8,128)S(1)}, f32[144,128]{1,0:T(8,128)S(1)}, u32[]{:S(2)}, u32[]{:S(2)}) %collective-permute-start.5) | collective-permute-done | bytes 73760 | tf_op jit(solution)/shard_map/ppermute | solution.py:610
  18.1 1.7 %collective-permute-start.8 = (f32[64,128]{1,0:T(8,128)S(1)}, f32[64,128]{1,0:T(8,128)S(1)}, u32[]{:S(2)}, u32[]{:S(2)}) collective-permute-start(f32[64,128]{1,0:T(8,128)S(1)} %get-tuple-element.40), channel_id=1, source_target_pairs={{0,25},{1,24},{8,17},{9,16},{16,9},{17,8},{24,1},{25,0},{2,27},{3,... | collective-permute-start | bytes 98312 | tf_op jit(solution)/shard_map/ppermute | solution.py:623
  19.8 0.0 collective-permute-start.6
  19.8 1.2 %collective-permute-start.7 = (f32[64,128]{1,0:T(8,128)S(1)}, f32[64,128]{1,0:T(8,128)S(1)}, u32[]{:S(2)}, u32[]{:S(2)}) collective-permute-start(f32[64,128]{1,0:T(8,128)S(1)} %get-tuple-element.39), channel_id=1, source_target_pairs={{0,17},{1,16},{8,25},{9,24},{16,1},{17,0},{24,9},{25,8},{2,19},{3,... | collective-permute-start | bytes 98312 | tf_op jit(solution)/shard_map/ppermute | solution.py:623
  21.0 2.4 %collective-permute-done.8.section.refs_2_ = f32[64,128]{1,0:T(8,128)S(1)} collective-permute-done((f32[64,128]{1,0:T(8,128)S(1)}, f32[64,128]{1,0:T(8,128)S(1)}, u32[]{:S(2)}, u32[]{:S(2)}) %collective-permute-start.8) | collective-permute-done | bytes 32800 | tf_op jit(solution)/shard_map/ppermute | solution.py:623
  23.4 0.3 %place.2 = (bf16[96,1664]{1,0:T(8,128)(2,1)S(1)}, bf16[96,1664]{1,0:T(8,128)(2,1)S(1)}, f32[384,128]{1,0:T(8,128)S(1)}) custom-call(f32[64,128]{1,0:T(8,128)S(1)} %collective-permute-done.8.section.refs_2_, s32[8,128]{1,0:T(8,128)S(1)} %get-tuple-element.41.slots.refs_3_), custom_call_target="tpu_custom_call" | custom-call | tf_op jit(solution)/shard_map/place/pallas_call | solution.py:633
  23.7 0.0 collective-permute-done.6.section.refs_0_
  23.7 0.3 %place.3 = (bf16[96,1664]{1,0:T(8,128)(2,1)S(1)}, bf16[96,1664]{1,0:T(8,128)(2,1)S(1)}, f32[384,128]{1,0:T(8,128)S(1)}) custom-call(f32[64,128]{1,0:T(8,128)S(1)} %collective-permute-done.6.section.refs_0_, s32[8,128]{1,0:T(8,128)S(1)} %get-tuple-element.41.slots.refs_3_, ...), custom_call_target="tpu_custom_call", output_to_operand_aliasing={{0}: (2, {}), {1}: (3, {}), {2}: (4, {})} | custom-call | tf_op jit(solution)/shard_map/place/pallas_call | solution.py:633
  24.0 0.1 collective-permute-done.7.refs_1_
  24.1 1.2 %finish.1 = f32[768,128]{1,0:T(8,128)} custom-call(f32[64,128]{1,0:T(8,128)S(1)} %collective-permute-done.6.section.refs_0_, f32[64,128]{1,0:T(8,128)S(1)} %collective-permute-done.7.refs_1_, f32[64,128]{1,0:T(8,128)S(1)} %collective-permute-done.8.section.refs_2_, s32[8,128]{1,0:T(8,128)S(1)} %get-tuple-element.41.slots.refs_3_, ...), custom_call_target="tpu_custom_call" | custom-call | tf_op jit(solution)/shard_map/finish/pallas_call | solution.py:642
  (1 shorter events, 0.0 us)
Async XLA Ops:
  1.2 4.7 %collective-permute-start = (s32[8,128]{1,0:T(8,128)S(1)}, s32[8,128]{1,0:T(8,128)S(1)}, u32[]{:S(2)}, u32[]{:S(2)}) collective-permute-start(s32[8,128]{1,0:T(8,128)S(1)} %get-tuple-element.27), channel_id=1, source_target_pairs={{0,8},{1,17},{8,0},{9,25},{16,24},{17,1},{24,16},{25,9},{2,10},{3,... | collective-permute-start | bytes 12296 | tf_op jit(solution)/shard_map/ppermute | solution.py:567
  4.3 4.8 %collective-permute-start.2 = (s32[8,128]{1,0:T(8,128)S(1)}, s32[8,128]{1,0:T(8,128)S(1)}, u32[]{:S(2)}, u32[]{:S(2)}) collective-permute-start(s32[8,128]{1,0:T(8,128)S(1)} %get-tuple-element.28), channel_id=1, source_target_pairs={{0,25},{1,24},{8,17},{9,16},{16,9},{17,8},{24,1},{25,0},{2,27},{3,... | collective-permute-start | bytes 12296 | tf_op jit(solution)/shard_map/ppermute | solution.py:568
  5.9 3.2 %collective-permute-start.1 = (s32[8,128]{1,0:T(8,128)S(1)}, s32[8,128]{1,0:T(8,128)S(1)}, u32[]{:S(2)}, u32[]{:S(2)}) collective-permute-start(s32[8,128]{1,0:T(8,128)S(1)} %collective-permute-done.refs_0_), channel_id=1, source_target_pairs={{0,1},{1,0},{2,3},{3,2},{4,5},{5,4},{6,7},{7,6},{8,9},{9,8},{10,11... | collective-permute-start | bytes 12296 | tf_op jit(solution)/shard_map/ppermute | solution.py:569
  10.7 5.6 %collective-permute-start.3 = (f32[144,128]{1,0:T(8,128)S(1)}, f32[144,128]{1,0:T(8,128)S(1)}, u32[]{:S(2)}, u32[]{:S(2)}) collective-permute-start(f32[144,128]{1,0:T(8,128)S(1)} %get-tuple-element.34), channel_id=1, source_target_pairs={{0,6},{2,4},{4,2},{6,0},{1,7},{3,5},{5,3},{7,1},{8,14},{10,12},{12... | collective-permute-start | bytes 221192 | tf_op jit(solution)/shard_map/ppermute | solution.py:610
  13.2 4.4 %collective-permute-start.4 = (f32[144,128]{1,0:T(8,128)S(1)}, f32[144,128]{1,0:T(8,128)S(1)}, u32[]{:S(2)}, u32[]{:S(2)}) collective-permute-start(f32[144,128]{1,0:T(8,128)S(1)} %get-tuple-element.35), channel_id=1, source_target_pairs={{0,4},{2,6},{4,0},{6,2},{1,5},{3,7},{5,1},{7,3},{8,12},{10,14},{12... | collective-permute-start | bytes 221192 | tf_op jit(solution)/shard_map/ppermute | solution.py:610
  13.7 4.4 %collective-permute-start.5 = (f32[144,128]{1,0:T(8,128)S(1)}, f32[144,128]{1,0:T(8,128)S(1)}, u32[]{:S(2)}, u32[]{:S(2)}) collective-permute-start(f32[144,128]{1,0:T(8,128)S(1)} %get-tuple-element.36), channel_id=1, source_target_pairs={{0,2},{2,0},{4,6},{6,4},{1,3},{3,1},{5,7},{7,5},{8,10},{10,8},{12,... | collective-permute-start | bytes 221192 | tf_op jit(solution)/shard_map/ppermute | solution.py:610
  18.1 5.3 %collective-permute-start.8 = (f32[64,128]{1,0:T(8,128)S(1)}, f32[64,128]{1,0:T(8,128)S(1)}, u32[]{:S(2)}, u32[]{:S(2)}) collective-permute-start(f32[64,128]{1,0:T(8,128)S(1)} %get-tuple-element.40), channel_id=1, source_target_pairs={{0,25},{1,24},{8,17},{9,16},{16,9},{17,8},{24,1},{25,0},{2,27},{3,... | collective-permute-start | bytes 98312 | tf_op jit(solution)/shard_map/ppermute | solution.py:623
  19.8 3.9 %collective-permute-start.6 = (f32[64,128]{1,0:T(8,128)S(1)}, f32[64,128]{1,0:T(8,128)S(1)}, u32[]{:S(2)}, u32[]{:S(2)}) collective-permute-start(f32[64,128]{1,0:T(8,128)S(1)} %get-tuple-element.38), channel_id=1, source_target_pairs={{0,9},{1,8},{8,1},{9,0},{16,25},{17,24},{24,17},{25,16},{2,11},{3,... | collective-permute-start | bytes 98312 | tf_op jit(solution)/shard_map/ppermute | solution.py:623
  19.8 4.2 %collective-permute-start.7 = (f32[64,128]{1,0:T(8,128)S(1)}, f32[64,128]{1,0:T(8,128)S(1)}, u32[]{:S(2)}, u32[]{:S(2)}) collective-permute-start(f32[64,128]{1,0:T(8,128)S(1)} %get-tuple-element.39), channel_id=1, source_target_pairs={{0,17},{1,16},{8,25},{9,24},{16,1},{17,0},{24,9},{25,8},{2,19},{3,... | collective-permute-start | bytes 98312 | tf_op jit(solution)/shard_map/ppermute | solution.py:623

commit v8 on v7

--- a/solution.py
+++ b/solution.py
@@ -28,6 +28,14 @@
 
 def answer_round(number, groups):
     return number if groups == ROUNDS + 1 else (1, 0, 2)[number]
+
+
+def quotient(value, divisor):
+    return value >> (divisor - 1).bit_length()
+
+
+def remainder(value, divisor):
+    return value & (divisor - 1)
 
 
 def iota(shape, dimension):
@@ -96,11 +104,8 @@
     state_copy = pltpu.make_async_copy(state_any, state, sems.at[2])
     terrain_copy = pltpu.make_async_copy(terrain_any, terrain, sems.at[3])
 
-    @pl.when(side == 0)
-    def _():
-        terrain_copy.start()
-        state_copy.start()
-
+    terrain_copy.start()
+    state_copy.start()
     for copy in copies:
         copy.wait()
     owners = owner_ref[...]
@@ -115,11 +120,8 @@
         target[...] = jnp.zeros(target.shape, jnp.int32)
         for line in range(half):
             target[line : line + 1, :] = jnp.where(side == 0, pages[here][line], pages[there][line])
-
-    @pl.when(side == 0)
-    def _():
-        terrain_copy.wait()
-        state_copy.wait()
+    terrain_copy.wait()
+    state_copy.wait()
 
 
 def fold(values, least):
@@ -144,7 +146,7 @@
             sums = [jnp.zeros(shape, jnp.float32) for _ in range(fields)]
             code = jnp.zeros(shape, jnp.int32)
             for chunk in range(tiles // per):
-                here = high == chunk * per + sub // lev_dev
+                here = high == chunk * per + quotient(sub, lev_dev)
                 for field in range(fields):
                     start = field * tiles * lev_dev + chunk * SUBLANES
                     got = gather_lanes(state[start : start + SUBLANES, :], low)
@@ -160,7 +162,7 @@
                 for level in range(lev_dev):
                     one = both
                     for turn in range(1, lev_dev):
-                        one = jnp.where((sub - level) % lev_dev == turn, pltpu.roll(both, turn, 0), one)
+                        one = jnp.where(remainder(sub - level, lev_dev) == turn, pltpu.roll(both, turn, 0), one)
                     placed = jnp.where(source == group * lev_dev + level, one, placed)
                 row = ((section * fields + field) * quarters + quarter) * levels
                 scratch[row : row + levels, :] = placed
@@ -217,13 +219,9 @@
         mass[index : index + 1, :] = product[2 * rows : 2 * rows + 1]
 
 
-def prepare_kernel(lev_dev, fields, groups, terrain_0, block_owner, block_row, *refs):
-    sources, (state, packed, table, facts) = refs[:3], refs[3:7]
-    terrain, weight, owners, rows, sems = refs[7:]
-    copies = [
-        pltpu.make_async_copy(source, target, sems.at[2 + index])
-        for index, (source, target) in enumerate(zip(sources, (state, terrain, weight)))
-    ]
+def prepare_kernel(lev_dev, fields, groups, state, terrain, *refs):
+    block_owner, block_row, weight_any, packed, table, facts, weight, owners, rows, sems = refs
+    weight_copy = pltpu.make_async_copy(weight_any, weight, sems.at[2])
     owner_copy = pltpu.make_async_copy(block_owner, owners, sems.at[0])
     row_copy = pltpu.make_async_copy(block_row, rows, sems.at[1])
     tile, side, group = lax.axis_index("grid"), lax.axis_index("side"), lax.axis_index("lev")
@@ -235,15 +233,14 @@
         bits = (levels - 1).bit_length()
         total = jnp.zeros((tiles, LANES), jnp.int32)
         for level in range(levels):
-            total = total | (terrain_0[pl.ds(level, tiles, stride=levels), :] << (bits * level))
+            total = total | (terrain[pl.ds(level, tiles, stride=levels), :] << (bits * level))
         packed[...] = total
 
     @pl.when(side == 1)
     def _():
-        for copy in copies:
-            copy.start()
         owner_copy.start()
         row_copy.start()
+        weight_copy.start()
         blocks = owners.shape[1]
         lane = iota((1, LANES), 1)
         partners = [partner_of(tile, number, groups) for number in range(ROUNDS)]
@@ -269,8 +266,7 @@
         facts[SUBLANES:, :] = jnp.zeros((SUBLANES, LANES), jnp.float32)
         for number in range(2 * ROUNDS):
             facts[SUBLANES + number : SUBLANES + number + 1, :] = carry[ROUNDS + number]
-        for copy in copies:
-            copy.wait()
+        weight_copy.wait()
         block_rows(lev_dev, fields, tiles, group, state, terrain, weight, table, facts)
 
 
@@ -334,9 +330,9 @@
             names = facts[SUBLANES + number : SUBLANES + number + 1, :].astype(jnp.int32)
             names = jnp.broadcast_to(names, shape)
             for quarter in range(quarters):
-                name = gather_lanes(names, quarter * per + lane // coarse)
-                low = (name & (per - 1)) * coarse + lane % coarse
-                here = (sub == name // per) & (name >= 0)
+                name = gather_lanes(names, quarter * per + quotient(lane, coarse))
+                low = remainder(name, per) * coarse + remainder(lane, coarse)
+                here = sub == quotient(name, per)
                 for kind, source in enumerate(sources):
                     got = jnp.where(here, gather_lanes(source, low), 0.0)
                     row = kind * quarters + quarter
@@ -355,7 +351,7 @@
     chunks = lev_dev * fields * quarters // SUBLANES
     for tile in range(panel_tiles):
         place = jnp.broadcast_to(slots[tile : tile + 1, :], shape)
-        here = place >> LANE_BITS == number * quarters + sub % quarters
+        here = place >> LANE_BITS == number * quarters + remainder(sub, quarters)
         low = place & (LANES - 1)
         for chunk in range(chunks):
             got = gather_lanes(section[chunk * SUBLANES : (chunk + 1) * SUBLANES, :], low)
@@ -424,7 +420,7 @@
                 chunk = (level * fields + field) // share
                 row = (tile * chunks + chunk) * SUBLANES
                 rim = jnp.sum(
-                    jnp.where(sub // quarters == part, found[row : row + SUBLANES, :], 0.0),
+                    jnp.where(quotient(sub, quarters) == part, found[row : row + SUBLANES, :], 0.0),
                     axis=0,
                     keepdims=True,
                 )
@@ -447,7 +443,7 @@
         turned = runs_of(section, quarters, lev_dev * fields + 1)
         if number:
             turned = pltpu.roll(jnp.broadcast_to(turned, (SUBLANES, LANES)), number * width, 1)[0:1]
-        runs = jnp.where(lane // width == number, turned, runs)
+        runs = jnp.where(quotient(lane, width) == number, turned, runs)
     lands = (tile == jnp.broadcast_to(runs >> shift, tile.shape)).astype(jnp.bfloat16)
     lands = lands[:, : ROUNDS * width]
 
@@ -465,8 +461,8 @@
 
 
 def finish_kernel(lev_dev, fields, coarse, groups, number, *refs):
-    sections, slots, kept, state, state_1 = refs[:3], refs[3], refs[4:7], refs[7], refs[8]
-    out, spread_high, spread_low, found, staged, sems = refs[9:]
+    sections, slots, kept, state = refs[:3], refs[3], refs[4:7], refs[7]
+    out, spread_high, spread_low, found, staged, sems = refs[8:]
     quarters = slots.shape[0] // 2
     tiles = state.shape[0] // (fields * lev_dev)
     rows = tiles * lev_dev
@@ -496,7 +492,7 @@
     def _():
         found[...] = kept[2][...]
         place_panel(lev_dev, fields, answer_round(number, groups), False, sections[number], slots, found)
-        finish_panel(lev_dev, fields, tiles, slots.shape[0], found, state_1, staged, send)
+        finish_panel(lev_dev, fields, tiles, slots.shape[0], found, state, staged, send)
 
     for copy in copies:
         copy.wait()
@@ -538,8 +534,7 @@
         terrain_level.reshape(levels, tiles, LANES).transpose(1, 0, 2).reshape(tiles * levels, LANES)
     )
     page = struct((panel_tiles, LANES), jnp.int32)
-    sources = [in_hbm(state), in_hbm(terrain), in_hbm(block_weight)]
-    first, second, slots, state_0, terrain_0 = pl.pallas_call(
+    first, second, slots, state, terrain = pl.pallas_call(
         functools.partial(list_kernel, groups),
         out_shape=[page] * 3 + [struct(state.shape), struct(terrain.shape, jnp.int32)],
         in_specs=specs(*[pl.ANY] * 4),
@@ -554,7 +549,8 @@
     )(
         in_hbm(panel_owner.reshape(page.shape)),
         in_hbm(panel_cell.reshape(page.shape)),
-        *sources[:2],
+        in_hbm(state),
+        in_hbm(terrain),
     )
 
     def towards(number_of, cross):
@@ -570,31 +566,30 @@
     lists = [first, third, second]
     scratch_rows = ROUNDS * fields * quarters
     table_shape = (scratch_rows * SUBLANES, LANES)
-    state_1, packed, table, facts = pl.pallas_call(
+    packed, table, facts = pl.pallas_call(
         functools.partial(prepare_kernel, lev_dev, fields, groups),
         out_shape=[
-            struct(state.shape),
             struct((tiles, LANES), jnp.int32),
             struct((fields * blocks * coarse // LANES * levels, LANES)),
             struct((2 * SUBLANES, LANES)),
         ],
-        in_specs=specs(VMEM, *[pl.ANY] * 5),
-        out_specs=specs(*[VMEM] * 4),
+        in_specs=specs(*[VMEM] * 2, *[pl.ANY] * 3),
+        out_specs=specs(*[VMEM] * 3),
         scratch_shapes=[
-            VMEM(terrain.shape, jnp.int32),
             VMEM(block_weight.shape, jnp.float32),
             SMEM((1, blocks), jnp.int32),
             SMEM((1, blocks), jnp.int32),
-            pltpu.SemaphoreType.DMA((5,)),
+            pltpu.SemaphoreType.DMA((3,)),
         ],
         cost_estimate=pl.CostEstimate(flops=0, bytes_accessed=8_000_000, transcendentals=0),
         compiler_params=params(),
         name="prepare",
     )(
-        terrain_0,
+        state,
+        terrain,
         in_hbm(block_owner.reshape(1, blocks)),
         in_hbm(block_row.reshape(1, blocks)),
-        *sources,
+        in_hbm(block_weight),
     )
     part = struct((lev_dev * scratch_rows, LANES))
     parts = pl.pallas_call(
@@ -605,7 +600,7 @@
         scratch_shapes=[VMEM(table_shape, jnp.float32)],
         compiler_params=params(),
         name="produce",
-    )(*lists, state_0, packed, table)
+    )(*lists, state, packed, table)
     arrived = [parts[0]] + [
         lax.ppermute(parts[distance], "lev", [(rank, rank ^ distance) for rank in range(partners)])
         for distance in range(partners - 1, 0, -1)
@@ -642,13 +637,13 @@
     result = pl.pallas_call(
         functools.partial(finish_kernel, *sizes, SECTION_ORDER[-1]),
         out_shape=pltpu.HBM(state.shape, jnp.float32),
-        in_specs=specs(*[VMEM] * 9),
+        in_specs=specs(*[VMEM] * 8),
         out_specs=pl.BlockSpec(memory_space=pltpu.HBM),
         scratch_shapes=[VMEM(one.shape, one.dtype) for one in kept]
         + [VMEM(state.shape, jnp.float32), pltpu.SemaphoreType.DMA((fields,))],
         compiler_params=params(),
         name="finish",
-    )(*sections, slots, *held, state_0, state_1)
+    )(*sections, slots, *held, state)
     return (
         result.reshape(fields, tiles, lev_dev, LANES)
         .transpose(2, 0, 1, 3)

time: 25.6 us -> 25.6 us (level)
  no operation moved by 1% of the time
where the time goes in v8:
time: 25.6 us; the launch traced here: 25.3 us
  starting transfers between devices  12.1 us (47%)
  waiting for transfers between devices  8.59 us (34%)
  Pallas kernels  4.61 us (18%)
    ppermute x3, waiting for transfers between devices, on_device(): lax.ppermute(parts[distance], 'lev', [(rank, rank ^ distance) for rank in...  3.82 us
    ppermute x3, starting transfers between devices, on_device(): lax.ppermute(parts[distance], 'lev', [(rank, rank ^ distance) for rank in...  3.55 us
    ppermute x1, starting transfers between devices, on_device(): first = lax.ppermute(first, ('grid', 'side'), towards(lambda side: side, 0))  3.09 us
    ppermute x3, starting transfers between devices, on_device(): lax.ppermute(sections[number], ('grid', 'side'), towards(lambda side: num...  2.9 us
    ppermute x3, waiting for transfers between devices, on_device(): lax.ppermute(sections[number], ('grid', 'side'), towards(lambda side: num...  2.57 us
    ppermute x1, waiting for transfers between devices, on_device(): second = lax.ppermute(second, ('grid', 'side'), towards(lambda side: 2, 1))  2.15 us
    ppermute x1, starting transfers between devices, on_device(): second = lax.ppermute(second, ('grid', 'side'), towards(lambda side: 2, 1))  1.54 us
    pallas_call x1, Pallas kernels, on_device(): pl.pallas_call(functools.partial(produce_kernel, lev_dev, fields, partner...  1.52 us
  transfers between devices with their start and end apart: 9, of which 6 were waited for; matrix products, arithmetic and copies ran while one was open for 0% of the time, Pallas kernels for 3%

profile of v8, /device:TPU:0, one launch (start us, length us, event | category | flops | bytes accessed | tf_op | source)
XLA Modules:
  0.0 25.3 jit_solution(5270754452459113714)
XLA Ops:
  0.0 1.2 %lists.1 = (s32[8,128]{1,0:T(8,128)S(1)}, s32[8,128]{1,0:T(8,128)S(1)}, s32[8,128]{1,0:T(8,128)S(1)}, f32[768,128]{1,0:T(8,128)S(1)}, s32[512,128]{1,0:T(8,128)S(1)}) custom-call(s32[8,128]{1,0:T(8,128)} %bitcast.21, s32[8,128]{1,0:T(8,128)} %bitcast.22, f32[768,128]{1,0:T(8,128)} %bitcast.19, s32[512,128]{1,0:T(8,128)} %bitcast.20), custom_call_target="tpu_custom_call" | custom-call | tf_op jit(solution)/shard_map/lists/pallas_call | solution.py:537
  1.2 3.1 %collective-permute-start = (s32[8,128]{1,0:T(8,128)S(1)}, s32[8,128]{1,0:T(8,128)S(1)}, u32[]{:S(2)}, u32[]{:S(2)}) collective-permute-start(s32[8,128]{1,0:T(8,128)S(1)} %get-tuple-element.26), channel_id=1, source_target_pairs={{0,8},{1,17},{8,0},{9,25},{16,24},{17,1},{24,16},{25,9},{2,10},{3,... | collective-permute-start | bytes 12296 | tf_op jit(solution)/shard_map/ppermute | solution.py:563
  4.3 1.5 %collective-permute-start.2 = (s32[8,128]{1,0:T(8,128)S(1)}, s32[8,128]{1,0:T(8,128)S(1)}, u32[]{:S(2)}, u32[]{:S(2)}) collective-permute-start(s32[8,128]{1,0:T(8,128)S(1)} %get-tuple-element.27), channel_id=1, source_target_pairs={{0,25},{1,24},{8,17},{9,16},{16,9},{17,8},{24,1},{25,0},{2,27},{3,... | collective-permute-start | bytes 12296 | tf_op jit(solution)/shard_map/ppermute | solution.py:564
  5.9 0.0 collective-permute-done.refs_0_
  5.9 1.0 %collective-permute-start.1 = (s32[8,128]{1,0:T(8,128)S(1)}, s32[8,128]{1,0:T(8,128)S(1)}, u32[]{:S(2)}, u32[]{:S(2)}) collective-permute-start(s32[8,128]{1,0:T(8,128)S(1)} %collective-permute-done.refs_0_), channel_id=1, source_target_pairs={{0,1},{1,0},{2,3},{3,2},{4,5},{5,4},{6,7},{7,6},{8,9},{9,8},{10,11... | collective-permute-start | bytes 12296 | tf_op jit(solution)/shard_map/ppermute | solution.py:565
  6.9 0.1 prepare.1
  7.0 2.2 %collective-permute-done.2.refs_2_ = s32[8,128]{1,0:T(8,128)S(1)} collective-permute-done((s32[8,128]{1,0:T(8,128)S(1)}, s32[8,128]{1,0:T(8,128)S(1)}, u32[]{:S(2)}, u32[]{:S(2)}) %collective-permute-start.2) | collective-permute-done | bytes 4128 | tf_op jit(solution)/shard_map/ppermute | solution.py:564
  9.2 0.0 collective-permute-done.1.refs_1_
  9.2 1.5 %produce.1 = (f32[144,128]{1,0:T(8,128)S(1)}, f32[144,128]{1,0:T(8,128)S(1)}, f32[144,128]{1,0:T(8,128)S(1)}, f32[144,128]{1,0:T(8,128)S(1)}) custom-call(s32[8,128]{1,0:T(8,128)S(1)} %collective-permute-done.refs_0_, s32[8,128]{1,0:T(8,128)S(1)} %collective-permute-done.1.refs_1_, s32[8,128]{1,0:T(8,128)S(1)} %collective-permute-done.2.refs_2_, ...), custom_call_target="tpu_custom_call" | custom-call | tf_op jit(solution)/shard_map/produce/pallas_call | solution.py:595
  10.7 2.5 %collective-permute-start.3 = (f32[144,128]{1,0:T(8,128)S(1)}, f32[144,128]{1,0:T(8,128)S(1)}, u32[]{:S(2)}, u32[]{:S(2)}) collective-permute-start(f32[144,128]{1,0:T(8,128)S(1)} %get-tuple-element.33), channel_id=1, source_target_pairs={{0,6},{2,4},{4,2},{6,0},{1,7},{3,5},{5,3},{7,1},{8,14},{10,12},{12... | collective-permute-start | bytes 221192 | tf_op jit(solution)/shard_map/ppermute | solution.py:605
  13.2 0.5 %collective-permute-start.4 = (f32[144,128]{1,0:T(8,128)S(1)}, f32[144,128]{1,0:T(8,128)S(1)}, u32[]{:S(2)}, u32[]{:S(2)}) collective-permute-start(f32[144,128]{1,0:T(8,128)S(1)} %get-tuple-element.34), channel_id=1, source_target_pairs={{0,4},{2,6},{4,0},{6,2},{1,5},{3,7},{5,1},{7,3},{8,12},{10,14},{12... | collective-permute-start | bytes 221192 | tf_op jit(solution)/shard_map/ppermute | solution.py:605
  13.7 0.5 %collective-permute-start.5 = (f32[144,128]{1,0:T(8,128)S(1)}, f32[144,128]{1,0:T(8,128)S(1)}, u32[]{:S(2)}, u32[]{:S(2)}) collective-permute-start(f32[144,128]{1,0:T(8,128)S(1)} %get-tuple-element.35), channel_id=1, source_target_pairs={{0,2},{2,0},{4,6},{6,4},{1,3},{3,1},{5,7},{7,5},{8,10},{10,8},{12,... | collective-permute-start | bytes 221192 | tf_op jit(solution)/shard_map/ppermute | solution.py:605
  14.2 2.1 %collective-permute-done.3.refs_1_ = f32[144,128]{1,0:T(8,128)S(1)} collective-permute-done((f32[144,128]{1,0:T(8,128)S(1)}, f32[144,128]{1,0:T(8,128)S(1)}, u32[]{:S(2)}, u32[]{:S(2)}) %collective-permute-start.3) | collective-permute-done | bytes 73760 | tf_op jit(solution)/shard_map/ppermute | solution.py:605
  16.3 1.3 %collective-permute-done.4.refs_2_ = f32[144,128]{1,0:T(8,128)S(1)} collective-permute-done((f32[144,128]{1,0:T(8,128)S(1)}, f32[144,128]{1,0:T(8,128)S(1)}, u32[]{:S(2)}, u32[]{:S(2)}) %collective-permute-start.4) | collective-permute-done | bytes 73760 | tf_op jit(solution)/shard_map/ppermute | solution.py:605
  17.5 0.5 %collective-permute-done.5.refs_3_ = f32[144,128]{1,0:T(8,128)S(1)} collective-permute-done((f32[144,128]{1,0:T(8,128)S(1)}, f32[144,128]{1,0:T(8,128)S(1)}, u32[]{:S(2)}, u32[]{:S(2)}) %collective-permute-start.5) | collective-permute-done | bytes 73760 | tf_op jit(solution)/shard_map/ppermute | solution.py:605
  18.1 1.8 %collective-permute-start.8 = (f32[64,128]{1,0:T(8,128)S(1)}, f32[64,128]{1,0:T(8,128)S(1)}, u32[]{:S(2)}, u32[]{:S(2)}) collective-permute-start(f32[64,128]{1,0:T(8,128)S(1)} %get-tuple-element.39), channel_id=1, source_target_pairs={{0,25},{1,24},{8,17},{9,16},{16,9},{17,8},{24,1},{25,0},{2,27},{3,... | collective-permute-start | bytes 98312 | tf_op jit(solution)/shard_map/ppermute | solution.py:618
  19.9 0.0 collective-permute-start.6
  19.9 1.1 %collective-permute-start.7 = (f32[64,128]{1,0:T(8,128)S(1)}, f32[64,128]{1,0:T(8,128)S(1)}, u32[]{:S(2)}, u32[]{:S(2)}) collective-permute-start(f32[64,128]{1,0:T(8,128)S(1)} %get-tuple-element.38), channel_id=1, source_target_pairs={{0,17},{1,16},{8,25},{9,24},{16,1},{17,0},{24,9},{25,8},{2,19},{3,... | collective-permute-start | bytes 98312 | tf_op jit(solution)/shard_map/ppermute | solution.py:618
  21.0 2.4 %collective-permute-done.8.section.refs_2_ = f32[64,128]{1,0:T(8,128)S(1)} collective-permute-done((f32[64,128]{1,0:T(8,128)S(1)}, f32[64,128]{1,0:T(8,128)S(1)}, u32[]{:S(2)}, u32[]{:S(2)}) %collective-permute-start.8) | collective-permute-done | bytes 32800 | tf_op jit(solution)/shard_map/ppermute | solution.py:618
  23.4 0.3 %place.2 = (bf16[96,1664]{1,0:T(8,128)(2,1)S(1)}, bf16[96,1664]{1,0:T(8,128)(2,1)S(1)}, f32[384,128]{1,0:T(8,128)S(1)}) custom-call(f32[64,128]{1,0:T(8,128)S(1)} %collective-permute-done.8.section.refs_2_, s32[8,128]{1,0:T(8,128)S(1)} %get-tuple-element.40.slots.refs_3_), custom_call_target="tpu_custom_call" | custom-call | tf_op jit(solution)/shard_map/place/pallas_call | solution.py:628
  23.7 0.0 collective-permute-done.6.section.refs_0_
  23.7 0.3 %place.3 = (bf16[96,1664]{1,0:T(8,128)(2,1)S(1)}, bf16[96,1664]{1,0:T(8,128)(2,1)S(1)}, f32[384,128]{1,0:T(8,128)S(1)}) custom-call(f32[64,128]{1,0:T(8,128)S(1)} %collective-permute-done.6.section.refs_0_, s32[8,128]{1,0:T(8,128)S(1)} %get-tuple-element.40.slots.refs_3_, ...), custom_call_target="tpu_custom_call", output_to_operand_aliasing={{0}: (2, {}), {1}: (3, {}), {2}: (4, {})} | custom-call | tf_op jit(solution)/shard_map/place/pallas_call | solution.py:628
  24.0 0.2 collective-permute-done.7.refs_1_
  24.2 1.2 %finish.1 = f32[768,128]{1,0:T(8,128)} custom-call(f32[64,128]{1,0:T(8,128)S(1)} %collective-permute-done.6.section.refs_0_, f32[64,128]{1,0:T(8,128)S(1)} %collective-permute-done.7.refs_1_, f32[64,128]{1,0:T(8,128)S(1)} %collective-permute-done.8.section.refs_2_, s32[8,128]{1,0:T(8,128)S(1)} %get-tuple-element.40.slots.refs_3_, ...), custom_call_target="tpu_custom_call" | custom-call | tf_op jit(solution)/shard_map/finish/pallas_call | solution.py:637
  (1 shorter events, 0.0 us)
Async XLA Ops:
  1.2 4.7 %collective-permute-start = (s32[8,128]{1,0:T(8,128)S(1)}, s32[8,128]{1,0:T(8,128)S(1)}, u32[]{:S(2)}, u32[]{:S(2)}) collective-permute-start(s32[8,128]{1,0:T(8,128)S(1)} %get-tuple-element.26), channel_id=1, source_target_pairs={{0,8},{1,17},{8,0},{9,25},{16,24},{17,1},{24,16},{25,9},{2,10},{3,... | collective-permute-start | bytes 12296 | tf_op jit(solution)/shard_map/ppermute | solution.py:563
  4.3 4.8 %collective-permute-start.2 = (s32[8,128]{1,0:T(8,128)S(1)}, s32[8,128]{1,0:T(8,128)S(1)}, u32[]{:S(2)}, u32[]{:S(2)}) collective-permute-start(s32[8,128]{1,0:T(8,128)S(1)} %get-tuple-element.27), channel_id=1, source_target_pairs={{0,25},{1,24},{8,17},{9,16},{16,9},{17,8},{24,1},{25,0},{2,27},{3,... | collective-permute-start | bytes 12296 | tf_op jit(solution)/shard_map/ppermute | solution.py:564
  5.9 3.3 %collective-permute-start.1 = (s32[8,128]{1,0:T(8,128)S(1)}, s32[8,128]{1,0:T(8,128)S(1)}, u32[]{:S(2)}, u32[]{:S(2)}) collective-permute-start(s32[8,128]{1,0:T(8,128)S(1)} %collective-permute-done.refs_0_), channel_id=1, source_target_pairs={{0,1},{1,0},{2,3},{3,2},{4,5},{5,4},{6,7},{7,6},{8,9},{9,8},{10,11... | collective-permute-start | bytes 12296 | tf_op jit(solution)/shard_map/ppermute | solution.py:565
  10.7 5.6 %collective-permute-start.3 = (f32[144,128]{1,0:T(8,128)S(1)}, f32[144,128]{1,0:T(8,128)S(1)}, u32[]{:S(2)}, u32[]{:S(2)}) collective-permute-start(f32[144,128]{1,0:T(8,128)S(1)} %get-tuple-element.33), channel_id=1, source_target_pairs={{0,6},{2,4},{4,2},{6,0},{1,7},{3,5},{5,3},{7,1},{8,14},{10,12},{12... | collective-permute-start | bytes 221192 | tf_op jit(solution)/shard_map/ppermute | solution.py:605
  13.2 4.4 %collective-permute-start.4 = (f32[144,128]{1,0:T(8,128)S(1)}, f32[144,128]{1,0:T(8,128)S(1)}, u32[]{:S(2)}, u32[]{:S(2)}) collective-permute-start(f32[144,128]{1,0:T(8,128)S(1)} %get-tuple-element.34), channel_id=1, source_target_pairs={{0,4},{2,6},{4,0},{6,2},{1,5},{3,7},{5,1},{7,3},{8,12},{10,14},{12... | collective-permute-start | bytes 221192 | tf_op jit(solution)/shard_map/ppermute | solution.py:605
  13.7 4.4 %collective-permute-start.5 = (f32[144,128]{1,0:T(8,128)S(1)}, f32[144,128]{1,0:T(8,128)S(1)}, u32[]{:S(2)}, u32[]{:S(2)}) collective-permute-start(f32[144,128]{1,0:T(8,128)S(1)} %get-tuple-element.35), channel_id=1, source_target_pairs={{0,2},{2,0},{4,6},{6,4},{1,3},{3,1},{5,7},{7,5},{8,10},{10,8},{12,... | collective-permute-start | bytes 221192 | tf_op jit(solution)/shard_map/ppermute | solution.py:605
  18.1 5.3 %collective-permute-start.8 = (f32[64,128]{1,0:T(8,128)S(1)}, f32[64,128]{1,0:T(8,128)S(1)}, u32[]{:S(2)}, u32[]{:S(2)}) collective-permute-start(f32[64,128]{1,0:T(8,128)S(1)} %get-tuple-element.39), channel_id=1, source_target_pairs={{0,25},{1,24},{8,17},{9,16},{16,9},{17,8},{24,1},{25,0},{2,27},{3,... | collective-permute-start | bytes 98312 | tf_op jit(solution)/shard_map/ppermute | solution.py:618
  19.9 3.8 %collective-permute-start.6 = (f32[64,128]{1,0:T(8,128)S(1)}, f32[64,128]{1,0:T(8,128)S(1)}, u32[]{:S(2)}, u32[]{:S(2)}) collective-permute-start(f32[64,128]{1,0:T(8,128)S(1)} %get-tuple-element.37), channel_id=1, source_target_pairs={{0,9},{1,8},{8,1},{9,0},{16,25},{17,24},{24,17},{25,16},{2,11},{3,... | collective-permute-start | bytes 98312 | tf_op jit(solution)/shard_map/ppermute | solution.py:618
  19.9 4.3 %collective-permute-start.7 = (f32[64,128]{1,0:T(8,128)S(1)}, f32[64,128]{1,0:T(8,128)S(1)}, u32[]{:S(2)}, u32[]{:S(2)}) collective-permute-start(f32[64,128]{1,0:T(8,128)S(1)} %get-tuple-element.38), channel_id=1, source_target_pairs={{0,17},{1,16},{8,25},{9,24},{16,1},{17,0},{24,9},{25,8},{2,19},{3,... | collective-permute-start | bytes 98312 | tf_op jit(solution)/shard_map/ppermute | solution.py:618

commit v9 on v7

--- a/solution.py
+++ b/solution.py
@@ -12,7 +12,7 @@
 SUBLANES = 8
 VALUE_BITS = 24
 ROW_BITS = 16
-SECTION_ORDER = (2, 0, 1)
+SECTION_ORDER = (1, 2, 0)
 HELD_ROWS = 16
 ROUNDS = 3
 DIGIT_BITS = 3

time: 25.6 us -> 25.7 us (level)
  waiting for transfers between devices: 8.48 us -> 8.81 us
    ppermute x3, waiting for transfers between devices: 2.48 us -> 2.81 us  [on_device(): lax.ppermute(sections[number], ('grid', 'side'), towards(lambda side: num...]
where the time goes in v9:
time: 25.7 us; the launch traced here: 25.5 us
  starting transfers between devices  12 us (47%)
  waiting for transfers between devices  8.81 us (34%)
  Pallas kernels  4.63 us (18%)
    ppermute x3, waiting for transfers between devices, on_device(): lax.ppermute(parts[distance], 'lev', [(rank, rank ^ distance) for rank in...  3.82 us
    ppermute x3, starting transfers between devices, on_device(): lax.ppermute(parts[distance], 'lev', [(rank, rank ^ distance) for rank in...  3.55 us
    ppermute x1, starting transfers between devices, on_device(): first = lax.ppermute(first, ('grid', 'side'), towards(lambda side: side, 0))  3.09 us
    ppermute x3, starting transfers between devices, on_device(): lax.ppermute(sections[number], ('grid', 'side'), towards(lambda side: num...  2.82 us
    ppermute x3, waiting for transfers between devices, on_device(): lax.ppermute(sections[number], ('grid', 'side'), towards(lambda side: num...  2.81 us
    ppermute x1, waiting for transfers between devices, on_device(): second = lax.ppermute(second, ('grid', 'side'), towards(lambda side: 2, 1))  2.13 us
    ppermute x1, starting transfers between devices, on_device(): second = lax.ppermute(second, ('grid', 'side'), towards(lambda side: 2, 1))  1.54 us
    pallas_call x1, Pallas kernels, on_device(): pl.pallas_call(functools.partial(produce_kernel, lev_dev, fields, partner...  1.52 us
  transfers between devices with their start and end apart: 9, of which 6 were waited for; matrix products, arithmetic and copies ran while one was open for 0% of the time, Pallas kernels for 3%

profile of v9, /device:TPU:0, one launch (start us, length us, event | category | flops | bytes accessed | tf_op | source)
XLA Modules:
  0.0 25.5 jit_solution(9682263539084267192)
XLA Ops:
  0.0 1.2 %lists.1 = (s32[8,128]{1,0:T(8,128)S(1)}, s32[8,128]{1,0:T(8,128)S(1)}, s32[8,128]{1,0:T(8,128)S(1)}, f32[768,128]{1,0:T(8,128)S(1)}, s32[512,128]{1,0:T(8,128)S(1)}) custom-call(s32[8,128]{1,0:T(8,128)} %bitcast.23, s32[8,128]{1,0:T(8,128)} %bitcast.24, f32[768,128]{1,0:T(8,128)} %bitcast.19, s32[512,128]{1,0:T(8,128)} %bitcast.21), custom_call_target="tpu_custom_call" | custom-call | tf_op jit(solution)/shard_map/lists/pallas_call | solution.py:542
  1.2 3.1 %collective-permute-start = (s32[8,128]{1,0:T(8,128)S(1)}, s32[8,128]{1,0:T(8,128)S(1)}, u32[]{:S(2)}, u32[]{:S(2)}) collective-permute-start(s32[8,128]{1,0:T(8,128)S(1)} %get-tuple-element.27), channel_id=1, source_target_pairs={{0,8},{1,17},{8,0},{9,25},{16,24},{17,1},{24,16},{25,9},{2,10},{3,... | collective-permute-start | bytes 12296 | tf_op jit(solution)/shard_map/ppermute | solution.py:567
  4.3 1.5 %collective-permute-start.2 = (s32[8,128]{1,0:T(8,128)S(1)}, s32[8,128]{1,0:T(8,128)S(1)}, u32[]{:S(2)}, u32[]{:S(2)}) collective-permute-start(s32[8,128]{1,0:T(8,128)S(1)} %get-tuple-element.28), channel_id=1, source_target_pairs={{0,25},{1,24},{8,17},{9,16},{16,9},{17,8},{24,1},{25,0},{2,27},{3,... | collective-permute-start | bytes 12296 | tf_op jit(solution)/shard_map/ppermute | solution.py:568
  5.9 0.0 collective-permute-done.refs_0_
  5.9 1.0 %collective-permute-start.1 = (s32[8,128]{1,0:T(8,128)S(1)}, s32[8,128]{1,0:T(8,128)S(1)}, u32[]{:S(2)}, u32[]{:S(2)}) collective-permute-start(s32[8,128]{1,0:T(8,128)S(1)} %collective-permute-done.refs_0_), channel_id=1, source_target_pairs={{0,1},{1,0},{2,3},{3,2},{4,5},{5,4},{6,7},{7,6},{8,9},{9,8},{10,11... | collective-permute-start | bytes 12296 | tf_op jit(solution)/shard_map/ppermute | solution.py:569
  6.9 0.1 prepare.1
  7.0 2.1 %collective-permute-done.2.refs_2_ = s32[8,128]{1,0:T(8,128)S(1)} collective-permute-done((s32[8,128]{1,0:T(8,128)S(1)}, s32[8,128]{1,0:T(8,128)S(1)}, u32[]{:S(2)}, u32[]{:S(2)}) %collective-permute-start.2) | collective-permute-done | bytes 4128 | tf_op jit(solution)/shard_map/ppermute | solution.py:568
  9.1 0.0 collective-permute-done.1.refs_1_
  9.2 1.5 %produce.1 = (f32[144,128]{1,0:T(8,128)S(1)}, f32[144,128]{1,0:T(8,128)S(1)}, f32[144,128]{1,0:T(8,128)S(1)}, f32[144,128]{1,0:T(8,128)S(1)}) custom-call(s32[8,128]{1,0:T(8,128)S(1)} %collective-permute-done.refs_0_, s32[8,128]{1,0:T(8,128)S(1)} %collective-permute-done.1.refs_1_, s32[8,128]{1,0:T(8,128)S(1)} %collective-permute-done.2.refs_2_, ...), custom_call_target="tpu_custom_call" | custom-call | tf_op jit(solution)/shard_map/produce/pallas_call | solution.py:600
  10.7 2.5 %collective-permute-start.3 = (f32[144,128]{1,0:T(8,128)S(1)}, f32[144,128]{1,0:T(8,128)S(1)}, u32[]{:S(2)}, u32[]{:S(2)}) collective-permute-start(f32[144,128]{1,0:T(8,128)S(1)} %get-tuple-element.34), channel_id=1, source_target_pairs={{0,6},{2,4},{4,2},{6,0},{1,7},{3,5},{5,3},{7,1},{8,14},{10,12},{12... | collective-permute-start | bytes 221192 | tf_op jit(solution)/shard_map/ppermute | solution.py:610
  13.2 0.5 %collective-permute-start.4 = (f32[144,128]{1,0:T(8,128)S(1)}, f32[144,128]{1,0:T(8,128)S(1)}, u32[]{:S(2)}, u32[]{:S(2)}) collective-permute-start(f32[144,128]{1,0:T(8,128)S(1)} %get-tuple-element.35), channel_id=1, source_target_pairs={{0,4},{2,6},{4,0},{6,2},{1,5},{3,7},{5,1},{7,3},{8,12},{10,14},{12... | collective-permute-start | bytes 221192 | tf_op jit(solution)/shard_map/ppermute | solution.py:610
  13.7 0.5 %collective-permute-start.5 = (f32[144,128]{1,0:T(8,128)S(1)}, f32[144,128]{1,0:T(8,128)S(1)}, u32[]{:S(2)}, u32[]{:S(2)}) collective-permute-start(f32[144,128]{1,0:T(8,128)S(1)} %get-tuple-element.36), channel_id=1, source_target_pairs={{0,2},{2,0},{4,6},{6,4},{1,3},{3,1},{5,7},{7,5},{8,10},{10,8},{12,... | collective-permute-start | bytes 221192 | tf_op jit(solution)/shard_map/ppermute | solution.py:610
  14.2 2.1 %collective-permute-done.3.refs_1_ = f32[144,128]{1,0:T(8,128)S(1)} collective-permute-done((f32[144,128]{1,0:T(8,128)S(1)}, f32[144,128]{1,0:T(8,128)S(1)}, u32[]{:S(2)}, u32[]{:S(2)}) %collective-permute-start.3) | collective-permute-done | bytes 73760 | tf_op jit(solution)/shard_map/ppermute | solution.py:610
  16.3 1.3 %collective-permute-done.4.refs_2_ = f32[144,128]{1,0:T(8,128)S(1)} collective-permute-done((f32[144,128]{1,0:T(8,128)S(1)}, f32[144,128]{1,0:T(8,128)S(1)}, u32[]{:S(2)}, u32[]{:S(2)}) %collective-permute-start.4) | collective-permute-done | bytes 73760 | tf_op jit(solution)/shard_map/ppermute | solution.py:610
  17.5 0.5 %collective-permute-done.5.refs_3_ = f32[144,128]{1,0:T(8,128)S(1)} collective-permute-done((f32[144,128]{1,0:T(8,128)S(1)}, f32[144,128]{1,0:T(8,128)S(1)}, u32[]{:S(2)}, u32[]{:S(2)}) %collective-permute-start.5) | collective-permute-done | bytes 73760 | tf_op jit(solution)/shard_map/ppermute | solution.py:610
  18.1 0.8 %collective-permute-start.7 = (f32[64,128]{1,0:T(8,128)S(1)}, f32[64,128]{1,0:T(8,128)S(1)}, u32[]{:S(2)}, u32[]{:S(2)}) collective-permute-start(f32[64,128]{1,0:T(8,128)S(1)} %get-tuple-element.39), channel_id=1, source_target_pairs={{0,17},{1,16},{8,25},{9,24},{16,1},{17,0},{24,9},{25,8},{2,19},{3,... | collective-permute-start | bytes 98312 | tf_op jit(solution)/shard_map/ppermute | solution.py:623
  18.9 1.3 %collective-permute-start.8 = (f32[64,128]{1,0:T(8,128)S(1)}, f32[64,128]{1,0:T(8,128)S(1)}, u32[]{:S(2)}, u32[]{:S(2)}) collective-permute-start(f32[64,128]{1,0:T(8,128)S(1)} %get-tuple-element.40), channel_id=1, source_target_pairs={{0,25},{1,24},{8,17},{9,16},{16,9},{17,8},{24,1},{25,0},{2,27},{3,... | collective-permute-start | bytes 98312 | tf_op jit(solution)/shard_map/ppermute | solution.py:623
  20.2 0.7 %collective-permute-start.6 = (f32[64,128]{1,0:T(8,128)S(1)}, f32[64,128]{1,0:T(8,128)S(1)}, u32[]{:S(2)}, u32[]{:S(2)}) collective-permute-start(f32[64,128]{1,0:T(8,128)S(1)} %get-tuple-element.38), channel_id=1, source_target_pairs={{0,9},{1,8},{8,1},{9,0},{16,25},{17,24},{24,17},{25,16},{2,11},{3,... | collective-permute-start | bytes 98312 | tf_op jit(solution)/shard_map/ppermute | solution.py:623
  20.9 1.8 %collective-permute-done.7.section.refs_1_ = f32[64,128]{1,0:T(8,128)S(1)} collective-permute-done((f32[64,128]{1,0:T(8,128)S(1)}, f32[64,128]{1,0:T(8,128)S(1)}, u32[]{:S(2)}, u32[]{:S(2)}) %collective-permute-start.7) | collective-permute-done | bytes 32800 | tf_op jit(solution)/shard_map/ppermute | solution.py:623
  22.7 0.3 %place.2 = (bf16[96,1664]{1,0:T(8,128)(2,1)S(1)}, bf16[96,1664]{1,0:T(8,128)(2,1)S(1)}, f32[384,128]{1,0:T(8,128)S(1)}) custom-call(f32[64,128]{1,0:T(8,128)S(1)} %collective-permute-done.7.section.refs_1_, s32[8,128]{1,0:T(8,128)S(1)} %get-tuple-element.41.slots.refs_3_), custom_call_target="tpu_custom_call" | custom-call | tf_op jit(solution)/shard_map/place/pallas_call | solution.py:633
  23.0 1.0 %collective-permute-done.8.section.refs_2_ = f32[64,128]{1,0:T(8,128)S(1)} collective-permute-done((f32[64,128]{1,0:T(8,128)S(1)}, f32[64,128]{1,0:T(8,128)S(1)}, u32[]{:S(2)}, u32[]{:S(2)}) %collective-permute-start.8) | collective-permute-done | bytes 32800 | tf_op jit(solution)/shard_map/ppermute | solution.py:623
  24.0 0.3 %place.3 = (bf16[96,1664]{1,0:T(8,128)(2,1)S(1)}, bf16[96,1664]{1,0:T(8,128)(2,1)S(1)}, f32[384,128]{1,0:T(8,128)S(1)}) custom-call(f32[64,128]{1,0:T(8,128)S(1)} %collective-permute-done.8.section.refs_2_, s32[8,128]{1,0:T(8,128)S(1)} %get-tuple-element.41.slots.refs_3_, ...), custom_call_target="tpu_custom_call", output_to_operand_aliasing={{0}: (2, {}), {1}: (3, {}), {2}: (4, {})} | custom-call | tf_op jit(solution)/shard_map/place/pallas_call | solution.py:633
  24.3 0.0 collective-permute-done.6.refs_0_
  24.3 1.2 %finish.1 = f32[768,128]{1,0:T(8,128)} custom-call(f32[64,128]{1,0:T(8,128)S(1)} %collective-permute-done.6.refs_0_, f32[64,128]{1,0:T(8,128)S(1)} %collective-permute-done.7.section.refs_1_, f32[64,128]{1,0:T(8,128)S(1)} %collective-permute-done.8.section.refs_2_, s32[8,128]{1,0:T(8,128)S(1)} %get-tuple-element.41.slots.refs_3_, ...), custom_call_target="tpu_custom_call" | custom-call | tf_op jit(solution)/shard_map/finish/pallas_call | solution.py:642
  (1 shorter events, 0.0 us)
Async XLA Ops:
  1.2 4.7 %collective-permute-start = (s32[8,128]{1,0:T(8,128)S(1)}, s32[8,128]{1,0:T(8,128)S(1)}, u32[]{:S(2)}, u32[]{:S(2)}) collective-permute-start(s32[8,128]{1,0:T(8,128)S(1)} %get-tuple-element.27), channel_id=1, source_target_pairs={{0,8},{1,17},{8,0},{9,25},{16,24},{17,1},{24,16},{25,9},{2,10},{3,... | collective-permute-start | bytes 12296 | tf_op jit(solution)/shard_map/ppermute | solution.py:567
  4.3 4.8 %collective-permute-start.2 = (s32[8,128]{1,0:T(8,128)S(1)}, s32[8,128]{1,0:T(8,128)S(1)}, u32[]{:S(2)}, u32[]{:S(2)}) collective-permute-start(s32[8,128]{1,0:T(8,128)S(1)} %get-tuple-element.28), channel_id=1, source_target_pairs={{0,25},{1,24},{8,17},{9,16},{16,9},{17,8},{24,1},{25,0},{2,27},{3,... | collective-permute-start | bytes 12296 | tf_op jit(solution)/shard_map/ppermute | solution.py:568
  5.9 3.2 %collective-permute-start.1 = (s32[8,128]{1,0:T(8,128)S(1)}, s32[8,128]{1,0:T(8,128)S(1)}, u32[]{:S(2)}, u32[]{:S(2)}) collective-permute-start(s32[8,128]{1,0:T(8,128)S(1)} %collective-permute-done.refs_0_), channel_id=1, source_target_pairs={{0,1},{1,0},{2,3},{3,2},{4,5},{5,4},{6,7},{7,6},{8,9},{9,8},{10,11... | collective-permute-start | bytes 12296 | tf_op jit(solution)/shard_map/ppermute | solution.py:569
  10.7 5.6 %collective-permute-start.3 = (f32[144,128]{1,0:T(8,128)S(1)}, f32[144,128]{1,0:T(8,128)S(1)}, u32[]{:S(2)}, u32[]{:S(2)}) collective-permute-start(f32[144,128]{1,0:T(8,128)S(1)} %get-tuple-element.34), channel_id=1, source_target_pairs={{0,6},{2,4},{4,2},{6,0},{1,7},{3,5},{5,3},{7,1},{8,14},{10,12},{12... | collective-permute-start | bytes 221192 | tf_op jit(solution)/shard_map/ppermute | solution.py:610
  13.2 4.4 %collective-permute-start.4 = (f32[144,128]{1,0:T(8,128)S(1)}, f32[144,128]{1,0:T(8,128)S(1)}, u32[]{:S(2)}, u32[]{:S(2)}) collective-permute-start(f32[144,128]{1,0:T(8,128)S(1)} %get-tuple-element.35), channel_id=1, source_target_pairs={{0,4},{2,6},{4,0},{6,2},{1,5},{3,7},{5,1},{7,3},{8,12},{10,14},{12... | collective-permute-start | bytes 221192 | tf_op jit(solution)/shard_map/ppermute | solution.py:610
  13.7 4.4 %collective-permute-start.5 = (f32[144,128]{1,0:T(8,128)S(1)}, f32[144,128]{1,0:T(8,128)S(1)}, u32[]{:S(2)}, u32[]{:S(2)}) collective-permute-start(f32[144,128]{1,0:T(8,128)S(1)} %get-tuple-element.36), channel_id=1, source_target_pairs={{0,2},{2,0},{4,6},{6,4},{1,3},{3,1},{5,7},{7,5},{8,10},{10,8},{12,... | collective-permute-start | bytes 221192 | tf_op jit(solution)/shard_map/ppermute | solution.py:610
  18.1 4.7 %collective-permute-start.7 = (f32[64,128]{1,0:T(8,128)S(1)}, f32[64,128]{1,0:T(8,128)S(1)}, u32[]{:S(2)}, u32[]{:S(2)}) collective-permute-start(f32[64,128]{1,0:T(8,128)S(1)} %get-tuple-element.39), channel_id=1, source_target_pairs={{0,17},{1,16},{8,25},{9,24},{16,1},{17,0},{24,9},{25,8},{2,19},{3,... | collective-permute-start | bytes 98312 | tf_op jit(solution)/shard_map/ppermute | solution.py:623
  18.9 5.1 %collective-permute-start.8 = (f32[64,128]{1,0:T(8,128)S(1)}, f32[64,128]{1,0:T(8,128)S(1)}, u32[]{:S(2)}, u32[]{:S(2)}) collective-permute-start(f32[64,128]{1,0:T(8,128)S(1)} %get-tuple-element.40), channel_id=1, source_target_pairs={{0,25},{1,24},{8,17},{9,16},{16,9},{17,8},{24,1},{25,0},{2,27},{3,... | collective-permute-start | bytes 98312 | tf_op jit(solution)/shard_map/ppermute | solution.py:623
  20.2 4.1 %collective-permute-start.6 = (f32[64,128]{1,0:T(8,128)S(1)}, f32[64,128]{1,0:T(8,128)S(1)}, u32[]{:S(2)}, u32[]{:S(2)}) collective-permute-start(f32[64,128]{1,0:T(8,128)S(1)} %get-tuple-element.38), channel_id=1, source_target_pairs={{0,9},{1,8},{8,1},{9,0},{16,25},{17,24},{24,17},{25,16},{2,11},{3,... | collective-permute-start | bytes 98312 | tf_op jit(solution)/shard_map/ppermute | solution.py:623
